TPU v7x, 512 devices: a whole 4x8x8 slice. The times are simulated.
512 devices in a mesh: gx: 4 (over x), gy: 8 (over z), gz: 16 (over y, core).
Axes of the slice: x: 4, y: 8, z: 8, core: 2. Of those that a mesh axis runs over, the one named last changes fastest.
Arguments:
- right_side: float32 [128, 256, 512], P('gz', 'gy', 'gx'), may hold values from -6 to 6
- guess: float32 [128, 256, 512], P('gz', 'gy', 'gx'), may hold values from -6 to 6
- coefficient: float32 [128, 256, 512], P('gz', 'gy', 'gx'), may hold values from 0.3 to 3
Outputs:
- solution: float32 [128, 256, 512], P('gz', 'gy', 'gx')
- residual: float32 [128, 256, 512], P('gz', 'gy', 'gx')
All inputs are finite; a program needn't handle non-finite values.
Results may differ from a plain program's by a relative error of at most 0.00035.
Values sent between devices are 32-bit elements; how exact they have to be, the bound alone decides.
No kernel may reach another device: no remote copies, remote signals or barrier semaphores. Data moves between devices by JAX's collectives and lax.ppermute only.
A program may use at most 64 MiB of HBM per device.

v0:
```python
import jax
import jax.numpy as jnp
from jax import lax
from jax.sharding import PartitionSpec as P

ITERS = 6


lower_bound = 0.5
upper_bound = 2.0


def with_halo(cells, sides, width):
    for axis, dim in sides:
        count = lax.axis_size(axis)
        ends = count - 1
        head = lax.slice_in_dim(cells, 0, width, axis=dim)
        tail = lax.slice_in_dim(cells, cells.shape[dim] - width, cells.shape[dim], axis=dim)
        cells = jnp.concatenate(
            [
                lax.ppermute(tail, axis, [(i, (i + 1) % count) for i in range(ends)]),
                cells,
                lax.ppermute(head, axis, [((i + 1) % count, i) for i in range(ends)]),
            ],
            axis=dim,
        )
    return cells


def neighbours(padded):
    centre = padded[1:-1, 1:-1, 1:-1]
    others = [
        padded[2:, 1:-1, 1:-1],
        padded[:-2, 1:-1, 1:-1],
        padded[1:-1, 2:, 1:-1],
        padded[1:-1, :-2, 1:-1],
        padded[1:-1, 1:-1, 2:],
        padded[1:-1, 1:-1, :-2],
    ]
    return (others, centre)


def stencil(source_padded, coeff_padded, scale):
    values, centre_value = neighbours(source_padded)
    coeffs, centre_coeff = neighbours(coeff_padded)
    total = jnp.zeros_like(centre_value)
    for value, coeff in zip(values, coeffs):
        total = total + 0.5 * (centre_coeff + coeff) * (centre_value - value)
    return scale * total


def diagonal_of(coeff_padded, scale):
    coeffs, centre_coeff = neighbours(coeff_padded)
    total = jnp.zeros_like(centre_coeff)
    for coeff in coeffs:
        total = total + 0.5 * (centre_coeff + coeff)
    return scale * total


def coarsen(source):
    depth, rows, cols = source.shape
    return source.reshape(depth // 2, 2, rows // 2, 2, cols // 2, 2).mean(axis=(1, 3, 5))


def refine_axis(padded, dimension):
    count = padded.shape[dimension] - 2
    before = lax.slice_in_dim(padded, 0, count, axis=dimension)
    centre = lax.slice_in_dim(padded, 1, count + 1, axis=dimension)
    after = lax.slice_in_dim(padded, 2, count + 2, axis=dimension)
    stacked = jnp.stack(
        [0.75 * centre + 0.25 * before, 0.75 * centre + 0.25 * after], axis=dimension + 1
    )
    new_shape = list(centre.shape)
    new_shape[dimension] = 2 * count
    return stacked.reshape(new_shape)


def prolong(padded):
    for dimension in range(3):
        padded = refine_axis(padded, dimension)
    return padded


def chebyshev(current, remainder, apply_op, inverse):
    theta = 0.5 * (upper_bound + lower_bound)
    delta = 0.5 * (upper_bound - lower_bound)
    sigma = theta / delta
    rho = 1.0 / sigma
    update = remainder * inverse / theta
    current = current + update
    remainder = remainder - apply_op(update)
    rho_next = 1.0 / (2.0 * sigma - rho)
    update = rho_next * rho * update + 2.0 * rho_next / delta * (remainder * inverse)
    current = current + update
    remainder = remainder - apply_op(update)
    return (current, remainder)


def conjugate(coarse_rhs, apply_op, total):
    answer = jnp.zeros_like(coarse_rhs)
    remainder = coarse_rhs
    direction = coarse_rhs
    norm_now = total(jnp.sum(remainder * remainder))
    for repeat in range(ITERS):
        image = apply_op(direction)
        alpha = norm_now / total(jnp.sum(direction * image))
        answer = answer + alpha * direction
        remainder = remainder - alpha * image
        if repeat + 1 < ITERS:
            norm_next = total(jnp.sum(remainder * remainder))
            direction = remainder + norm_next / norm_now * direction
            norm_now = norm_next
    return answer


def middle_apply(source, middle_coeff):
    rimmed = with_halo(source, (("gx", 2), ("gy", 1), ("gz", 0)), 1)
    return stencil(rimmed, middle_coeff, 0.25)


def local(right_side, guess, coefficient):
    kappa_one = coarsen(coefficient)
    kappa_two = coarsen(kappa_one)
    middle_coeff = with_halo(kappa_one, (("gx", 2), ("gy", 1), ("gz", 0)), 1)
    guess_padded, fine_coeff = (
        with_halo(guess, (("gx", 2), ("gy", 1), ("gz", 0)), 1),
        with_halo(coefficient, (("gx", 2), ("gy", 1), ("gz", 0)), 1),
    )
    fine_inverse = 1.0 / diagonal_of(fine_coeff, 1.0)

    def apply_fine(source):
        rimmed = with_halo(source, (("gx", 2), ("gy", 1), ("gz", 0)), 1)
        return stencil(rimmed, fine_coeff, 1.0)

    fine_iterate, fine_rest = chebyshev(
        guess, right_side - stencil(guess_padded, fine_coeff, 1.0), apply_fine, fine_inverse
    )

    def apply_middle(source):
        return middle_apply(source, middle_coeff)

    middle_inverse = 1.0 / diagonal_of(middle_coeff, 0.25)
    middle_rhs = coarsen(fine_rest)
    middle_iterate, middle_rest = chebyshev(
        jnp.zeros_like(middle_rhs), middle_rhs, apply_middle, middle_inverse
    )
    coarse_rhs = coarsen(middle_rest)
    depth, rows, cols = coarse_rhs.shape
    count_x = lax.axis_size("gx")
    count_z = lax.axis_size("gz")
    stacks = (
        lax.all_gather(coarse_rhs[None], ("gx", "gz"), axis=0, tiled=True),
        lax.all_gather(kappa_two[None], ("gx", "gz"), axis=0, tiled=True),
    )

    def assemble(stack):
        parts = stack.reshape(count_x, count_z, depth, rows, cols)
        return parts.transpose(1, 2, 3, 0, 4).reshape(count_z * depth, rows, count_x * cols)

    block_rhs = assemble(stacks[0])
    block_coeff = assemble(stacks[1])
    coeff_rimmed = with_halo(block_coeff, (("gy", 1),), 1)
    block_coeff_padded = jnp.pad(coeff_rimmed, ((1, 1), (0, 0), (1, 1)))

    def apply_group(source):
        rimmed = with_halo(source, (("gy", 1),), 1)
        return stencil(jnp.pad(rimmed, ((1, 1), (0, 0), (1, 1))), block_coeff_padded, 0.0625)

    def group_total(values):
        return lax.psum(values, "gy")

    block_answer = conjugate(block_rhs, apply_group, group_total)
    coarse_answer = lax.dynamic_slice(
        block_answer,
        (lax.axis_index("gz") * depth, 0, lax.axis_index("gx") * cols),
        (depth, rows, cols),
    )
    coarse_padded = with_halo(coarse_answer, (("gx", 2), ("gy", 1), ("gz", 0)), 1)
    middle_iterate = middle_iterate + prolong(coarse_padded)
    middle_iterate, middle_rest = chebyshev(
        middle_iterate, middle_rhs - apply_middle(middle_iterate), apply_middle, middle_inverse
    )
    middle_padded = with_halo(middle_iterate, (("gx", 2), ("gy", 1), ("gz", 0)), 1)
    solution = fine_iterate + prolong(middle_padded)
    solution, residual = chebyshev(
        solution, right_side - apply_fine(solution), apply_fine, fine_inverse
    )
    return (solution, residual)


def solution(mesh):
    return jax.shard_map(
        local,
        mesh=mesh,
        in_specs=(P("gz", "gy", "gx"), P("gz", "gy", "gx"), P("gz", "gy", "gx")),
        out_specs=(P("gz", "gy", "gx"), P("gz", "gy", "gx")),
        check_vma=False,
    )
```

profile of v0, /device:TPU:1, one launch (start us, length us, event | category | flops | bytes accessed | tf_op | source)
XLA Modules:
  0.0 748.3 jit_solution(12663118546225069302)
XLA Ops:
  1.7 4.0 collective-permute-start
  8.0 4.0 collective-permute-start.5
  14.3 4.0 collective-permute-start.2
  20.5 4.6 collective-permute-start.7
  27.4 5.2 collective-permute-start.10
  35.4 3.6 collective-permute-start.11
  47.0 4.3 collective-permute-start.12
  53.2 3.8 collective-permute-done.13
  57.1 4.6 collective-permute-start.14
  63.1 10.5 %reshape.66 = f32[4,2,16,2,64,2]{5,4,3,2,1,0:T(8,128)} reshape(f32[8,32,128]{2,1,0:T(8,128)} %param.5) | data formatting | bytes 262144 | tf_op jit(solution)/shard_map/reshape | solution.py:62
  73.6 4.0 reduce_sum.145
  79.7 4.6 collective-permute-start.17
  90.4 4.0 collective-permute-start.24
  95.8 5.8 collective-permute-start.20
  103.1 5.5 collective-permute-start.26
  112.0 5.6 collective-permute-start.23
  123.7 9.8 %reshape.65 = f32[4,2,16,2,64,2]{5,4,3,2,1,0:T(8,128)} reshape(f32[8,32,128]{2,1,0:T(8,128)S(1)} %fusion.153) | data formatting | bytes 262144 | tf_op jit(solution)/shard_map/reshape | solution.py:62
  133.4 4.0 reduce_sum.144
  137.8 4.3 collective-permute-start.30
  146.8 5.5 collective-permute-start.32
  169.9 58.4 %all-gather.1 = f32[128,8,32]{2,1,0:T(8,128)S(1)} all-gather(f32[2,8,32]{2,1,0:T(8,128)S(1)} %broadcast_multiply_fusion.2), channel_id=3, replica_groups=mesh['gx'=4,'gy'=8,'gz'=16] {'gx','gz'}, dimensions={0}, use_global_device_ids=true | all-gather | bytes 133120 | tf_op jit(solution)/shard_map/all_gather | solution.py:153
  229.0 4.8 collective-permute-start.38
  235.2 5.5 collective-permute-start.42
  249.9 51.9 %all-gather = f32[128,8,32]{2,1,0:T(8,128)S(1)} all-gather(f32[2,8,32]{2,1,0:T(8,128)S(1)} %broadcast_multiply_fusion.3), channel_id=2, replica_groups=mesh['gx'=4,'gy'=8,'gz'=16] {'gx','gz'}, dimensions={0}, use_global_device_ids=true | all-gather | bytes 133120 | tf_op jit(solution)/shard_map/all_gather | solution.py:152
  302.5 5.2 collective-permute-start.44
  314.2 15.8 %all-reduce.7 = (f32[]{:T(128)}, f32[]{:T(128)}) all-reduce(f32[]{:T(128)} %multiply_reduce_fusion, f32[]{:T(128)} %get-tuple-element.38), channel_id=1, replica_groups=mesh['gx'=4,'gy'=8,'gz'=16] {'gy'}, use_global_device_ids=true, to_apply=%region_4.5 | all-reduce | flops 2 | bytes 16 | tf_op jit(solution)/shard_map/psum | solution.py:170
  332.0 11.5 %psum.86 = f32[]{:T(128)} all-reduce(f32[]{:T(128)} %multiply_reduce_fusion.9), channel_id=1, replica_groups=mesh['gx'=4,'gy'=8,'gz'=16] {'gy'}, use_global_device_ids=true, to_apply=%region_9.10 | all-reduce | flops 1 | bytes 8 | tf_op jit(solution)/shard_map/psum | solution.py:170
  354.5 14.0 %psum.87 = f32[]{:T(128)} all-reduce(f32[]{:T(128)} %get-tuple-element.36), channel_id=1, replica_groups=mesh['gx'=4,'gy'=8,'gz'=16] {'gy'}, use_global_device_ids=true, to_apply=%region_11.12 | all-reduce | flops 1 | bytes 8 | tf_op jit(solution)/shard_map/psum | solution.py:170
  370.5 11.8 %psum.88 = f32[]{:T(128)} all-reduce(f32[]{:T(128)} %get-tuple-element.34), channel_id=1, replica_groups=mesh['gx'=4,'gy'=8,'gz'=16] {'gy'}, use_global_device_ids=true, to_apply=%region_13.14 | all-reduce | flops 1 | bytes 8 | tf_op jit(solution)/shard_map/psum | solution.py:170
  393.1 12.9 %psum.89 = f32[]{:T(128)} all-reduce(f32[]{:T(128)} %get-tuple-element.32), channel_id=1, replica_groups=mesh['gx'=4,'gy'=8,'gz'=16] {'gy'}, use_global_device_ids=true, to_apply=%region_15.16 | all-reduce | flops 1 | bytes 8 | tf_op jit(solution)/shard_map/psum | solution.py:170
  408.0 12.3 %psum.90 = f32[]{:T(128)} all-reduce(f32[]{:T(128)} %get-tuple-element.30), channel_id=1, replica_groups=mesh['gx'=4,'gy'=8,'gz'=16] {'gy'}, use_global_device_ids=true, to_apply=%region_17.18 | all-reduce | flops 1 | bytes 8 | tf_op jit(solution)/shard_map/psum | solution.py:170
  429.8 14.2 %psum.91 = f32[]{:T(128)} all-reduce(f32[]{:T(128)} %get-tuple-element.28), channel_id=1, replica_groups=mesh['gx'=4,'gy'=8,'gz'=16] {'gy'}, use_global_device_ids=true, to_apply=%region_19.20 | all-reduce | flops 1 | bytes 8 | tf_op jit(solution)/shard_map/psum | solution.py:170
  446.0 11.3 %psum.92 = f32[]{:T(128)} all-reduce(f32[]{:T(128)} %get-tuple-element.26), channel_id=1, replica_groups=mesh['gx'=4,'gy'=8,'gz'=16] {'gy'}, use_global_device_ids=true, to_apply=%region_21.22 | all-reduce | flops 1 | bytes 8 | tf_op jit(solution)/shard_map/psum | solution.py:170
  467.8 13.5 %psum.93 = f32[]{:T(128)} all-reduce(f32[]{:T(128)} %get-tuple-element.24), channel_id=1, replica_groups=mesh['gx'=4,'gy'=8,'gz'=16] {'gy'}, use_global_device_ids=true, to_apply=%region_23.24 | all-reduce | flops 1 | bytes 8 | tf_op jit(solution)/shard_map/psum | solution.py:170
  483.3 11.9 %psum.94 = f32[]{:T(128)} all-reduce(f32[]{:T(128)} %multiply_reduce_fusion.1), channel_id=1, replica_groups=mesh['gx'=4,'gy'=8,'gz'=16] {'gy'}, use_global_device_ids=true, to_apply=%region_25.26 | all-reduce | flops 1 | bytes 8 | tf_op jit(solution)/shard_map/psum | solution.py:170
  506.0 13.9 %psum.95 = f32[]{:T(128)} all-reduce(f32[]{:T(128)} %fusion.65), channel_id=1, replica_groups=mesh['gx'=4,'gy'=8,'gz'=16] {'gy'}, use_global_device_ids=true, to_apply=%region_27.28 | all-reduce | flops 1 | bytes 8 | tf_op jit(solution)/shard_map/psum | solution.py:170
  534.1 54.9 %collective-permute-start.60 = (f32[1,10,34]{2,1,0:T(8,128)S(1)}, f32[1,10,34]{2,1,0:T(8,128)S(1)}, u32[]{:S(2)}, u32[]{:S(2)}) collective-permute-start(f32[1,10,34]{2,1,0:T(8,128)S(1)} %get-tuple-element.167), channel_id=1, source_target_pairs={{0,1},{1,2},{2,3},{3,4},{4,5},{5,6},{6,7},{7,8},{8,9},{9,10},{10,1... | collective-permute-start | bytes 4088 | tf_op jit(solution)/shard_map/ppermute | solution.py:21
  606.2 4.0 collective-permute-done.65
  612.6 3.8 collective-permute-start.67
  625.4 4.8 collective-permute-start.70
  637.7 5.9 collective-permute-start.73
  659.2 7.1 collective-permute-start.78
  676.0 4.0 collective-permute-done.81
  690.3 4.7 collective-permute-start.85
  700.5 3.8 collective-permute-done.87
  713.7 7.1 collective-permute-start.91
  725.9 3.8 collective-permute-done.93
  739.1 7.1 collective-permute-start.97
  (356 shorter events, 249.3 us)
Async XLA Ops:
  1.7 11.6 %collective-permute-start = (f32[8,32,1]{2,1,0:T(8,128)S(1)}, f32[8,32,1]{2,1,0:T(8,128)S(1)}, u32[]{:S(2)}, u32[]{:S(2)}) collective-permute-start(f32[8,32,1]{2,1,0:T(8,128)S(1)} %get-tuple-element.119), channel_id=1, source_target_pairs={{0,128},{128,256},{256,384},{1,129},{129,257},{257,385},{2,130},{1... | collective-permute-start | bytes 3080 | tf_op jit(solution)/shard_map/ppermute | solution.py:21
  5.7 7.7 %collective-permute-start.1 = (f32[8,32,1]{2,1,0:T(8,128)S(1)}, f32[8,32,1]{2,1,0:T(8,128)S(1)}, u32[]{:S(2)}, u32[]{:S(2)}) collective-permute-start(f32[8,32,1]{2,1,0:T(8,128)S(1)} %get-tuple-element.120), channel_id=1, source_target_pairs={{128,0},{256,128},{384,256},{129,1},{257,129},{385,257},{130,2},{2... | collective-permute-start | bytes 3080 | tf_op jit(solution)/shard_map/ppermute | solution.py:23
  8.0 11.6 %collective-permute-start.5 = (f32[8,32,1]{2,1,0:T(8,128)S(1)}, f32[8,32,1]{2,1,0:T(8,128)S(1)}, u32[]{:S(2)}, u32[]{:S(2)}) collective-permute-start(f32[8,32,1]{2,1,0:T(8,128)S(1)} %get-tuple-element.122), channel_id=1, source_target_pairs={{0,128},{128,256},{256,384},{1,129},{129,257},{257,385},{2,130},{1... | collective-permute-start | bytes 3080 | tf_op jit(solution)/shard_map/ppermute | solution.py:21
  12.1 7.6 %collective-permute-start.6 = (f32[8,32,1]{2,1,0:T(8,128)S(1)}, f32[8,32,1]{2,1,0:T(8,128)S(1)}, u32[]{:S(2)}, u32[]{:S(2)}) collective-permute-start(f32[8,32,1]{2,1,0:T(8,128)S(1)} %get-tuple-element.121), channel_id=1, source_target_pairs={{128,0},{256,128},{384,256},{129,1},{257,129},{385,257},{130,2},{2... | collective-permute-start | bytes 3080 | tf_op jit(solution)/shard_map/ppermute | solution.py:23
  14.3 12.2 %collective-permute-start.2 = (f32[8,1,130]{2,0,1:T(8,128)S(1)}, f32[8,1,130]{2,0,1:T(8,128)S(1)}, u32[]{:S(2)}, u32[]{:S(2)}) collective-permute-start(f32[8,1,130]{2,0,1:T(8,128)S(1)} %copy.636), channel_id=1, source_target_pairs={{0,16},{16,32},{32,48},{48,64},{64,80},{80,96},{96,112},{1,17},{17... | collective-permute-start | bytes 12488 | tf_op jit(solution)/shard_map/ppermute | solution.py:21
  18.3 8.2 %collective-permute-start.3 = (f32[8,1,130]{2,0,1:T(8,128)S(1)}, f32[8,1,130]{2,0,1:T(8,128)S(1)}, u32[]{:S(2)}, u32[]{:S(2)}) collective-permute-start(f32[8,1,130]{2,0,1:T(8,128)S(1)} %copy.637), channel_id=1, source_target_pairs={{16,0},{32,16},{48,32},{64,48},{80,64},{96,80},{112,96},{17,1},{33... | collective-permute-start | bytes 12488 | tf_op jit(solution)/shard_map/ppermute | solution.py:23
  20.5 14.0 %collective-permute-start.7 = (f32[8,1,130]{2,0,1:T(8,128)S(1)}, f32[8,1,130]{2,0,1:T(8,128)S(1)}, u32[]{:S(2)}, u32[]{:S(2)}) collective-permute-start(f32[8,1,130]{2,0,1:T(8,128)S(1)} %copy.638), channel_id=1, source_target_pairs={{0,16},{16,32},{32,48},{48,64},{64,80},{80,96},{96,112},{1,17},{17... | collective-permute-start | bytes 12488 | tf_op jit(solution)/shard_map/ppermute | solution.py:21
  25.2 9.3 %collective-permute-start.8 = (f32[8,1,130]{2,0,1:T(8,128)S(1)}, f32[8,1,130]{2,0,1:T(8,128)S(1)}, u32[]{:S(2)}, u32[]{:S(2)}) collective-permute-start(f32[8,1,130]{2,0,1:T(8,128)S(1)} %copy.639), channel_id=1, source_target_pairs={{16,0},{32,16},{48,32},{64,48},{80,64},{96,80},{112,96},{17,1},{33... | collective-permute-start | bytes 12488 | tf_op jit(solution)/shard_map/ppermute | solution.py:23
  27.4 13.6 %collective-permute-start.10 = (f32[1,34,130]{2,1,0:T(8,128)S(1)}, f32[1,34,130]{2,1,0:T(8,128)S(1)}, u32[]{:S(2)}, u32[]{:S(2)}) collective-permute-start(f32[1,34,130]{2,1,0:T(8,128)S(1)} %get-tuple-element.75), channel_id=1, source_target_pairs={{0,1},{1,2},{2,3},{3,4},{4,5},{5,6},{6,7},{7,8},{8,9},{9,10},{10,1... | collective-permute-start | bytes 53048 | tf_op jit(solution)/shard_map/ppermute | solution.py:21
  32.5 8.4 %collective-permute-start.4 = (f32[1,34,130]{2,1,0:T(8,128)S(1)}, f32[1,34,130]{2,1,0:T(8,128)S(1)}, u32[]{:S(2)}, u32[]{:S(2)}) collective-permute-start(f32[1,34,130]{2,1,0:T(8,128)S(1)} %get-tuple-element.76), channel_id=1, source_target_pairs={{1,0},{2,1},{3,2},{4,3},{5,4},{6,5},{7,6},{8,7},{9,8},{10,9},{11,1... | collective-permute-start | bytes 53048 | tf_op jit(solution)/shard_map/ppermute | solution.py:23
  47.0 6.2 collective-permute-start.12
  57.1 20.5 %collective-permute-start.14 = (f32[8,1,130]{2,0,1:T(8,128)S(1)}, f32[8,1,130]{2,0,1:T(8,128)S(1)}, u32[]{:S(2)}, u32[]{:S(2)}) collective-permute-start(f32[8,1,130]{2,0,1:T(8,128)S(1)} %copy.593), channel_id=1, source_target_pairs={{0,16},{16,32},{32,48},{48,64},{64,80},{80,96},{96,112},{1,17},{17... | collective-permute-start | bytes 12488 | tf_op jit(solution)/shard_map/ppermute | solution.py:21
  61.8 15.9 %collective-permute-start.15 = (f32[8,1,130]{2,0,1:T(8,128)S(1)}, f32[8,1,130]{2,0,1:T(8,128)S(1)}, u32[]{:S(2)}, u32[]{:S(2)}) collective-permute-start(f32[8,1,130]{2,0,1:T(8,128)S(1)} %copy.594), channel_id=1, source_target_pairs={{16,0},{32,16},{48,32},{64,48},{80,64},{96,80},{112,96},{17,1},{33... | collective-permute-start | bytes 12488 | tf_op jit(solution)/shard_map/ppermute | solution.py:23
  77.8 6.6 collective-permute-start.16
  85.9 9.8 %collective-permute-start.18 = (f32[8,32,1]{2,1,0:T(8,128)S(1)}, f32[8,32,1]{2,1,0:T(8,128)S(1)}, u32[]{:S(2)}, u32[]{:S(2)}) collective-permute-start(f32[8,32,1]{2,1,0:T(8,128)S(1)} %get-tuple-element.116), channel_id=1, source_target_pairs={{0,128},{128,256},{256,384},{1,129},{129,257},{257,385},{2,130},{1... | collective-permute-start | bytes 3080 | tf_op jit(solution)/shard_map/ppermute | solution.py:21
  89.0 6.7 collective-permute-start.19
  90.4 12.6 %collective-permute-start.24 = (f32[4,16,1]{2,1,0:T(8,128)S(1)}, f32[4,16,1]{2,1,0:T(8,128)S(1)}, u32[]{:S(2)}, u32[]{:S(2)}) collective-permute-start(f32[4,16,1]{2,1,0:T(8,128)S(1)} %get-tuple-element.161), channel_id=1, source_target_pairs={{0,128},{128,256},{256,384},{1,129},{129,257},{257,385},{2,130},{1... | collective-permute-start | bytes 776 | tf_op jit(solution)/shard_map/ppermute | solution.py:21
  94.4 8.6 %collective-permute-start.25 = (f32[4,16,1]{2,1,0:T(8,128)S(1)}, f32[4,16,1]{2,1,0:T(8,128)S(1)}, u32[]{:S(2)}, u32[]{:S(2)}) collective-permute-start(f32[4,16,1]{2,1,0:T(8,128)S(1)} %get-tuple-element.162), channel_id=1, source_target_pairs={{128,0},{256,128},{384,256},{129,1},{257,129},{385,257},{130,2},{2... | collective-permute-start | bytes 776 | tf_op jit(solution)/shard_map/ppermute | solution.py:23
  95.8 14.1 %collective-permute-start.20 = (f32[8,1,130]{2,0,1:T(8,128)S(1)}, f32[8,1,130]{2,0,1:T(8,128)S(1)}, u32[]{:S(2)}, u32[]{:S(2)}) collective-permute-start(f32[8,1,130]{2,0,1:T(8,128)S(1)} %copy.599), channel_id=1, source_target_pairs={{0,16},{16,32},{32,48},{48,64},{64,80},{80,96},{96,112},{1,17},{17... | collective-permute-start | bytes 12488 | tf_op jit(solution)/shard_map/ppermute | solution.py:21
  101.7 8.2 %collective-permute-start.21 = (f32[8,1,130]{2,0,1:T(8,128)S(1)}, f32[8,1,130]{2,0,1:T(8,128)S(1)}, u32[]{:S(2)}, u32[]{:S(2)}) collective-permute-start(f32[8,1,130]{2,0,1:T(8,128)S(1)} %copy.600), channel_id=1, source_target_pairs={{16,0},{32,16},{48,32},{64,48},{80,64},{96,80},{112,96},{17,1},{33... | collective-permute-start | bytes 12488 | tf_op jit(solution)/shard_map/ppermute | solution.py:23
  103.1 14.5 %collective-permute-start.26 = (f32[4,1,66]{2,1,0:T(1,128)S(1)}, f32[4,1,66]{2,1,0:T(1,128)S(1)}, u32[]{:S(2)}, u32[]{:S(2)}) collective-permute-start(f32[4,1,66]{2,1,0:T(1,128)S(1)} %get-tuple-element.143), channel_id=1, source_target_pairs={{0,16},{16,32},{32,48},{48,64},{64,80},{80,96},{96,112},{1,17},{17... | collective-permute-start | bytes 3176 | tf_op jit(solution)/shard_map/ppermute | solution.py:21
  108.6 9.0 %collective-permute-start.27 = (f32[4,1,66]{2,1,0:T(1,128)S(1)}, f32[4,1,66]{2,1,0:T(1,128)S(1)}, u32[]{:S(2)}, u32[]{:S(2)}) collective-permute-start(f32[4,1,66]{2,1,0:T(1,128)S(1)} %get-tuple-element.144), channel_id=1, source_target_pairs={{16,0},{32,16},{48,32},{64,48},{80,64},{96,80},{112,96},{17,1},{33... | collective-permute-start | bytes 3176 | tf_op jit(solution)/shard_map/ppermute | solution.py:23
  110.0 13.3 %collective-permute-start.22 = (f32[1,34,130]{2,1,0:T(8,128)S(1)}, f32[1,34,130]{2,1,0:T(8,128)S(1)}, u32[]{:S(2)}, u32[]{:S(2)}) collective-permute-start(f32[1,34,130]{2,1,0:T(8,128)S(1)} %get-tuple-element.71), channel_id=1, source_target_pairs={{1,0},{2,1},{3,2},{4,3},{5,4},{6,5},{7,6},{8,7},{9,8},{10,9},{11,1... | collective-permute-start | bytes 53048 | tf_op jit(solution)/shard_map/ppermute | solution.py:23
  112.0 11.3 %collective-permute-start.23 = (f32[1,34,130]{2,1,0:T(8,128)S(1)}, f32[1,34,130]{2,1,0:T(8,128)S(1)}, u32[]{:S(2)}, u32[]{:S(2)}) collective-permute-start(f32[1,34,130]{2,1,0:T(8,128)S(1)} %get-tuple-element.72), channel_id=1, source_target_pairs={{0,1},{1,2},{2,3},{3,4},{4,5},{5,6},{6,7},{7,8},{8,9},{9,10},{10,1... | collective-permute-start | bytes 53048 | tf_op jit(solution)/shard_map/ppermute | solution.py:21
  117.7 19.8 %collective-permute-start.28 = (f32[1,18,66]{2,1,0:T(8,128)S(1)}, f32[1,18,66]{2,1,0:T(8,128)S(1)}, u32[]{:S(2)}, u32[]{:S(2)}) collective-permute-start(f32[1,18,66]{2,1,0:T(8,128)S(1)} %get-tuple-element.131), channel_id=1, source_target_pairs={{1,0},{2,1},{3,2},{4,3},{5,4},{6,5},{7,6},{8,7},{9,8},{10,9},{11,1... | collective-permute-start | bytes 14264 | tf_op jit(solution)/shard_map/ppermute | solution.py:23
  119.6 17.8 %collective-permute-start.29 = (f32[1,18,66]{2,1,0:T(8,128)S(1)}, f32[1,18,66]{2,1,0:T(8,128)S(1)}, u32[]{:S(2)}, u32[]{:S(2)}) collective-permute-start(f32[1,18,66]{2,1,0:T(8,128)S(1)} %get-tuple-element.132), channel_id=1, source_target_pairs={{0,1},{1,2},{2,3},{3,4},{4,5},{5,6},{6,7},{7,8},{8,9},{9,10},{10,1... | collective-permute-start | bytes 14264 | tf_op jit(solution)/shard_map/ppermute | solution.py:21
  146.8 8.0 %collective-permute-start.32 = (f32[4,1,66]{2,1,0:T(1,128)S(1)}, f32[4,1,66]{2,1,0:T(1,128)S(1)}, u32[]{:S(2)}, u32[]{:S(2)}) collective-permute-start(f32[4,1,66]{2,1,0:T(1,128)S(1)} %get-tuple-element.142), channel_id=1, source_target_pairs={{0,16},{16,32},{32,48},{48,64},{64,80},{80,96},{96,112},{1,17},{17... | collective-permute-start | bytes 3176 | tf_op jit(solution)/shard_map/ppermute | solution.py:21
  158.2 6.4 collective-permute-start.34
  165.7 63.1 %collective-permute-start.36 = (f32[4,16,1]{2,1,0:T(8,128)S(1)}, f32[4,16,1]{2,1,0:T(8,128)S(1)}, u32[]{:S(2)}, u32[]{:S(2)}) collective-permute-start(f32[4,16,1]{2,1,0:T(8,128)S(1)} %get-tuple-element.158), channel_id=1, source_target_pairs={{0,128},{128,256},{256,384},{1,129},{129,257},{257,385},{2,130},{1... | collective-permute-start | bytes 776 | tf_op jit(solution)/shard_map/ppermute | solution.py:21
  168.6 60.3 %collective-permute-start.37 = (f32[4,16,1]{2,1,0:T(8,128)S(1)}, f32[4,16,1]{2,1,0:T(8,128)S(1)}, u32[]{:S(2)}, u32[]{:S(2)}) collective-permute-start(f32[4,16,1]{2,1,0:T(8,128)S(1)} %get-tuple-element.157), channel_id=1, source_target_pairs={{128,0},{256,128},{384,256},{129,1},{257,129},{385,257},{130,2},{2... | collective-permute-start | bytes 776 | tf_op jit(solution)/shard_map/ppermute | solution.py:23
  229.0 13.0 %collective-permute-start.38 = (f32[4,1,66]{2,1,0:T(1,128)S(1)}, f32[4,1,66]{2,1,0:T(1,128)S(1)}, u32[]{:S(2)}, u32[]{:S(2)}) collective-permute-start(f32[4,1,66]{2,1,0:T(1,128)S(1)} %get-tuple-element.140), channel_id=1, source_target_pairs={{0,16},{16,32},{32,48},{48,64},{64,80},{80,96},{96,112},{1,17},{17... | collective-permute-start | bytes 3176 | tf_op jit(solution)/shard_map/ppermute | solution.py:21
  233.8 8.1 %collective-permute-start.39 = (f32[4,1,66]{2,1,0:T(1,128)S(1)}, f32[4,1,66]{2,1,0:T(1,128)S(1)}, u32[]{:S(2)}, u32[]{:S(2)}) collective-permute-start(f32[4,1,66]{2,1,0:T(1,128)S(1)} %get-tuple-element.139), channel_id=1, source_target_pairs={{16,0},{32,16},{48,32},{64,48},{80,64},{96,80},{112,96},{17,1},{33... | collective-permute-start | bytes 3176 | tf_op jit(solution)/shard_map/ppermute | solution.py:23
  235.2 12.5 %collective-permute-start.42 = (f32[32,1,128]{2,1,0:T(1,128)S(1)}, f32[32,1,128]{2,1,0:T(1,128)S(1)}, u32[]{:S(2)}, u32[]{:S(2)}) collective-permute-start(f32[32,1,128]{2,1,0:T(1,128)S(1)} %get-tuple-element.112), channel_id=1, source_target_pairs={{0,16},{16,32},{32,48},{48,64},{64,80},{80,96},{96,112},{1,17},{17... | collective-permute-start | bytes 49160 | tf_op jit(solution)/shard_map/ppermute | solution.py:21
  240.6 7.0 collective-permute-start.43
  242.1 6.0 collective-permute-start.40
  302.5 7.3 collective-permute-start.44
  534.1 56.8 %collective-permute-start.60 = (f32[1,10,34]{2,1,0:T(8,128)S(1)}, f32[1,10,34]{2,1,0:T(8,128)S(1)}, u32[]{:S(2)}, u32[]{:S(2)}) collective-permute-start(f32[1,10,34]{2,1,0:T(8,128)S(1)} %get-tuple-element.167), channel_id=1, source_target_pairs={{0,1},{1,2},{2,3},{3,4},{4,5},{5,6},{6,7},{7,8},{8,9},{9,10},{10,1... | collective-permute-start | bytes 4088 | tf_op jit(solution)/shard_map/ppermute | solution.py:21
  610.3 6.2 collective-permute-start.66
  625.4 6.2 collective-permute-start.70
  634.9 8.7 %collective-permute-start.72 = (f32[1,18,66]{2,1,0:T(8,128)S(1)}, f32[1,18,66]{2,1,0:T(8,128)S(1)}, u32[]{:S(2)}, u32[]{:S(2)}) collective-permute-start(f32[1,18,66]{2,1,0:T(8,128)S(1)} %get-tuple-element.123), channel_id=1, source_target_pairs={{1,0},{2,1},{3,2},{4,3},{5,4},{6,5},{7,6},{8,7},{9,8},{10,9},{11,1... | collective-permute-start | bytes 14264 | tf_op jit(solution)/shard_map/ppermute | solution.py:23
  637.7 6.8 collective-permute-start.73
  659.2 9.0 %collective-permute-start.78 = (f32[1,18,66]{2,1,0:T(8,128)S(1)}, f32[1,18,66]{2,1,0:T(8,128)S(1)}, u32[]{:S(2)}, u32[]{:S(2)}) collective-permute-start(f32[1,18,66]{2,1,0:T(8,128)S(1)} %get-tuple-element.147), channel_id=1, source_target_pairs={{0,1},{1,2},{2,3},{3,4},{4,5},{5,6},{6,7},{7,8},{8,9},{9,10},{10,1... | collective-permute-start | bytes 14264 | tf_op jit(solution)/shard_map/ppermute | solution.py:21
  674.0 5.9 collective-permute-start.81
  687.5 7.6 %collective-permute-start.84 = (f32[1,34,130]{2,1,0:T(8,128)S(1)}, f32[1,34,130]{2,1,0:T(8,128)S(1)}, u32[]{:S(2)}, u32[]{:S(2)}) collective-permute-start(f32[1,34,130]{2,1,0:T(8,128)S(1)} %get-tuple-element.69), channel_id=1, source_target_pairs={{1,0},{2,1},{3,2},{4,3},{5,4},{6,5},{7,6},{8,7},{9,8},{10,9},{11,1... | collective-permute-start | bytes 53048 | tf_op jit(solution)/shard_map/ppermute | solution.py:23
  711.8 9.0 %collective-permute-start.90 = (f32[1,34,130]{2,1,0:T(8,128)S(1)}, f32[1,34,130]{2,1,0:T(8,128)S(1)}, u32[]{:S(2)}, u32[]{:S(2)}) collective-permute-start(f32[1,34,130]{2,1,0:T(8,128)S(1)} %get-tuple-element.67), channel_id=1, source_target_pairs={{1,0},{2,1},{3,2},{4,3},{5,4},{6,5},{7,6},{8,7},{9,8},{10,9},{11,1... | collective-permute-start | bytes 53048 | tf_op jit(solution)/shard_map/ppermute | solution.py:23
  713.7 8.2 %collective-permute-start.91 = (f32[1,34,130]{2,1,0:T(8,128)S(1)}, f32[1,34,130]{2,1,0:T(8,128)S(1)}, u32[]{:S(2)}, u32[]{:S(2)}) collective-permute-start(f32[1,34,130]{2,1,0:T(8,128)S(1)} %get-tuple-element.68), channel_id=1, source_target_pairs={{0,1},{1,2},{2,3},{3,4},{4,5},{5,6},{6,7},{7,8},{8,9},{9,10},{10,1... | collective-permute-start | bytes 53048 | tf_op jit(solution)/shard_map/ppermute | solution.py:21
  737.2 9.8 %collective-permute-start.96 = (f32[1,34,130]{2,1,0:T(8,128)S(1)}, f32[1,34,130]{2,1,0:T(8,128)S(1)}, u32[]{:S(2)}, u32[]{:S(2)}) collective-permute-start(f32[1,34,130]{2,1,0:T(8,128)S(1)} %get-tuple-element.65), channel_id=1, source_target_pairs={{1,0},{2,1},{3,2},{4,3},{5,4},{6,5},{7,6},{8,7},{9,8},{10,9},{11,1... | collective-permute-start | bytes 53048 | tf_op jit(solution)/shard_map/ppermute | solution.py:23
  739.1 8.2 %collective-permute-start.97 = (f32[1,34,130]{2,1,0:T(8,128)S(1)}, f32[1,34,130]{2,1,0:T(8,128)S(1)}, u32[]{:S(2)}, u32[]{:S(2)}) collective-permute-start(f32[1,34,130]{2,1,0:T(8,128)S(1)} %get-tuple-element.66), channel_id=1, source_target_pairs={{0,1},{1,2},{2,3},{3,4},{4,5},{5,6},{6,7},{7,8},{8,9},{9,10},{10,1... | collective-permute-start | bytes 53048 | tf_op jit(solution)/shard_map/ppermute | solution.py:21
  (70 other events, 4151.5 us)
where the time goes:
time: 758 us; the launch traced here: 748 us
  starting transfers between devices  319 us (42%)
  blocking collectives  253 us (33%)
  waiting for transfers between devices  94.7 us (12%)
  other arithmetic  35.7 us (5%)
  local copies, waits for them, and re-layouts  28 us (4%)
  between operations  17.2 us (2%)
    ppermute x49, starting transfers between devices, with_halo(): lax.ppermute(tail, axis, [(i, (i + 1) % count) for i in range(ends)])  243 us
    psum x11, blocking collectives, group_total(): return lax.psum(values, 'gy')  143 us
    ppermute x49, waiting for transfers between devices, with_halo(): lax.ppermute(head, axis, [((i + 1) % count, i) for i in range(ends)])  85.8 us
    ppermute x49, starting transfers between devices, with_halo(): lax.ppermute(head, axis, [((i + 1) % count, i) for i in range(ends)])  76.2 us
    all_gather x1, blocking collectives, local(): lax.all_gather(kappa_two[None], ('gx', 'gz'), axis=0, tiled=True)  58.4 us
    all_gather x1, blocking collectives, local(): lax.all_gather(coarse_rhs[None], ('gx', 'gz'), axis=0, tiled=True)  51.9 us
    reshape x3, local copies, waits for them, and re-layouts, coarsen(): source.reshape(depth // 2, 2, rows // 2, 2, cols // 2, 2)  21.4 us
  transfers between devices with their start and end apart: 98, of which 38 were waited for; matrix products, arithmetic and copies ran while one was open for 5% of the time, Pallas kernels for 0%

commit v1 on v0

v1 whole, which is shorter than its diff:
```python
import jax
import jax.numpy as jnp
from jax import lax
from jax.experimental import pallas as pl
from jax.experimental.pallas import tpu as pltpu
from jax.sharding import PartitionSpec as P


ITERS = 6
THETA = 1.25
DELTA = 0.75
SIGMA = THETA / DELTA
RHO = 1.0 / SIGMA
RHO_NEXT = 1.0 / (2.0 * SIGMA - RHO)
FIRST = 1.0 / THETA
KEEP = RHO_NEXT * RHO
GAIN = 2.0 * RHO_NEXT / DELTA

F32 = jnp.float32
BF16 = jnp.bfloat16
VMEM = pl.BlockSpec(memory_space=pltpu.VMEM)
LIMIT = 40 * 1024 * 1024


def shift(value, by, axis):
    return pltpu.roll(value, by % value.shape[axis], axis)


def ahead(value, axis):
    return shift(value, -1, axis)


def behind(value, axis):
    return shift(value, 1, axis)


def iota(shape, axis):
    return lax.broadcasted_iota(jnp.int32, shape, axis)


def exact_dot(value, matrix):
    high = value.astype(BF16)
    rest = value - high.astype(F32)
    middle = rest.astype(BF16)
    low = (rest - middle.astype(F32)).astype(BF16)
    parts = [jnp.dot(part, matrix, preferred_element_type=F32) for part in (low, middle, high)]
    return parts[0] + parts[1] + parts[2]


def pick(condition, number):
    return jnp.where(condition, jnp.float32(number), jnp.float32(0.0))


def refine_matrix(size, out_size):
    parent = iota((size, out_size), 0)
    child = iota((size, out_size), 1)
    own = lax.shift_right_arithmetic(child, 1)
    other = (own + 2 * (child & 1) - 1 + size) & (size - 1)
    wide = out_size // 2
    if wide < size:
        own = jnp.where(child >= out_size * 3 // 4, own + size - wide, own)
        other = (own + 2 * (child & 1) - 1 + size) & (size - 1)
    return (pick(parent == own, 0.75) + pick(parent == other, 0.25)).astype(BF16)


def xpack_kernel(mid, low, high, ylow, yhigh, window, to_left, to_right):
    for a in range(3):
        window[a * 24 : a * 24 + 8, 1:5] = low[a].reshape(8, 4, 8, 128)
        window[a * 24 + 8 : a * 24 + 16, 1:5] = mid[a].reshape(8, 4, 8, 128)
        window[a * 24 + 16 : a * 24 + 24, 1:5] = high[a].reshape(8, 4, 8, 128)
        window[a * 24 : a * 24 + 24, 0] = ylow[a]
        window[a * 24 : a * 24 + 24, 5] = yhigh[a]
    slot = lax.shift_right_logical(iota((8, 128), 1), 3)

    def group(i, carry):
        for packed in range(3):
            left = jnp.zeros((8, 128), F32)
            right = jnp.zeros((8, 128), F32)
            for s in range(16):
                j = packed * 16 + s
                tile = window[8 * i + j // 6, j % 6]
                left = jnp.where(slot == s, shift(tile, 8 * s, 1), left)
                right = jnp.where(slot == s, shift(tile, 8 * s + 8, 1), right)
            to_left[3 * i + packed] = left
            to_right[3 * i + packed] = right
        return carry

    lax.fori_loop(0, 9, group, 0)


def plane(ref, z):
    return ref[pl.ds(6 * z, 6)].reshape(48, 256)


def put(ref, z, value):
    ref[pl.ds(6 * z, 6)] = value.reshape(6, 8, 256)


def inner_flux(v, wx, wy):
    fx = wx * (ahead(v, 1) - v)
    fy = wy * (ahead(v, 0) - v)
    return (fx - behind(fx, 1)) + (fy - behind(fy, 0))


def sweep(first, last, source, wx, wy, wz, step):
    v = plane(source, first)
    carry = (v, plane(wz, first - 1) * (v - plane(source, first - 1)))

    def body(z, carry):
        v, below = carry
        after = plane(source, z + 1)
        above = plane(wz, z) * (after - v)
        step(z, v, inner_flux(v, plane(wx, z), plane(wy, z)) + (above - below))
        return (after, above)

    lax.fori_loop(first, last + 1, body, carry)


def zpair(low_face):
    pad = jnp.zeros((1,) + low_face.shape[1:], F32)
    return jnp.concatenate([low_face, pad], 0) - jnp.concatenate([pad, low_face], 0)


def middle_weights(kappa):
    half = 0.125 * kappa
    wx = half + ahead(half, 2)
    wy = half + ahead(half, 1)
    wz = half[:-1] + half[1:]
    pad = jnp.zeros((1,) + half.shape[1:], F32)
    diag = wx + behind(wx, 2) + wy + behind(wy, 1)
    diag = diag + jnp.concatenate([wz, pad], 0) + jnp.concatenate([pad, wz], 0)
    inside = kappa > 0.0
    inverse = jnp.where(inside, 1.0 / jnp.where(inside, diag, 1.0), 0.0)
    return wx, wy, wz, inverse


def middle_minus(v, weights):
    wx, wy, wz, _ = weights
    fx = wx * (ahead(v, 2) - v)
    fy = wy * (ahead(v, 1) - v)
    return (fx - behind(fx, 2)) + (fy - behind(fy, 1)) + zpair(wz * (v[1:] - v[:-1]))


def down_kernel(
    window, from_left, from_right,
    share, um_out, mr_out, k1_out, iterate, right, wx, wy, wz, inverse,
    kappa, guess, rest, update, second, sums_a, sums_b, line,
):
    lane = iota((8, 128), 1)

    def unpack(i, dest, base):
        for packed in range(3):
            hi = from_right[base * 9 + 3 * i + packed]
            lo = from_left[base * 9 + 3 * i + packed]
            for s in range(16):
                j = packed * 16 + s
                edge = jnp.where(lane < 8, shift(hi, -8 * s, 1), 0.0)
                edge = jnp.where(lane >= 120, shift(lo, 120 - 8 * s, 1), edge)
                dest[48 * i + j, :, 0:128] = window[base * 24 + 8 * i + j // 6, j % 6]
                dest[48 * i + j, :, 128:256] = edge

    def unpack_all(i, carry):
        unpack(i, guess, 0)
        unpack(i, right, 1)
        unpack(i, kappa, 2)
        return carry

    lax.fori_loop(0, 3, unpack_all, 0)

    def weights(z, carry):
        half, below = carry
        after = 0.5 * plane(kappa, z + 1)
        x = half + ahead(half, 1)
        y = half + ahead(half, 0)
        above = half + after
        diag = x + behind(x, 1) + y + behind(y, 0) + above + below
        inside = half > 0.0
        put(wx, z, x)
        put(wy, z, y)
        put(wz, z, above)
        put(inverse, z, jnp.where(inside, 1.0 / jnp.where(inside, diag, 1.0), 0.0))
        return (after, above)

    half0 = 0.5 * plane(kappa, 0)
    half1 = 0.5 * plane(kappa, 1)
    put(wz, 0, half0 + half1)
    lax.fori_loop(1, 23, weights, (half1, half0 + half1))

    def first(z, v, minus):
        r = plane(right, z) + minus
        put(rest, z, r)
        put(update, z, FIRST * r * plane(inverse, z))

    sweep(1, 22, guess, wx, wy, wz, first)

    def next_step(z, v, minus):
        r = plane(rest, z) + minus
        d = KEEP * v + GAIN * (r * plane(inverse, z))
        put(rest, z, r)
        put(second, z, d)
        put(iterate, z, plane(guess, z) + v + d)

    sweep(2, 21, update, wx, wy, wz, next_step)

    def last(z, v, minus):
        put(rest, z, plane(rest, z) + minus)

    sweep(3, 20, second, wx, wy, wz, last)

    def add_pairs(ref, start, count, at):
        def body(m, carry):
            pair = plane(ref, start + 2 * m) + plane(ref, start + 2 * m + 1)
            rows = pl.ds(pl.multiple_of((at + m) * 48, 48), 48)
            sums_a[rows, :] = pair[:, :128]
            sums_b[rows, :] = pair[:, 128:]
            return carry

        lax.fori_loop(0, count, body, 0)

    add_pairs(rest, 4, 8, 0)
    add_pairs(kappa, 0, 12, 8)

    def fold(ref):
        return ref[pl.ds(0, 480, stride=2), :] + ref[pl.ds(1, 480, stride=2), :]

    coarsen = pick(lax.shift_right_logical(iota((256, 128), 0), 1) == iota((256, 128), 1), 0.125)
    both = exact_dot(jnp.concatenate([fold(sums_a), fold(sums_b)], 1), coarsen.astype(BF16))
    both = both.reshape(20, 24, 128)
    kappa_one = both[8:]
    pad = jnp.zeros((2, 24, 128), F32)
    rhs = jnp.concatenate([pad, both[:8], pad], 0)
    weights_one = middle_weights(kappa_one)
    inverse_one = weights_one[3]
    d = FIRST * (rhs * inverse_one)
    r = rhs + middle_minus(d, weights_one)
    d2 = KEEP * d + GAIN * (r * inverse_one)
    r = r + middle_minus(d2, weights_one)
    um_out[...] = d + d2
    mr_out[...] = rhs
    k1_out[...] = kappa_one

    cell = iota((128, 128), 0)
    place = iota((128, 128), 1)
    total = jnp.zeros((24, 128), F32)
    for q, field in enumerate((r[4] + r[5], r[6] + r[7], kappa_one[4] + kappa_one[5], kappa_one[6] + kappa_one[7])):
        to = (cell < 64) & (lax.shift_right_logical(cell, 1) + 32 * q == place)
        total = total + exact_dot(field, pick(to, 0.125).astype(BF16))
    line[...] = total
    cells = line[pl.ds(4, 8, stride=2), :] + line[pl.ds(5, 8, stride=2), :]
    cells = pltpu.roll(cells, 32 * lax.axis_index("gx"), 1)
    share[...] = jnp.broadcast_to(cells[None], (128, 8, 128))


def cplane(ref, z):
    return ref[pl.ds(8 * z, 8)].reshape(64, 128)


def cput(ref, z, value):
    ref[pl.ds(8 * z, 8)] = value.reshape(8, 8, 128)


def coarse_kernel(gathered, out, kappa, wx, wy, wz, diag, rest, direction, image, answer):
    lane = iota((8, 128), 1)
    group = lax.shift_right_logical(lane, 5)
    nothing = jnp.zeros((64, 128), F32)
    for ref in (kappa, direction):
        cput(ref, 0, nothing)
        cput(ref, 33, nothing)
    cput(wz, 0, nothing)
    answer[...] = jnp.zeros_like(answer)

    def assemble(gz, carry):
        for gy in range(8):
            pieces = [gathered[gx, gy * 16 + gz] for gx in range(4)]
            for q in range(4):
                merged = pieces[0]
                for gx in range(1, 4):
                    merged = jnp.where(group == (q + gx) % 4, pieces[gx], merged)
                merged = shift(merged, -32 * q, 1)
                if q < 2:
                    rest[(2 * gz + q) * 8 + gy] = merged
                    direction[(2 * gz + q + 1) * 8 + gy] = merged
                else:
                    kappa[(2 * gz + q - 1) * 8 + gy] = merged
        return carry

    lax.fori_loop(0, 16, assemble, 0)
    inner_x = iota((64, 128), 1) < 127
    inner_y = iota((64, 128), 0) < 63
    first_x = iota((64, 128), 1) > 0
    first_y = iota((64, 128), 0) > 0

    def weights(z, total):
        half = 0.03125 * cplane(kappa, z + 1)
        before = 0.03125 * cplane(kappa, z)
        after = 0.03125 * cplane(kappa, z + 2)
        x = jnp.where(inner_x, ahead(half, 1), 0.0)
        y = jnp.where(inner_y, ahead(half, 0), 0.0)
        cput(wx, z, jnp.where(inner_x, half + x, 0.0))
        cput(wy, z, jnp.where(inner_y, half + y, 0.0))
        cput(wz, z + 1, half + after)
        x = x + jnp.where(first_x, behind(half, 1), 0.0)
        y = y + jnp.where(first_y, behind(half, 0), 0.0)
        cput(diag, z, 6.0 * half + x + y + (before + after))
        r = cplane(rest, z)
        return total + (r * r).reshape(8, 8, 128).sum(0)

    zero = jnp.zeros((8, 128), F32)

    def whole(total):
        return jnp.sum(jnp.sum(total, axis=0, keepdims=True), axis=1, keepdims=True)

    norm = whole(lax.fori_loop(0, 32, weights, zero))

    def apply(z, total):
        v = cplane(direction, z + 1)
        x = cplane(wx, z)
        y = cplane(wy, z)
        w = cplane(diag, z) * v
        w = w - (x * ahead(v, 1) + behind(x * v, 1))
        w = w - (y * ahead(v, 0) + behind(y * v, 0))
        w = w - (cplane(wz, z + 1) * cplane(direction, z + 2) + cplane(wz, z) * cplane(direction, z))
        cput(image, z, w)
        return total + (v * w).reshape(8, 8, 128).sum(0)

    def add_answer(z, alpha):
        at = pl.ds((z + 3) * 10 + 1, 8)
        answer[at] = answer[at] + (alpha * cplane(direction, z + 1)).reshape(8, 8, 128)

    for repeat in range(ITERS):
        alpha = norm / whole(lax.fori_loop(0, 32, apply, zero))
        if repeat + 1 < ITERS:

            def step(z, total):
                add_answer(z, alpha)
                r = cplane(rest, z) - alpha * cplane(image, z)
                cput(rest, z, r)
                return total + (r * r).reshape(8, 8, 128).sum(0)

            norm_next = whole(lax.fori_loop(0, 32, step, zero))
            beta = norm_next / norm

            def turn(z, carry):
                cput(direction, z + 1, cplane(rest, z) + beta * cplane(direction, z + 1))
                return carry

            lax.fori_loop(0, 32, turn, 0)
            norm = norm_next
        else:

            def finish(z, carry):
                add_answer(z, alpha)
                return carry

            lax.fori_loop(0, 32, finish, 0)

    gx = lax.axis_index("gx")
    gy = lax.axis_index("gy")
    gz = lax.axis_index("gz")
    wide = iota((24, 128), 1)
    position = jnp.where(wide < 64, wide, wide - 128) + 32 * gx
    known = (position >= 0) & (position < 128)
    for z in range(8):
        block = answer[pl.ds((2 * gz + z) * 10 + gy, 3)].reshape(24, 128)
        out[z] = jnp.where(known, pltpu.roll(block, (128 - 32 * gx) & 127, 1), 0.0)


def up_kernel(
    coarse, um, mr, k1, iterate, right, wx, wy, wz, inverse,
    solution_out, residual_out,
    line, fine_a, fine_b, current, rest, update, second,
):
    c = coarse[...]
    even = 0.75 * c[1:7] + 0.25 * c[0:6]
    odd = 0.75 * c[1:7] + 0.25 * c[2:8]
    c = jnp.stack([even, odd], 1).reshape(12, 24, 128)
    matrix = refine_matrix(128, 128)
    line[pl.ds(0, 288, stride=2), :] = exact_dot((0.75 * c + 0.25 * behind(c, 1)).reshape(288, 128), matrix)
    line[pl.ds(1, 288, stride=2), :] = exact_dot((0.75 * c + 0.25 * ahead(c, 1)).reshape(288, 128), matrix)
    correction = shift(line[...].reshape(12, 48, 128), -12, 1)[:, :24]

    kappa_one = k1[...]
    weights = middle_weights(kappa_one)
    inverse_one = weights[3]
    u = jnp.where(kappa_one > 0.0, um[...] + correction, 0.0)
    r = mr[...] + middle_minus(u, weights)
    d = FIRST * (r * inverse_one)
    u = u + d
    r = r + middle_minus(d, weights)
    u = u + (KEEP * d + GAIN * (r * inverse_one))

    even = 0.75 * u[2:10] + 0.25 * u[1:9]
    odd = 0.75 * u[2:10] + 0.25 * u[3:11]
    m = jnp.stack([even, odd], 1).reshape(16, 24, 128)
    matrix = refine_matrix(128, 256)
    for parity, near in enumerate((behind(m, 1), ahead(m, 1))):
        value = exact_dot((0.75 * m + 0.25 * near).reshape(384, 128), matrix)
        fine_a[pl.ds(parity, 384, stride=2), :] = value[:, :128]
        fine_b[pl.ds(parity, 384, stride=2), :] = value[:, 128:]

    def begin(z, carry):
        rows = pl.ds(pl.multiple_of((z - 4) * 48, 48), 48)
        fine = jnp.concatenate([fine_a[rows, :], fine_b[rows, :]], 1)
        put(current, z, jnp.where(plane(inverse, z) > 0.0, plane(iterate, z) + fine, 0.0))
        return carry

    lax.fori_loop(4, 20, begin, 0)

    def first(z, v, minus):
        r = plane(right, z) + minus
        put(rest, z, r)
        put(update, z, FIRST * r * plane(inverse, z))

    sweep(5, 18, current, wx, wy, wz, first)

    def next_step(z, v, minus):
        r = plane(rest, z) + minus
        d = KEEP * v + GAIN * (r * plane(inverse, z))
        put(rest, z, r)
        put(second, z, d)
        put(current, z, plane(current, z) + v + d)

    sweep(6, 17, update, wx, wy, wz, next_step)

    def last(z, v, minus):
        residual_out[z - 8] = (plane(rest, z) + minus)[8:40, :128]
        solution_out[z - 8] = plane(current, z)[8:40, :128]

    sweep(8, 15, second, wx, wy, wz, last)


def run(kernel, outs, scratch, *args):
    return pl.pallas_call(
        kernel,
        out_shape=[jax.ShapeDtypeStruct(shape, F32) for shape in outs],
        in_specs=[VMEM] * len(args),
        out_specs=[VMEM] * len(outs),
        scratch_shapes=[pltpu.VMEM(shape, F32) for shape in scratch],
        compiler_params=pltpu.CompilerParams(vmem_limit_bytes=LIMIT),
    )(*args)


def up(axis):
    return [(i, i + 1) for i in range(lax.axis_size(axis) - 1)]


def down(axis):
    return [(i + 1, i) for i in range(lax.axis_size(axis) - 1)]


def both_ways(to_low, to_high, axis):
    return lax.ppermute(to_high, axis, up(axis)), lax.ppermute(to_low, axis, down(axis))


def local(right_side, guess, coefficient):
    mine = jnp.stack([guess, right_side, coefficient])
    low, high = both_ways(mine, mine, "gz")
    column = jnp.concatenate([low, mine, high], 1)
    ylow, yhigh = both_ways(column[:, :, :8], column[:, :, 24:], "gy")
    window, to_left, to_right = run(
        xpack_kernel, [(72, 6, 8, 128), (27, 8, 128), (27, 8, 128)], [], mine, low, high, ylow, yhigh
    )
    from_left, from_right = both_ways(to_left, to_right, "gx")

    fine = (144, 8, 256)
    middle = (12, 24, 128)
    share, um, mr, k1, *arrays = run(
        down_kernel,
        [(128, 8, 128), middle, middle, middle] + [fine] * 6,
        [fine] * 5 + [(960, 128)] * 2 + [(24, 128)],
        window, from_left, from_right,
    )
    plane_of = lax.all_to_all(share, ("gy", "gz"), 0, 0)
    whole = lax.all_to_all(jnp.broadcast_to(plane_of[None], (4, 128, 8, 128)), "gx", 0, 0)

    pair = jnp.stack([um, mr])[:, 4:8, 4:20, :64]
    low, high = both_ways(pair, pair, "gz")
    pair = jnp.concatenate([low, pair, high], 1)
    low, high = both_ways(pair[:, :, :4], pair[:, :, 12:], "gy")
    pair = jnp.concatenate([low, pair, high], 2)
    low, high = both_ways(pair[..., :4], pair[..., 60:], "gx")
    pair = jnp.concatenate([pair, high, jnp.zeros((2, 12, 24, 56), F32), low], 3)

    coarse_grid = (256, 8, 128)
    padded = (272, 8, 128)
    coarse = run(
        coarse_kernel,
        [(8, 24, 128)],
        [padded] + [coarse_grid] * 2 + [padded] + [coarse_grid] * 2 + [padded, coarse_grid, (380, 8, 128)],
        whole,
    )[0]
    solution, residual = run(
        up_kernel,
        [(8, 32, 128)] * 2,
        [(576, 128)] + [(768, 128)] * 2 + [fine] * 4,
        coarse, pair[0], pair[1], k1, *arrays,
    )
    return solution, residual


def solution(mesh):
    spec = P("gz", "gy", "gx")
    return jax.shard_map(
        local, mesh=mesh, in_specs=(spec, spec, spec), out_specs=(spec, spec), check_vma=False
    )
```

time: 758 us -> 178 us (0.23); the launches traced: 748 us -> 177 us
  starting transfers between devices: 319 us -> 36.9 us
  blocking collectives: 253 us -> 40.7 us
  waiting for transfers between devices: 94.7 us -> 29.2 us
  Pallas kernels: 0 us -> 53.4 us
  other arithmetic: 35.7 us -> 3.05 us
  between operations: 17.2 us -> 0.86 us
  local copies, waits for them, and re-layouts: 28 us -> 12.7 us
    ppermute x98 -> x12, starting transfers between devices: 319 us -> 33.1 us  [the longest x6 17.3 us: both_ways(): lax.ppermute(to_high, axis, up(axis))]
    psum x11 -> x0, blocking collectives: 143 us -> none  [group_total(): return lax.psum(values, 'gy')]
    all_gather x2 -> x0, blocking collectives: 110 us -> none  [the longest x1 58.4 us: local(): lax.all_gather(kappa_two[None], ('gx', 'gz'), axis=0, tiled=True)]
    ppermute x98 -> x12, waiting for transfers between devices: 94.7 us -> 29.2 us  [the longest x6 21.3 us: both_ways(): lax.ppermute(to_low, axis, down(axis))]
    pallas_call x0 -> x4, Pallas kernels: none -> 53.4 us  [run(): pl.pallas_call(kernel, out_shape=[jax.ShapeDtypeStruct(shape, F32) for sh...]
    all_to_all x0 -> x1, blocking collectives: none -> 40.7 us  [local(): plane_of = lax.all_to_all(share, ('gy', 'gz'), 0, 0)]
    reshape x7 -> x0, local copies, waits for them, and re-layouts: 22.1 us -> none  [the longest x3 21.4 us: coarsen(): source.reshape(depth // 2, 2, rows // 2, 2, cols // 2, 2)]
    reduce_sum x16 -> x0, other arithmetic: 20 us -> none  [the longest x4 8.32 us: coarsen(): source.reshape(depth // 2, 2, rows // 2, 2, cols // 2, 2)]
  transfers between devices with their start and end apart: 98 -> 13, of which waited for: 38 -> 9; matrix products, arithmetic and copies ran while one was open for 5% -> 1% of each run, Pallas kernels for 0% -> 0%
where the time goes in v1:
time: 178 us; the launch traced here: 177 us
  Pallas kernels  53.4 us (30%)
  blocking collectives  40.7 us (23%)
  starting transfers between devices  36.9 us (21%)
  waiting for transfers between devices  29.2 us (16%)
  local copies, waits for them, and re-layouts  12.7 us (7%)
  other arithmetic  3.05 us (2%)
    pallas_call x4, Pallas kernels, run(): pl.pallas_call(kernel, out_shape=[jax.ShapeDtypeStruct(shape, F32) for sh...  53.4 us
    all_to_all x1, blocking collectives, local(): plane_of = lax.all_to_all(share, ('gy', 'gz'), 0, 0)  40.7 us
    ppermute x6, waiting for transfers between devices, both_ways(): lax.ppermute(to_low, axis, down(axis))  21.3 us
    ppermute x6, starting transfers between devices, both_ways(): lax.ppermute(to_high, axis, up(axis))  17.3 us
    ppermute x6, starting transfers between devices, both_ways(): lax.ppermute(to_low, axis, down(axis))  15.9 us
    unnamed x28, local copies, waits for them, and re-layouts  10.3 us
    ppermute x6, waiting for transfers between devices, both_ways(): lax.ppermute(to_high, axis, up(axis))  7.89 us
    all_to_all x1, starting transfers between devices, local(): lax.all_to_all(jnp.broadcast_to(plane_of[None], (4, 128, 8, 128)), 'gx',...  3.72 us
  transfers between devices with their start and end apart: 13, of which 9 were waited for; matrix products, arithmetic and copies ran while one was open for 1% of the time, Pallas kernels for 0%

profile of v1, /device:TPU:1, one launch (start us, length us, event | category | flops | bytes accessed | tf_op | source)
XLA Modules:
  0.0 176.7 jit_solution(18151064782866955623)
XLA Ops:
  0.6 1.1 pad_maximum_fusion.mid
  1.7 8.8 %collective-permute-start.1 = (f32[3,8,32,128]{3,2,1,0:T(8,128)S(1)}, f32[3,8,32,128]{3,2,1,0:T(8,128)S(1)}, u32[]{:S(2)}, u32[]{:S(2)}) collective-permute-start(f32[3,8,32,128]{3,2,1,0:T(8,128)S(1)} %pad_maximum_fusion.mid), channel_id=1, source_target_pairs={{1,0},{2,1},{3,2},{4,3},{5,4},{6,5},{7,6},{8,7},{9,8},{10,9},{11,1... | collective-permute-start | bytes 1179656 | tf_op jit(solution)/shard_map/ppermute | solution.py:452
  10.5 1.9 %collective-permute-start = (f32[3,8,32,128]{3,2,1,0:T(8,128)S(1)}, f32[3,8,32,128]{3,2,1,0:T(8,128)S(1)}, u32[]{:S(2)}, u32[]{:S(2)}) collective-permute-start(f32[3,8,32,128]{3,2,1,0:T(8,128)S(1)} %pad_maximum_fusion.mid), channel_id=1, source_target_pairs={{0,1},{1,2},{2,3},{3,4},{4,5},{5,6},{6,7},{7,8},{8,9},{9,10},{10,1... | collective-permute-start | bytes 1179656 | tf_op jit(solution)/shard_map/ppermute | solution.py:452
  12.4 0.0 collective-permute-done.1.high
  12.4 4.7 %collective-permute-done.low = f32[3,8,32,128]{3,2,1,0:T(8,128)S(1)} collective-permute-done((f32[3,8,32,128]{3,2,1,0:T(8,128)S(1)}, f32[3,8,32,128]{3,2,1,0:T(8,128)S(1)}, u32[]{:S(2)}, u32[]{:S(2)}) %collective-permute-start) | collective-permute-done | bytes 393248 | tf_op jit(solution)/shard_map/ppermute | solution.py:452
  17.1 0.9 pad_maximum_fusion.1
  18.0 1.3 collective-permute-start.3
  19.3 4.0 %collective-permute-start.2 = (f32[3,24,8,128]{3,2,1,0:T(8,128)S(1)}, f32[3,24,8,128]{3,2,1,0:T(8,128)S(1)}, u32[]{:S(2)}, u32[]{:S(2)}) collective-permute-start(f32[3,24,8,128]{3,2,1,0:T(8,128)S(1)} %get-tuple-element.29), channel_id=1, source_target_pairs={{0,16},{16,32},{32,48},{48,64},{64,80},{80,96},{96,112},{1,17},{17... | collective-permute-start | bytes 884744 | tf_op jit(solution)/shard_map/ppermute | solution.py:452
  23.3 2.9 %collective-permute-done.3.yhigh = f32[3,24,8,128]{3,2,1,0:T(8,128)S(1)} collective-permute-done((f32[3,24,8,128]{3,2,1,0:T(8,128)S(1)}, f32[3,24,8,128]{3,2,1,0:T(8,128)S(1)}, u32[]{:S(2)}, u32[]{:S(2)}) %collective-permute-start.3) | collective-permute-done | bytes 294944 | tf_op jit(solution)/shard_map/ppermute | solution.py:452
  26.2 1.8 collective-permute-done.2.ylow
  28.0 1.6 shard_map.50
  29.6 1.3 collective-permute-start.4
  30.9 1.3 collective-permute-start.5
  32.2 0.4 collective-permute-done.4.from_left
  32.6 3.8 %collective-permute-done.5.from_right = f32[27,8,128]{2,1,0:T(8,128)S(1)} collective-permute-done((f32[27,8,128]{2,1,0:T(8,128)S(1)}, f32[27,8,128]{2,1,0:T(8,128)S(1)}, u32[]{:S(2)}, u32[]{:S(2)}) %collective-permute-start.5) | collective-permute-done | bytes 110624 | tf_op jit(solution)/shard_map/ppermute | solution.py:452
  36.4 16.3 %shard_map.51 = (f32[128,8,128]{2,1,0:T(8,128)S(1)}, f32[12,24,128]{2,1,0:T(8,128)S(1)}, f32[12,24,128]{2,1,0:T(8,128)S(1)}, f32[12,24,128]{2,1,0:T(8,128)S(1)},...) custom-call(f32[72,6,8,128]{3,2,1,0:T(8,128)S(1)} %get-tuple-element, ...), custom_call_target="tpu_custom_call" | custom-call | tf_op jit(solution)/shard_map/pallas_call | solution.py:433
  52.7 1.0 copy-done
  53.7 1.0 copy-done.2
  54.8 1.0 copy-done.4
  55.8 1.0 copy-done.6
  56.8 1.0 copy-done.8
  57.9 40.7 %all_to_all.10 = f32[128,8,128]{2,1,0:T(8,128)S(1)} all-to-all(f32[128,8,128]{2,1,0:T(8,128)S(1)} %get-tuple-element.18), channel_id=1, replica_groups=mesh['gx'=4,'gy'=8,'gz'=16] {'gy','gz'}, dimensions={0} | all-to-all | bytes 1048576 | tf_op jit(solution)/shard_map/all_to_all | solution.py:473
  98.6 1.5 broadcast_in_dim.4
  100.1 3.7 %all-to-all-start.1 = ((f32[4,128,8,128]{3,2,1,0:T(8,128)}), f32[4,128,8,128]{3,2,1,0:T(8,128)S(1)}, u32[]{:S(2)}, u32[]{:S(2)}) async-start(f32[4,128,8,128]{3,2,1,0:T(8,128)} %broadcast_in_dim.4), calls=%async_computation.1 | async-start | bytes 4194304 | tf_op jit(solution)/shard_map/all_to_all | solution.py:474
  103.8 0.8 pad_maximum_fusion.8
  104.6 1.9 %collective-permute-start.7 = (f32[2,4,16,64]{3,2,1,0:T(8,128)S(1)}, f32[2,4,16,64]{3,2,1,0:T(8,128)S(1)}, u32[]{:S(2)}, u32[]{:S(2)}) collective-permute-start(f32[2,4,16,64]{3,2,1,0:T(8,128)S(1)} %pad_maximum_fusion.8), channel_id=1, source_target_pairs={{1,0},{2,1},{3,2},{4,3},{5,4},{6,5},{7,6},{8,7},{9,8},{10,9},{11,1... | collective-permute-start | bytes 98312 | tf_op jit(solution)/shard_map/ppermute | solution.py:452
  106.5 3.6 %collective-permute-start.6 = (f32[2,4,16,64]{3,2,1,0:T(8,128)S(1)}, f32[2,4,16,64]{3,2,1,0:T(8,128)S(1)}, u32[]{:S(2)}, u32[]{:S(2)}) collective-permute-start(f32[2,4,16,64]{3,2,1,0:T(8,128)S(1)} %pad_maximum_fusion.8), channel_id=1, source_target_pairs={{0,1},{1,2},{2,3},{3,4},{4,5},{5,6},{6,7},{7,8},{8,9},{9,10},{10,1... | collective-permute-start | bytes 98312 | tf_op jit(solution)/shard_map/ppermute | solution.py:452
  110.2 0.3 collective-permute-done.7
  110.5 1.0 collective-permute-done.6
  111.5 2.3 %collective-permute-start.8 = (f32[2,12,4,64]{3,2,1,0:T(4,128)S(1)}, f32[2,12,4,64]{3,2,1,0:T(4,128)S(1)}, u32[]{:S(2)}, u32[]{:S(2)}) collective-permute-start(f32[2,12,4,64]{3,2,1,0:T(4,128)S(1)} %get-tuple-element.34), channel_id=1, source_target_pairs={{0,16},{16,32},{32,48},{48,64},{64,80},{80,96},{96,112},{1,17},{17... | collective-permute-start | bytes 73736 | tf_op jit(solution)/shard_map/ppermute | solution.py:452
  113.8 1.3 collective-permute-start.9
  115.1 0.0 collective-permute-done.8
  115.1 3.8 %collective-permute-done.9 = f32[2,12,4,64]{3,2,1,0:T(4,128)S(1)} collective-permute-done((f32[2,12,4,64]{3,2,1,0:T(4,128)S(1)}, f32[2,12,4,64]{3,2,1,0:T(4,128)S(1)}, u32[]{:S(2)}, u32[]{:S(2)}) %collective-permute-start.9) | collective-permute-done | bytes 24608 | tf_op jit(solution)/shard_map/ppermute | solution.py:452
  118.9 0.1 pad_maximum_fusion.6
  119.0 0.1 fusion
  119.1 1.3 collective-permute-start.10
  120.4 4.1 %collective-permute-start.11 = (f32[2,12,24,4]{3,2,1,0:T(8,128)S(1)}, f32[2,12,24,4]{3,2,1,0:T(8,128)S(1)}, u32[]{:S(2)}, u32[]{:S(2)}) collective-permute-start(f32[2,12,24,4]{3,2,1,0:T(8,128)S(1)} %get-tuple-element.33), channel_id=1, source_target_pairs={{0,128},{128,256},{256,384},{1,129},{129,257},{257,385},{2,130},{1... | collective-permute-start | bytes 27656 | tf_op jit(solution)/shard_map/ppermute | solution.py:452
  124.6 0.1 pad.6.clone
  124.6 10.5 %collective-permute-done.10 = f32[2,12,24,4]{3,2,1,0:T(8,128)S(1)} collective-permute-done((f32[2,12,24,4]{3,2,1,0:T(8,128)S(1)}, f32[2,12,24,4]{3,2,1,0:T(8,128)S(1)}, u32[]{:S(2)}, u32[]{:S(2)}) %collective-permute-start.10) | collective-permute-done | bytes 9248 | tf_op jit(solution)/shard_map/ppermute | solution.py:452
  135.2 0.0 collective-permute-done.11
  135.2 0.2 pad_maximum_fusion.7
  135.4 0.7 slice_bitcast_fusion
  136.1 27.7 %shard_map.52.coarse = f32[8,24,128]{2,1,0:T(8,128)S(1)} custom-call(f32[4,128,8,128]{3,2,1,0:T(8,128)S(1)} %all-to-all-done.1.gathered), custom_call_target="tpu_custom_call" | custom-call | tf_op jit(solution)/shard_map/pallas_call | solution.py:433
  163.8 1.3 copy-done.3
  165.1 1.3 copy-done.5
  166.4 1.3 copy-done.7
  167.6 1.3 copy-done.9
  168.9 7.7 %shard_map.53 = (f32[8,32,128]{2,1,0:T(8,128)}, f32[8,32,128]{2,1,0:T(8,128)}) custom-call(f32[8,24,128]{2,1,0:T(8,128)S(1)} %shard_map.52.coarse, f32[12,24,128]{2,1,0:T(8,128)S(1)} %copy-done.10, f32[12,24,128]{2,1,0:T(8,128)S(1)} %get-tuple-element.30.mr, f32[12,24,128]{2,1,0:T(8,128)S(1)} %copy-done.13, f32[144,8,256]{2,1,0:T(8,128)S(1)} %get-tuple-element.22.iterate, ...), custom_call_target="tpu_custom_call" | custom-call | tf_op jit(solution)/shard_map/pallas_call | solution.py:433
  (22 shorter events, 0.1 us)
Async XLA Ops:
  1.7 10.7 %collective-permute-start.1 = (f32[3,8,32,128]{3,2,1,0:T(8,128)S(1)}, f32[3,8,32,128]{3,2,1,0:T(8,128)S(1)}, u32[]{:S(2)}, u32[]{:S(2)}) collective-permute-start(f32[3,8,32,128]{3,2,1,0:T(8,128)S(1)} %pad_maximum_fusion.mid), channel_id=1, source_target_pairs={{1,0},{2,1},{3,2},{4,3},{5,4},{6,5},{7,6},{8,7},{9,8},{10,9},{11,1... | collective-permute-start | bytes 1179656 | tf_op jit(solution)/shard_map/ppermute | solution.py:452
  10.5 6.6 %collective-permute-start = (f32[3,8,32,128]{3,2,1,0:T(8,128)S(1)}, f32[3,8,32,128]{3,2,1,0:T(8,128)S(1)}, u32[]{:S(2)}, u32[]{:S(2)}) collective-permute-start(f32[3,8,32,128]{3,2,1,0:T(8,128)S(1)} %pad_maximum_fusion.mid), channel_id=1, source_target_pairs={{0,1},{1,2},{2,3},{3,4},{4,5},{5,6},{6,7},{7,8},{8,9},{9,10},{10,1... | collective-permute-start | bytes 1179656 | tf_op jit(solution)/shard_map/ppermute | solution.py:452
  18.0 8.2 %collective-permute-start.3 = (f32[3,24,8,128]{3,2,1,0:T(8,128)S(1)}, f32[3,24,8,128]{3,2,1,0:T(8,128)S(1)}, u32[]{:S(2)}, u32[]{:S(2)}) collective-permute-start(f32[3,24,8,128]{3,2,1,0:T(8,128)S(1)} %get-tuple-element.28), channel_id=1, source_target_pairs={{16,0},{32,16},{48,32},{64,48},{80,64},{96,80},{112,96},{17,1},{33... | collective-permute-start | bytes 884744 | tf_op jit(solution)/shard_map/ppermute | solution.py:452
  19.3 8.7 %collective-permute-start.2 = (f32[3,24,8,128]{3,2,1,0:T(8,128)S(1)}, f32[3,24,8,128]{3,2,1,0:T(8,128)S(1)}, u32[]{:S(2)}, u32[]{:S(2)}) collective-permute-start(f32[3,24,8,128]{3,2,1,0:T(8,128)S(1)} %get-tuple-element.29), channel_id=1, source_target_pairs={{0,16},{16,32},{32,48},{48,64},{64,80},{80,96},{96,112},{1,17},{17... | collective-permute-start | bytes 884744 | tf_op jit(solution)/shard_map/ppermute | solution.py:452
  29.6 3.0 %collective-permute-start.4 = (f32[27,8,128]{2,1,0:T(8,128)S(1)}, f32[27,8,128]{2,1,0:T(8,128)S(1)}, u32[]{:S(2)}, u32[]{:S(2)}) collective-permute-start(f32[27,8,128]{2,1,0:T(8,128)S(1)} %get-tuple-element.16), channel_id=1, source_target_pairs={{0,128},{128,256},{256,384},{1,129},{129,257},{257,385},{2,130},{1... | collective-permute-start | bytes 331784 | tf_op jit(solution)/shard_map/ppermute | solution.py:452
  30.9 5.5 %collective-permute-start.5 = (f32[27,8,128]{2,1,0:T(8,128)S(1)}, f32[27,8,128]{2,1,0:T(8,128)S(1)}, u32[]{:S(2)}, u32[]{:S(2)}) collective-permute-start(f32[27,8,128]{2,1,0:T(8,128)S(1)} %get-tuple-element.17), channel_id=1, source_target_pairs={{128,0},{256,128},{384,256},{129,1},{257,129},{385,257},{130,2},{2... | collective-permute-start | bytes 331784 | tf_op jit(solution)/shard_map/ppermute | solution.py:452
  52.7 1.1 copy-start
  53.7 1.0 copy-start.2
  54.8 1.0 copy-start.4
  55.8 1.0 copy-start.6
  56.8 1.0 copy-start.8
  57.9 42.2 %copy-start.11 = (f32[12,24,128]{2,1,0:T(8,128)}, f32[12,24,128]{2,1,0:T(8,128)S(1)}, u32[]{:S(2)}) copy-start(f32[12,24,128]{2,1,0:T(8,128)S(1)} %get-tuple-element.20) | copy-start | bytes 442372
  57.9 42.2 %copy-start.12 = (f32[12,24,128]{2,1,0:T(8,128)}, f32[12,24,128]{2,1,0:T(8,128)S(1)}, u32[]{:S(2)}) copy-start(f32[12,24,128]{2,1,0:T(8,128)S(1)} %get-tuple-element.21.k1) | copy-start | bytes 442372
  100.1 36.0 %all-to-all-start.1 = ((f32[4,128,8,128]{3,2,1,0:T(8,128)}), f32[4,128,8,128]{3,2,1,0:T(8,128)S(1)}, u32[]{:S(2)}, u32[]{:S(2)}) async-start(f32[4,128,8,128]{3,2,1,0:T(8,128)} %broadcast_in_dim.4), calls=%async_computation.1 | async-start | bytes 4194304 | tf_op jit(solution)/shard_map/all_to_all | solution.py:474
  104.6 5.9 %collective-permute-start.7 = (f32[2,4,16,64]{3,2,1,0:T(8,128)S(1)}, f32[2,4,16,64]{3,2,1,0:T(8,128)S(1)}, u32[]{:S(2)}, u32[]{:S(2)}) collective-permute-start(f32[2,4,16,64]{3,2,1,0:T(8,128)S(1)} %pad_maximum_fusion.8), channel_id=1, source_target_pairs={{1,0},{2,1},{3,2},{4,3},{5,4},{6,5},{7,6},{8,7},{9,8},{10,9},{11,1... | collective-permute-start | bytes 98312 | tf_op jit(solution)/shard_map/ppermute | solution.py:452
  106.5 5.0 %collective-permute-start.6 = (f32[2,4,16,64]{3,2,1,0:T(8,128)S(1)}, f32[2,4,16,64]{3,2,1,0:T(8,128)S(1)}, u32[]{:S(2)}, u32[]{:S(2)}) collective-permute-start(f32[2,4,16,64]{3,2,1,0:T(8,128)S(1)} %pad_maximum_fusion.8), channel_id=1, source_target_pairs={{0,1},{1,2},{2,3},{3,4},{4,5},{5,6},{6,7},{7,8},{8,9},{9,10},{10,1... | collective-permute-start | bytes 98312 | tf_op jit(solution)/shard_map/ppermute | solution.py:452
  111.5 3.6 %collective-permute-start.8 = (f32[2,12,4,64]{3,2,1,0:T(4,128)S(1)}, f32[2,12,4,64]{3,2,1,0:T(4,128)S(1)}, u32[]{:S(2)}, u32[]{:S(2)}) collective-permute-start(f32[2,12,4,64]{3,2,1,0:T(4,128)S(1)} %get-tuple-element.34), channel_id=1, source_target_pairs={{0,16},{16,32},{32,48},{48,64},{64,80},{80,96},{96,112},{1,17},{17... | collective-permute-start | bytes 73736 | tf_op jit(solution)/shard_map/ppermute | solution.py:452
  113.8 5.1 %collective-permute-start.9 = (f32[2,12,4,64]{3,2,1,0:T(4,128)S(1)}, f32[2,12,4,64]{3,2,1,0:T(4,128)S(1)}, u32[]{:S(2)}, u32[]{:S(2)}) collective-permute-start(f32[2,12,4,64]{3,2,1,0:T(4,128)S(1)} %get-tuple-element.35), channel_id=1, source_target_pairs={{16,0},{32,16},{48,32},{64,48},{80,64},{96,80},{112,96},{17,1},{33... | collective-permute-start | bytes 73736 | tf_op jit(solution)/shard_map/ppermute | solution.py:452
  119.1 16.0 %collective-permute-start.10 = (f32[2,12,24,4]{3,2,1,0:T(8,128)S(1)}, f32[2,12,24,4]{3,2,1,0:T(8,128)S(1)}, u32[]{:S(2)}, u32[]{:S(2)}) collective-permute-start(f32[2,12,24,4]{3,2,1,0:T(8,128)S(1)} %get-tuple-element.32), channel_id=1, source_target_pairs={{128,0},{256,128},{384,256},{129,1},{257,129},{385,257},{130,2},{2... | collective-permute-start | bytes 27656 | tf_op jit(solution)/shard_map/ppermute | solution.py:452
  120.4 14.7 %collective-permute-start.11 = (f32[2,12,24,4]{3,2,1,0:T(8,128)S(1)}, f32[2,12,24,4]{3,2,1,0:T(8,128)S(1)}, u32[]{:S(2)}, u32[]{:S(2)}) collective-permute-start(f32[2,12,24,4]{3,2,1,0:T(8,128)S(1)} %get-tuple-element.33), channel_id=1, source_target_pairs={{0,128},{128,256},{256,384},{1,129},{129,257},{257,385},{2,130},{1... | collective-permute-start | bytes 27656 | tf_op jit(solution)/shard_map/ppermute | solution.py:452
  136.1 27.7 %copy-start.1 = (f32[144,8,256]{2,1,0:T(8,128)S(1)}, f32[144,8,256]{2,1,0:T(8,128)}, u32[]{:S(2)}) copy-start(f32[144,8,256]{2,1,0:T(8,128)} %copy-done) | copy-start | bytes 3538948
  136.1 27.7 %copy-start.10 = (f32[12,24,128]{2,1,0:T(8,128)S(1)}, f32[12,24,128]{2,1,0:T(8,128)}, u32[]{:S(2)}) copy-start(f32[12,24,128]{2,1,0:T(8,128)} %get-tuple-element.31.um) | copy-start | bytes 442372
  136.1 27.8 %copy-start.13 = (f32[12,24,128]{2,1,0:T(8,128)S(1)}, f32[12,24,128]{2,1,0:T(8,128)}, u32[]{:S(2)}) copy-start(f32[12,24,128]{2,1,0:T(8,128)} %copy-done.12) | copy-start | bytes 442372
  163.8 1.3 copy-start.3
  165.1 1.3 copy-start.5
  166.4 1.3 copy-start.7
  167.6 1.3 copy-start.9

commit v2 on v1

--- a/solution.py
+++ b/solution.py
@@ -19,7 +19,20 @@
 F32 = jnp.float32
 BF16 = jnp.bfloat16
 VMEM = pl.BlockSpec(memory_space=pltpu.VMEM)
-LIMIT = 40 * 1024 * 1024
+LIMIT = 20 * 1024 * 1024
+
+
+def loop(first, end, body, carry, unroll=8):
+    count = end - first
+    while count % unroll:
+        unroll -= 1
+
+    def several(i, carry):
+        for k in range(unroll):
+            carry = body(first + i * unroll + k, carry)
+        return carry
+
+    return lax.fori_loop(0, count // unroll, several, carry)
 
 
 def shift(value, by, axis):
@@ -85,7 +98,7 @@
             to_right[3 * i + packed] = right
         return carry
 
-    lax.fori_loop(0, 9, group, 0)
+    loop(0, 9, group, 0)
 
 
 def plane(ref, z):
@@ -113,7 +126,7 @@
         step(z, v, inner_flux(v, plane(wx, z), plane(wy, z)) + (above - below))
         return (after, above)
 
-    lax.fori_loop(first, last + 1, body, carry)
+    loop(first, last + 1, body, carry)
 
 
 def zpair(low_face):
@@ -143,7 +156,7 @@
 
 def down_kernel(
     window, from_left, from_right,
-    share, um_out, mr_out, k1_out, iterate, right, wx, wy, wz, inverse,
+    share, pair_out, k1_out, iterate, right, wx, wy, wz, inverse,
     kappa, guess, rest, update, second, sums_a, sums_b, line,
 ):
     lane = iota((8, 128), 1)
@@ -165,7 +178,7 @@
         unpack(i, kappa, 2)
         return carry
 
-    lax.fori_loop(0, 3, unpack_all, 0)
+    loop(0, 3, unpack_all, 0)
 
     def weights(z, carry):
         half, below = carry
@@ -184,7 +197,7 @@
     half0 = 0.5 * plane(kappa, 0)
     half1 = 0.5 * plane(kappa, 1)
     put(wz, 0, half0 + half1)
-    lax.fori_loop(1, 23, weights, (half1, half0 + half1))
+    loop(1, 23, weights, (half1, half0 + half1))
 
     def first(z, v, minus):
         r = plane(right, z) + minus
@@ -215,7 +228,7 @@
             sums_b[rows, :] = pair[:, 128:]
             return carry
 
-        lax.fori_loop(0, count, body, 0)
+        loop(0, count, body, 0)
 
     add_pairs(rest, 4, 8, 0)
     add_pairs(kappa, 0, 12, 8)
@@ -235,8 +248,10 @@
     r = rhs + middle_minus(d, weights_one)
     d2 = KEEP * d + GAIN * (r * inverse_one)
     r = r + middle_minus(d2, weights_one)
-    um_out[...] = d + d2
-    mr_out[...] = rhs
+    wide = iota((12, 24, 128), 2)
+    um = d + d2
+    pair = jnp.where(wide < 64, um, shift(rhs, 64, 2))
+    pair_out[...] = pair
     k1_out[...] = kappa_one
 
     cell = iota((128, 128), 0)
@@ -248,7 +263,76 @@
     line[...] = total
     cells = line[pl.ds(4, 8, stride=2), :] + line[pl.ds(5, 8, stride=2), :]
     cells = pltpu.roll(cells, 32 * lax.axis_index("gx"), 1)
-    share[...] = jnp.broadcast_to(cells[None], (128, 8, 128))
+    for slot in range(16):
+        share[slot, 4] = cells
+    gz = lax.axis_index("gz")
+    for step, planes in ((1, (um[4], um[5], um[6], rhs[5])), (-1, (um[5], um[6], um[7], rhs[6]))):
+        for k, value in enumerate(planes):
+            rows = shift(value, -4, 0)
+            share[(gz + step) & 15, k] = jnp.where(lane < 64, rows[:8], shift(rows[8:16], 64, 1))
+
+
+def turn_kernel(gathered, pair, share, pair_out):
+    lane = iota((8, 128), 1)
+    row = iota((8, 128), 0)
+    gy = lax.axis_index("gy")
+    gz = lax.axis_index("gz")
+    wide = iota((24, 128), 1)
+
+    def spread(tile):
+        value = jnp.concatenate([tile, shift(tile, 64, 1), jnp.zeros((8, 128), F32)], 0)
+        return shift(value, 4, 0)
+
+    planes = [pair[z] for z in range(12)]
+    for step, first, where_rhs in ((-1, 0, 1), (1, 9, 10)):
+        for k in range(3):
+            planes[first + k] = jnp.where(wide < 64, spread(gathered[(gz + step) & 15, k]), planes[first + k])
+        value = shift(spread(gathered[(gz + step) & 15, 3]), 64, 1)
+        planes[where_rhs] = jnp.where(wide < 64, planes[where_rhs], value)
+    for z in range(12):
+        pair_out[z] = planes[z]
+    for slot in range(8):
+        for g in range(16):
+            share[slot, 6 + g] = gathered[g, 4]
+    for k in range(6):
+        one, two = planes[2 * k], planes[2 * k + 1]
+        share[(gy - 1) & 7, k] = jnp.where(row < 4, shift(one[0:8], 4, 0), two[0:8])
+        share[(gy + 1) & 7, k] = jnp.where(row < 4, one[16:24], shift(two[16:24], 4, 0))
+
+
+def cross_kernel(gathered, pair, share, pair_out):
+    lane = iota((8, 128), 1)
+    row = iota((8, 128), 0)
+    slot_of = lax.shift_right_logical(lane, 3)
+    gx = lax.axis_index("gx")
+    gy = lax.axis_index("gy")
+    tiles = []
+    for k in range(6):
+        low = gathered[(gy - 1) & 7, k]
+        high = gathered[(gy + 1) & 7, k]
+        for odd in range(2):
+            value = pair[2 * k + odd]
+            above = low if odd == 0 else shift(low, 4, 0)
+            below = shift(high, 4, 0) if odd == 0 else high
+            tiles.append(jnp.where(row < 4, above, value[0:8]))
+            tiles.append(value[8:16])
+            tiles.append(jnp.where(row < 4, value[16:24], below))
+    for z in range(12):
+        for t in range(3):
+            pair_out[z, 8 * t : 8 * t + 8] = tiles[3 * z + t]
+    for packed in range(3):
+        left = jnp.zeros((8, 128), F32)
+        right = jnp.zeros((8, 128), F32)
+        for s, tile in enumerate(tiles[16 * packed : 16 * packed + 16]):
+            here = slot_of == s
+            first = (lane & 7) < 4
+            left = jnp.where(here, jnp.where(first, shift(tile, 8 * s, 1), shift(tile, 8 * s - 60, 1)), left)
+            right = jnp.where(here, jnp.where(first, shift(tile, 8 * s - 60, 1), shift(tile, 8 * s - 120, 1)), right)
+        share[(gx - 1) & 3, packed] = left
+        share[(gx + 1) & 3, packed] = right
+    for slot in range(4):
+        for g in range(8):
+            share[slot, 3 + 16 * g : 19 + 16 * g] = gathered[g, 6:22]
 
 
 def cplane(ref, z):
@@ -259,7 +343,7 @@
     ref[pl.ds(8 * z, 8)] = value.reshape(8, 8, 128)
 
 
-def coarse_kernel(gathered, out, kappa, wx, wy, wz, diag, rest, direction, image, answer):
+def conjugate(gathered, kappa, wx, wy, wz, diag, rest, direction, image, answer):
     lane = iota((8, 128), 1)
     group = lax.shift_right_logical(lane, 5)
     nothing = jnp.zeros((64, 128), F32)
@@ -271,7 +355,7 @@
 
     def assemble(gz, carry):
         for gy in range(8):
-            pieces = [gathered[gx, gy * 16 + gz] for gx in range(4)]
+            pieces = [gathered[gx, 3 + gy * 16 + gz] for gx in range(4)]
             for q in range(4):
                 merged = pieces[0]
                 for gx in range(1, 4):
@@ -284,7 +368,7 @@
                     kappa[(2 * gz + q - 1) * 8 + gy] = merged
         return carry
 
-    lax.fori_loop(0, 16, assemble, 0)
+    loop(0, 16, assemble, 0)
     inner_x = iota((64, 128), 1) < 127
     inner_y = iota((64, 128), 0) < 63
     first_x = iota((64, 128), 1) > 0
@@ -310,7 +394,7 @@
     def whole(total):
         return jnp.sum(jnp.sum(total, axis=0, keepdims=True), axis=1, keepdims=True)
 
-    norm = whole(lax.fori_loop(0, 32, weights, zero))
+    norm = whole(loop(0, 32, weights, zero))
 
     def apply(z, total):
         v = cplane(direction, z + 1)
@@ -328,7 +412,7 @@
         answer[at] = answer[at] + (alpha * cplane(direction, z + 1)).reshape(8, 8, 128)
 
     for repeat in range(ITERS):
-        alpha = norm / whole(lax.fori_loop(0, 32, apply, zero))
+        alpha = norm / whole(loop(0, 32, apply, zero))
         if repeat + 1 < ITERS:
 
             def step(z, total):
@@ -337,14 +421,14 @@
                 cput(rest, z, r)
                 return total + (r * r).reshape(8, 8, 128).sum(0)
 
-            norm_next = whole(lax.fori_loop(0, 32, step, zero))
+            norm_next = whole(loop(0, 32, step, zero))
             beta = norm_next / norm
 
             def turn(z, carry):
                 cput(direction, z + 1, cplane(rest, z) + beta * cplane(direction, z + 1))
                 return carry
 
-            lax.fori_loop(0, 32, turn, 0)
+            loop(0, 32, turn, 0)
             norm = norm_next
         else:
 
@@ -352,7 +436,7 @@
                 add_answer(z, alpha)
                 return carry
 
-            lax.fori_loop(0, 32, finish, 0)
+            loop(0, 32, finish, 0)
 
     gx = lax.axis_index("gx")
     gy = lax.axis_index("gy")
@@ -360,17 +444,36 @@
     wide = iota((24, 128), 1)
     position = jnp.where(wide < 64, wide, wide - 128) + 32 * gx
     known = (position >= 0) & (position < 128)
+    planes = []
     for z in range(8):
         block = answer[pl.ds((2 * gz + z) * 10 + gy, 3)].reshape(24, 128)
-        out[z] = jnp.where(known, pltpu.roll(block, (128 - 32 * gx) & 127, 1), 0.0)
+        planes.append(jnp.where(known, pltpu.roll(block, (128 - 32 * gx) & 127, 1), 0.0))
+    return jnp.stack(planes)
+
+
+def middle_fields(gathered, pair):
+    lane = iota((8, 128), 1)
+    gx = lax.axis_index("gx")
+    both = [[], []]
+    for v in range(36):
+        packed, s = v // 16, v % 16
+        low = gathered[(gx - 1) & 3, packed]
+        high = gathered[(gx + 1) & 3, packed]
+        tile = pair[v // 3, 8 * (v % 3) : 8 * (v % 3) + 8]
+        for k in range(2):
+            own = shift(tile, 64 * k, 1) if k else tile
+            edge = jnp.where(lane < 68, shift(high, 64 - 8 * s - 4 * k, 1), shift(low, 124 - 8 * s - 4 * k, 1))
+            both[k].append(jnp.where(lane < 64, own, edge))
+    return [jnp.stack(tiles).reshape(12, 24, 128) for tiles in both]
 
 
 def up_kernel(
-    coarse, um, mr, k1, iterate, right, wx, wy, wz, inverse,
+    gathered, pair, k1, iterate, right, wx, wy, wz, inverse,
     solution_out, residual_out,
-    line, fine_a, fine_b, current, rest, update, second,
+    line, fine_a, fine_b, current, rest, update, second, *grids,
 ):
-    c = coarse[...]
+    c = conjugate(gathered, *grids)
+    um, mr = middle_fields(gathered, pair)
     even = 0.75 * c[1:7] + 0.25 * c[0:6]
     odd = 0.75 * c[1:7] + 0.25 * c[2:8]
     c = jnp.stack([even, odd], 1).reshape(12, 24, 128)
@@ -382,8 +485,8 @@
     kappa_one = k1[...]
     weights = middle_weights(kappa_one)
     inverse_one = weights[3]
-    u = jnp.where(kappa_one > 0.0, um[...] + correction, 0.0)
-    r = mr[...] + middle_minus(u, weights)
+    u = jnp.where(kappa_one > 0.0, um + correction, 0.0)
+    r = mr + middle_minus(u, weights)
     d = FIRST * (r * inverse_one)
     u = u + d
     r = r + middle_minus(d, weights)
@@ -404,7 +507,7 @@
         put(current, z, jnp.where(plane(inverse, z) > 0.0, plane(iterate, z) + fine, 0.0))
         return carry
 
-    lax.fori_loop(4, 20, begin, 0)
+    loop(4, 20, begin, 0)
 
     def first(z, v, minus):
         r = plane(right, z) + minus
@@ -440,6 +543,21 @@
     )(*args)
 
 
+FINE = (144, 8, 256)
+MIDDLE = (12, 24, 128)
+COARSE = (256, 8, 128)
+PADDED = (272, 8, 128)
+XPACK = ([(72, 6, 8, 128), (27, 8, 128), (27, 8, 128)], [])
+DOWN = ([(16, 5, 8, 128), MIDDLE, MIDDLE] + [FINE] * 6, [FINE] * 5 + [(960, 128)] * 2 + [(24, 128)])
+TURN = ([(8, 22, 8, 128), MIDDLE], [])
+CROSS = ([(4, 131, 8, 128), MIDDLE], [])
+UP = (
+    [(8, 32, 128)] * 2,
+    [(576, 128)] + [(768, 128)] * 2 + [FINE] * 4
+    + [PADDED] + [COARSE] * 2 + [PADDED] + [COARSE] * 2 + [PADDED, COARSE, (380, 8, 128)],
+)
+
+
 def up(axis):
     return [(i, i + 1) for i in range(lax.axis_size(axis) - 1)]
 
@@ -458,44 +576,14 @@
     column = jnp.concatenate([low, mine, high], 1)
     ylow, yhigh = both_ways(column[:, :, :8], column[:, :, 24:], "gy")
     window, to_left, to_right = run(
-        xpack_kernel, [(72, 6, 8, 128), (27, 8, 128), (27, 8, 128)], [], mine, low, high, ylow, yhigh
+        xpack_kernel, *XPACK, mine, low, high, ylow, yhigh
     )
     from_left, from_right = both_ways(to_left, to_right, "gx")
 
-    fine = (144, 8, 256)
-    middle = (12, 24, 128)
-    share, um, mr, k1, *arrays = run(
-        down_kernel,
-        [(128, 8, 128), middle, middle, middle] + [fine] * 6,
-        [fine] * 5 + [(960, 128)] * 2 + [(24, 128)],
-        window, from_left, from_right,
-    )
-    plane_of = lax.all_to_all(share, ("gy", "gz"), 0, 0)
-    whole = lax.all_to_all(jnp.broadcast_to(plane_of[None], (4, 128, 8, 128)), "gx", 0, 0)
-
-    pair = jnp.stack([um, mr])[:, 4:8, 4:20, :64]
-    low, high = both_ways(pair, pair, "gz")
-    pair = jnp.concatenate([low, pair, high], 1)
-    low, high = both_ways(pair[:, :, :4], pair[:, :, 12:], "gy")
-    pair = jnp.concatenate([low, pair, high], 2)
-    low, high = both_ways(pair[..., :4], pair[..., 60:], "gx")
-    pair = jnp.concatenate([pair, high, jnp.zeros((2, 12, 24, 56), F32), low], 3)
-
-    coarse_grid = (256, 8, 128)
-    padded = (272, 8, 128)
-    coarse = run(
-        coarse_kernel,
-        [(8, 24, 128)],
-        [padded] + [coarse_grid] * 2 + [padded] + [coarse_grid] * 2 + [padded, coarse_grid, (380, 8, 128)],
-        whole,
-    )[0]
-    solution, residual = run(
-        up_kernel,
-        [(8, 32, 128)] * 2,
-        [(576, 128)] + [(768, 128)] * 2 + [fine] * 4,
-        coarse, pair[0], pair[1], k1, *arrays,
-    )
-    return solution, residual
+    share, pair, k1, *arrays = run(down_kernel, *DOWN, window, from_left, from_right)
+    share, pair = run(turn_kernel, *TURN, lax.all_to_all(share, "gz", 0, 0), pair)
+    share, pair = run(cross_kernel, *CROSS, lax.all_to_all(share, "gy", 0, 0), pair)
+    return run(up_kernel, *UP, lax.all_to_all(share, "gx", 0, 0), pair, k1, *arrays)
 
 
 def solution(mesh):

time: 178 us -> 145 us (0.81)
  blocking collectives: 40.7 us -> 85.2 us
  Pallas kernels: 53.4 us -> 24.2 us
  starting transfers between devices: 36.9 us -> 18.6 us
  waiting for transfers between devices: 29.2 us -> 13.5 us
  local copies, waits for them, and re-layouts: 12.7 us -> 0 us
    all_to_all x1 -> x3, blocking collectives: 40.7 us -> 85.2 us  [the longest x1 33.4 us: local(): lax.all_to_all(share, 'gy', 0, 0)]
    pallas_call x4 -> x5, Pallas kernels: 53.4 us -> 24.2 us  [run(): pl.pallas_call(kernel, out_shape=[jax.ShapeDtypeStruct(shape, F32) for sh...]
    ppermute x6 -> x3, waiting for transfers between devices: 21.3 us -> 6.66 us  [both_ways(): lax.ppermute(to_low, axis, down(axis))]
    unnamed x28 -> x0, local copies, waits for them, and re-layouts: 10.3 us -> none
    ppermute x6 -> x3, starting transfers between devices: 17.3 us -> 7.22 us  [both_ways(): lax.ppermute(to_high, axis, up(axis))]
    ppermute x6 -> x3, starting transfers between devices: 15.9 us -> 11.4 us  [both_ways(): lax.ppermute(to_low, axis, down(axis))]
    all_to_all x1 -> x0, starting transfers between devices: 3.72 us -> none  [local(): lax.all_to_all(jnp.broadcast_to(plane_of[None], (4, 128, 8, 128)), 'gx',...]
    ppermute x6 -> x3, waiting for transfers between devices: 7.89 us -> 6.88 us  [both_ways(): lax.ppermute(to_high, axis, up(axis))]
  transfers between devices with their start and end apart: 13 -> 6, of which waited for: 9 -> 5; matrix products, arithmetic and copies ran while one was open for 1% -> 0% of each run, Pallas kernels for 0% -> 0%
where the time goes in v2:
time: 145 us; the launch traced here: 144 us
  blocking collectives  85.2 us (59%)
  Pallas kernels  24.2 us (17%)
  starting transfers between devices  18.6 us (13%)
  waiting for transfers between devices  13.5 us (9%)
  other arithmetic  1.94 us (1%)
    all_to_all x1, blocking collectives, local(): lax.all_to_all(share, 'gy', 0, 0)  33.4 us
    all_to_all x1, blocking collectives, local(): lax.all_to_all(share, 'gx', 0, 0)  29.8 us
    pallas_call x5, Pallas kernels, run(): pl.pallas_call(kernel, out_shape=[jax.ShapeDtypeStruct(shape, F32) for sh...  24.2 us
    all_to_all x1, blocking collectives, local(): lax.all_to_all(share, 'gz', 0, 0)  22.1 us
    ppermute x3, starting transfers between devices, both_ways(): lax.ppermute(to_low, axis, down(axis))  11.4 us
    ppermute x3, starting transfers between devices, both_ways(): lax.ppermute(to_high, axis, up(axis))  7.22 us
    ppermute x3, waiting for transfers between devices, both_ways(): lax.ppermute(to_high, axis, up(axis))  6.88 us
    ppermute x3, waiting for transfers between devices, both_ways(): lax.ppermute(to_low, axis, down(axis))  6.66 us
  transfers between devices with their start and end apart: 6, of which 5 were waited for; matrix products, arithmetic and copies ran while one was open for 0% of the time, Pallas kernels for 0%

profile of v2, /device:TPU:1, one launch (start us, length us, event | category | flops | bytes accessed | tf_op | source)
XLA Modules:
  0.0 144.2 jit_solution(10722549254142601106)
XLA Ops:
  0.6 1.1 pad_maximum_fusion.mid
  1.7 8.8 %collective-permute-start.1 = (f32[3,8,32,128]{3,2,1,0:T(8,128)S(1)}, f32[3,8,32,128]{3,2,1,0:T(8,128)S(1)}, u32[]{:S(2)}, u32[]{:S(2)}) collective-permute-start(f32[3,8,32,128]{3,2,1,0:T(8,128)S(1)} %pad_maximum_fusion.mid), channel_id=1, source_target_pairs={{1,0},{2,1},{3,2},{4,3},{5,4},{6,5},{7,6},{8,7},{9,8},{10,9},{11,1... | collective-permute-start | bytes 1179656 | tf_op jit(solution)/shard_map/ppermute | solution.py:570
  10.5 1.9 %collective-permute-start = (f32[3,8,32,128]{3,2,1,0:T(8,128)S(1)}, f32[3,8,32,128]{3,2,1,0:T(8,128)S(1)}, u32[]{:S(2)}, u32[]{:S(2)}) collective-permute-start(f32[3,8,32,128]{3,2,1,0:T(8,128)S(1)} %pad_maximum_fusion.mid), channel_id=1, source_target_pairs={{0,1},{1,2},{2,3},{3,4},{4,5},{5,6},{6,7},{7,8},{8,9},{9,10},{10,1... | collective-permute-start | bytes 1179656 | tf_op jit(solution)/shard_map/ppermute | solution.py:570
  12.4 0.0 collective-permute-done.1.high
  12.4 4.7 %collective-permute-done.low = f32[3,8,32,128]{3,2,1,0:T(8,128)S(1)} collective-permute-done((f32[3,8,32,128]{3,2,1,0:T(8,128)S(1)}, f32[3,8,32,128]{3,2,1,0:T(8,128)S(1)}, u32[]{:S(2)}, u32[]{:S(2)}) %collective-permute-start) | collective-permute-done | bytes 393248 | tf_op jit(solution)/shard_map/ppermute | solution.py:570
  17.1 0.9 pad_maximum_fusion.1
  18.0 1.3 collective-permute-start.3
  19.3 4.0 %collective-permute-start.2 = (f32[3,24,8,128]{3,2,1,0:T(8,128)S(1)}, f32[3,24,8,128]{3,2,1,0:T(8,128)S(1)}, u32[]{:S(2)}, u32[]{:S(2)}) collective-permute-start(f32[3,24,8,128]{3,2,1,0:T(8,128)S(1)} %get-tuple-element.35), channel_id=1, source_target_pairs={{0,16},{16,32},{32,48},{48,64},{64,80},{80,96},{96,112},{1,17},{17... | collective-permute-start | bytes 884744 | tf_op jit(solution)/shard_map/ppermute | solution.py:570
  23.3 2.9 %collective-permute-done.3.yhigh = f32[3,24,8,128]{3,2,1,0:T(8,128)S(1)} collective-permute-done((f32[3,24,8,128]{3,2,1,0:T(8,128)S(1)}, f32[3,24,8,128]{3,2,1,0:T(8,128)S(1)}, u32[]{:S(2)}, u32[]{:S(2)}) %collective-permute-start.3) | collective-permute-done | bytes 294944 | tf_op jit(solution)/shard_map/ppermute | solution.py:570
  26.2 1.8 %collective-permute-done.2.ylow = f32[3,24,8,128]{3,2,1,0:T(8,128)S(1)} collective-permute-done((f32[3,24,8,128]{3,2,1,0:T(8,128)S(1)}, f32[3,24,8,128]{3,2,1,0:T(8,128)S(1)}, u32[]{:S(2)}, u32[]{:S(2)}) %collective-permute-start.2) | collective-permute-done | bytes 294944 | tf_op jit(solution)/shard_map/ppermute | solution.py:570
  28.0 1.2 shard_map.50
  29.1 1.3 collective-permute-start.4
  30.4 1.3 collective-permute-start.5
  31.7 0.4 collective-permute-done.4.from_left
  32.2 3.8 %collective-permute-done.5.from_right = f32[27,8,128]{2,1,0:T(8,128)S(1)} collective-permute-done((f32[27,8,128]{2,1,0:T(8,128)S(1)}, f32[27,8,128]{2,1,0:T(8,128)S(1)}, u32[]{:S(2)}, u32[]{:S(2)}) %collective-permute-start.5) | collective-permute-done | bytes 110624 | tf_op jit(solution)/shard_map/ppermute | solution.py:570
  35.9 8.6 %shard_map.51 = (f32[16,5,8,128]{3,2,1,0:T(8,128)S(1)}, f32[12,24,128]{2,1,0:T(8,128)S(1)}, f32[12,24,128]{2,1,0:T(8,128)S(1)}, f32[144,8,256]{2,1,0:T(8,128)S(1...) custom-call(f32[72,6,8,128]{3,2,1,0:T(8,128)S(1)} %get-tuple-element, ...), custom_call_target="tpu_custom_call" | custom-call | tf_op jit(solution)/shard_map/pallas_call | solution.py:536
  44.5 22.1 %all_to_all.15.gathered = f32[16,5,8,128]{3,2,1,0:T(8,128)S(1)} all-to-all(f32[16,5,8,128]{3,2,1,0:T(8,128)S(1)} %get-tuple-element.21), channel_id=1, replica_groups=mesh['gx'=4,'gy'=8,'gz'=16] {'gz'}, dimensions={0} | all-to-all | bytes 655360 | tf_op jit(solution)/shard_map/all_to_all | solution.py:584
  66.6 0.2 shard_map.52
  66.8 33.4 %all_to_all.16.gathered = f32[8,22,8,128]{3,2,1,0:T(8,128)S(1)} all-to-all(f32[8,22,8,128]{3,2,1,0:T(8,128)S(1)} %get-tuple-element.23), channel_id=1, replica_groups=mesh['gx'=4,'gy'=8,'gz'=16] {'gy'}, dimensions={0} | all-to-all | bytes 1441792 | tf_op jit(solution)/shard_map/all_to_all | solution.py:585
  100.1 0.2 shard_map.53
  100.4 29.8 %all_to_all.17.gathered = f32[4,131,8,128]{3,2,1,0:T(8,128)S(1)} all-to-all(f32[4,131,8,128]{3,2,1,0:T(8,128)S(1)} %get-tuple-element.25), channel_id=1, replica_groups=mesh['gx'=4,'gy'=8,'gz'=16] {'gx'}, dimensions={0} | all-to-all | bytes 4292608 | tf_op jit(solution)/shard_map/all_to_all | solution.py:586
  130.1 14.0 %shard_map.54 = (f32[8,32,128]{2,1,0:T(8,128)}, f32[8,32,128]{2,1,0:T(8,128)}) custom-call(f32[4,131,8,128]{3,2,1,0:T(8,128)S(1)} %all_to_all.17.gathered, f32[12,24,128]{2,1,0:T(8,128)S(1)} %get-tuple-element.26.pair, f32[12,24,128]{2,1,0:T(8,128)S(1)} %get-tuple-element.27.k1, f32[144,8,256]{2,1,0:T(8,128)S(1)} %get-tuple-element.28.iterate, ...), custom_call_target="tpu_custom_call" | custom-call | tf_op jit(solution)/shard_map/pallas_call | solution.py:536
Async XLA Ops:
  1.7 10.7 %collective-permute-start.1 = (f32[3,8,32,128]{3,2,1,0:T(8,128)S(1)}, f32[3,8,32,128]{3,2,1,0:T(8,128)S(1)}, u32[]{:S(2)}, u32[]{:S(2)}) collective-permute-start(f32[3,8,32,128]{3,2,1,0:T(8,128)S(1)} %pad_maximum_fusion.mid), channel_id=1, source_target_pairs={{1,0},{2,1},{3,2},{4,3},{5,4},{6,5},{7,6},{8,7},{9,8},{10,9},{11,1... | collective-permute-start | bytes 1179656 | tf_op jit(solution)/shard_map/ppermute | solution.py:570
  10.5 6.6 %collective-permute-start = (f32[3,8,32,128]{3,2,1,0:T(8,128)S(1)}, f32[3,8,32,128]{3,2,1,0:T(8,128)S(1)}, u32[]{:S(2)}, u32[]{:S(2)}) collective-permute-start(f32[3,8,32,128]{3,2,1,0:T(8,128)S(1)} %pad_maximum_fusion.mid), channel_id=1, source_target_pairs={{0,1},{1,2},{2,3},{3,4},{4,5},{5,6},{6,7},{7,8},{8,9},{9,10},{10,1... | collective-permute-start | bytes 1179656 | tf_op jit(solution)/shard_map/ppermute | solution.py:570
  18.0 8.2 %collective-permute-start.3 = (f32[3,24,8,128]{3,2,1,0:T(8,128)S(1)}, f32[3,24,8,128]{3,2,1,0:T(8,128)S(1)}, u32[]{:S(2)}, u32[]{:S(2)}) collective-permute-start(f32[3,24,8,128]{3,2,1,0:T(8,128)S(1)} %get-tuple-element.34), channel_id=1, source_target_pairs={{16,0},{32,16},{48,32},{64,48},{80,64},{96,80},{112,96},{17,1},{33... | collective-permute-start | bytes 884744 | tf_op jit(solution)/shard_map/ppermute | solution.py:570
  19.3 8.7 %collective-permute-start.2 = (f32[3,24,8,128]{3,2,1,0:T(8,128)S(1)}, f32[3,24,8,128]{3,2,1,0:T(8,128)S(1)}, u32[]{:S(2)}, u32[]{:S(2)}) collective-permute-start(f32[3,24,8,128]{3,2,1,0:T(8,128)S(1)} %get-tuple-element.35), channel_id=1, source_target_pairs={{0,16},{16,32},{32,48},{48,64},{64,80},{80,96},{96,112},{1,17},{17... | collective-permute-start | bytes 884744 | tf_op jit(solution)/shard_map/ppermute | solution.py:570
  29.1 3.0 %collective-permute-start.4 = (f32[27,8,128]{2,1,0:T(8,128)S(1)}, f32[27,8,128]{2,1,0:T(8,128)S(1)}, u32[]{:S(2)}, u32[]{:S(2)}) collective-permute-start(f32[27,8,128]{2,1,0:T(8,128)S(1)} %get-tuple-element.19), channel_id=1, source_target_pairs={{0,128},{128,256},{256,384},{1,129},{129,257},{257,385},{2,130},{1... | collective-permute-start | bytes 331784 | tf_op jit(solution)/shard_map/ppermute | solution.py:570
  30.4 5.5 %collective-permute-start.5 = (f32[27,8,128]{2,1,0:T(8,128)S(1)}, f32[27,8,128]{2,1,0:T(8,128)S(1)}, u32[]{:S(2)}, u32[]{:S(2)}) collective-permute-start(f32[27,8,128]{2,1,0:T(8,128)S(1)} %get-tuple-element.20), channel_id=1, source_target_pairs={{128,0},{256,128},{384,256},{129,1},{257,129},{385,257},{130,2},{2... | collective-permute-start | bytes 331784 | tf_op jit(solution)/shard_map/ppermute | solution.py:570

commit v3 on v2

--- a/solution.py
+++ b/solution.py
@@ -291,9 +291,10 @@
         planes[where_rhs] = jnp.where(wide < 64, planes[where_rhs], value)
     for z in range(12):
         pair_out[z] = planes[z]
-    for slot in range(8):
-        for g in range(16):
-            share[slot, 6 + g] = gathered[g, 4]
+    for g in range(8):
+        piece = gathered[2 * g + (gz & 1), 4]
+        for slot in range(8):
+            share[slot, 6 + g] = piece
     for k in range(6):
         one, two = planes[2 * k], planes[2 * k + 1]
         share[(gy - 1) & 7, k] = jnp.where(row < 4, shift(one[0:8], 4, 0), two[0:8])
@@ -332,7 +333,7 @@
         share[(gx + 1) & 3, packed] = right
     for slot in range(4):
         for g in range(8):
-            share[slot, 3 + 16 * g : 19 + 16 * g] = gathered[g, 6:22]
+            share[slot, 3 + 8 * g : 11 + 8 * g] = gathered[g, 6:14]
 
 
 def cplane(ref, z):
@@ -343,7 +344,7 @@
     ref[pl.ds(8 * z, 8)] = value.reshape(8, 8, 128)
 
 
-def conjugate(gathered, kappa, wx, wy, wz, diag, rest, direction, image, answer):
+def conjugate(gathered, other, kappa, wx, wy, wz, diag, rest, direction, image, answer):
     lane = iota((8, 128), 1)
     group = lax.shift_right_logical(lane, 5)
     nothing = jnp.zeros((64, 128), F32)
@@ -353,22 +354,25 @@
     cput(wz, 0, nothing)
     answer[...] = jnp.zeros_like(answer)
 
-    def assemble(gz, carry):
-        for gy in range(8):
-            pieces = [gathered[gx, 3 + gy * 16 + gz] for gx in range(4)]
-            for q in range(4):
-                merged = pieces[0]
-                for gx in range(1, 4):
-                    merged = jnp.where(group == (q + gx) % 4, pieces[gx], merged)
-                merged = shift(merged, -32 * q, 1)
-                if q < 2:
-                    rest[(2 * gz + q) * 8 + gy] = merged
-                    direction[(2 * gz + q + 1) * 8 + gy] = merged
-                else:
-                    kappa[(2 * gz + q - 1) * 8 + gy] = merged
-        return carry
-
-    loop(0, 16, assemble, 0)
+    for source, parity in ((gathered, lax.axis_index("gz") & 1), (other, 1 - (lax.axis_index("gz") & 1))):
+
+        def assemble(g, carry):
+            gz = 2 * g + parity
+            for gy in range(8):
+                pieces = [source[gx, 3 + gy * 8 + g] for gx in range(4)]
+                for q in range(4):
+                    merged = pieces[0]
+                    for gx in range(1, 4):
+                        merged = jnp.where(group == (q + gx) % 4, pieces[gx], merged)
+                    merged = shift(merged, -32 * q, 1)
+                    if q < 2:
+                        rest[(2 * gz + q) * 8 + gy] = merged
+                        direction[(2 * gz + q + 1) * 8 + gy] = merged
+                    else:
+                        kappa[(2 * gz + q - 1) * 8 + gy] = merged
+            return carry
+
+        loop(0, 8, assemble, 0, 2)
     inner_x = iota((64, 128), 1) < 127
     inner_y = iota((64, 128), 0) < 63
     first_x = iota((64, 128), 1) > 0
@@ -468,11 +472,11 @@
 
 
 def up_kernel(
-    gathered, pair, k1, iterate, right, wx, wy, wz, inverse,
+    gathered, other, pair, k1, iterate, right, wx, wy, wz, inverse,
     solution_out, residual_out,
     line, fine_a, fine_b, current, rest, update, second, *grids,
 ):
-    c = conjugate(gathered, *grids)
+    c = conjugate(gathered, other, *grids)
     um, mr = middle_fields(gathered, pair)
     even = 0.75 * c[1:7] + 0.25 * c[0:6]
     odd = 0.75 * c[1:7] + 0.25 * c[2:8]
@@ -549,8 +553,8 @@
 PADDED = (272, 8, 128)
 XPACK = ([(72, 6, 8, 128), (27, 8, 128), (27, 8, 128)], [])
 DOWN = ([(16, 5, 8, 128), MIDDLE, MIDDLE] + [FINE] * 6, [FINE] * 5 + [(960, 128)] * 2 + [(24, 128)])
-TURN = ([(8, 22, 8, 128), MIDDLE], [])
-CROSS = ([(4, 131, 8, 128), MIDDLE], [])
+TURN = ([(8, 14, 8, 128), MIDDLE], [])
+CROSS = ([(4, 67, 8, 128), MIDDLE], [])
 UP = (
     [(8, 32, 128)] * 2,
     [(576, 128)] + [(768, 128)] * 2 + [FINE] * 4
@@ -583,7 +587,9 @@
     share, pair, k1, *arrays = run(down_kernel, *DOWN, window, from_left, from_right)
     share, pair = run(turn_kernel, *TURN, lax.all_to_all(share, "gz", 0, 0), pair)
     share, pair = run(cross_kernel, *CROSS, lax.all_to_all(share, "gy", 0, 0), pair)
-    return run(up_kernel, *UP, lax.all_to_all(share, "gx", 0, 0), pair, k1, *arrays)
+    whole = lax.all_to_all(share, "gx", 0, 0)
+    other = lax.ppermute(whole, "gz", [(i, i ^ 1) for i in range(16)])
+    return run(up_kernel, *UP, whole, other, pair, k1, *arrays)
 
 
 def solution(mesh):

time: 145 us -> 134 us (0.924)
  blocking collectives: 85.2 us -> 68.4 us
  starting transfers between devices: 18.6 us -> 22 us
  waiting for transfers between devices: 13.5 us -> 15.9 us
    all_to_all x1, blocking collectives: 29.8 us -> 18.5 us  [local(): whole = lax.all_to_all(share, 'gx', 0, 0)]
    all_to_all x1, blocking collectives: 33.4 us -> 27.8 us  [local(): lax.all_to_all(share, 'gy', 0, 0)]
    ppermute x0 -> x1, starting transfers between devices: none -> 3.45 us  [local(): other = lax.ppermute(whole, 'gz', [(i, i ^ 1) for i in range(16)])]
    ppermute x0 -> x1, waiting for transfers between devices: none -> 2.33 us  [local(): other = lax.ppermute(whole, 'gz', [(i, i ^ 1) for i in range(16)])]
  transfers between devices with their start and end apart: 6 -> 7, of which waited for: 5 -> 6; matrix products, arithmetic and copies ran while one was open for 0% -> 0% of each run, Pallas kernels for 0% -> 0%
where the time goes in v3:
time: 134 us
  blocking collectives  68.4 us (51%)
  Pallas kernels  24.8 us (19%)
  starting transfers between devices  22 us (16%)
  waiting for transfers between devices  15.9 us (12%)
  other arithmetic  1.94 us (1%)
    all_to_all x1, blocking collectives, local(): lax.all_to_all(share, 'gy', 0, 0)  27.8 us
    pallas_call x5, Pallas kernels, run(): pl.pallas_call(kernel, out_shape=[jax.ShapeDtypeStruct(shape, F32) for sh...  24.8 us
    all_to_all x1, blocking collectives, local(): lax.all_to_all(share, 'gz', 0, 0)  22.1 us
    all_to_all x1, blocking collectives, local(): whole = lax.all_to_all(share, 'gx', 0, 0)  18.5 us
    ppermute x3, starting transfers between devices, both_ways(): lax.ppermute(to_low, axis, down(axis))  11.4 us
    ppermute x3, starting transfers between devices, both_ways(): lax.ppermute(to_high, axis, up(axis))  7.22 us
    ppermute x3, waiting for transfers between devices, both_ways(): lax.ppermute(to_high, axis, up(axis))  6.88 us
    ppermute x3, waiting for transfers between devices, both_ways(): lax.ppermute(to_low, axis, down(axis))  6.66 us
  transfers between devices with their start and end apart: 7, of which 6 were waited for; matrix products, arithmetic and copies ran while one was open for 0% of the time, Pallas kernels for 0%

profile of v3, /device:TPU:1, one launch (start us, length us, event | category | flops | bytes accessed | tf_op | source)
XLA Modules:
  0.0 133.7 jit_solution(8427509871745772230)
XLA Ops:
  0.6 1.1 pad_maximum_fusion.mid
  1.7 8.8 %collective-permute-start.1 = (f32[3,8,32,128]{3,2,1,0:T(8,128)S(1)}, f32[3,8,32,128]{3,2,1,0:T(8,128)S(1)}, u32[]{:S(2)}, u32[]{:S(2)}) collective-permute-start(f32[3,8,32,128]{3,2,1,0:T(8,128)S(1)} %pad_maximum_fusion.mid), channel_id=1, source_target_pairs={{1,0},{2,1},{3,2},{4,3},{5,4},{6,5},{7,6},{8,7},{9,8},{10,9},{11,1... | collective-permute-start | bytes 1179656 | tf_op jit(solution)/shard_map/ppermute | solution.py:574
  10.5 1.9 %collective-permute-start = (f32[3,8,32,128]{3,2,1,0:T(8,128)S(1)}, f32[3,8,32,128]{3,2,1,0:T(8,128)S(1)}, u32[]{:S(2)}, u32[]{:S(2)}) collective-permute-start(f32[3,8,32,128]{3,2,1,0:T(8,128)S(1)} %pad_maximum_fusion.mid), channel_id=1, source_target_pairs={{0,1},{1,2},{2,3},{3,4},{4,5},{5,6},{6,7},{7,8},{8,9},{9,10},{10,1... | collective-permute-start | bytes 1179656 | tf_op jit(solution)/shard_map/ppermute | solution.py:574
  12.4 0.0 collective-permute-done.1.high
  12.4 4.7 %collective-permute-done.low = f32[3,8,32,128]{3,2,1,0:T(8,128)S(1)} collective-permute-done((f32[3,8,32,128]{3,2,1,0:T(8,128)S(1)}, f32[3,8,32,128]{3,2,1,0:T(8,128)S(1)}, u32[]{:S(2)}, u32[]{:S(2)}) %collective-permute-start) | collective-permute-done | bytes 393248 | tf_op jit(solution)/shard_map/ppermute | solution.py:574
  17.1 0.9 pad_maximum_fusion.1
  18.0 1.3 collective-permute-start.3
  19.3 4.0 %collective-permute-start.2 = (f32[3,24,8,128]{3,2,1,0:T(8,128)S(1)}, f32[3,24,8,128]{3,2,1,0:T(8,128)S(1)}, u32[]{:S(2)}, u32[]{:S(2)}) collective-permute-start(f32[3,24,8,128]{3,2,1,0:T(8,128)S(1)} %get-tuple-element.35), channel_id=1, source_target_pairs={{0,16},{16,32},{32,48},{48,64},{64,80},{80,96},{96,112},{1,17},{17... | collective-permute-start | bytes 884744 | tf_op jit(solution)/shard_map/ppermute | solution.py:574
  23.3 2.9 %collective-permute-done.3.yhigh = f32[3,24,8,128]{3,2,1,0:T(8,128)S(1)} collective-permute-done((f32[3,24,8,128]{3,2,1,0:T(8,128)S(1)}, f32[3,24,8,128]{3,2,1,0:T(8,128)S(1)}, u32[]{:S(2)}, u32[]{:S(2)}) %collective-permute-start.3) | collective-permute-done | bytes 294944 | tf_op jit(solution)/shard_map/ppermute | solution.py:574
  26.2 1.8 %collective-permute-done.2.ylow = f32[3,24,8,128]{3,2,1,0:T(8,128)S(1)} collective-permute-done((f32[3,24,8,128]{3,2,1,0:T(8,128)S(1)}, f32[3,24,8,128]{3,2,1,0:T(8,128)S(1)}, u32[]{:S(2)}, u32[]{:S(2)}) %collective-permute-start.2) | collective-permute-done | bytes 294944 | tf_op jit(solution)/shard_map/ppermute | solution.py:574
  28.0 1.2 shard_map.50
  29.1 1.3 collective-permute-start.4
  30.4 1.3 collective-permute-start.5
  31.7 0.4 collective-permute-done.4.from_left
  32.2 3.8 %collective-permute-done.5.from_right = f32[27,8,128]{2,1,0:T(8,128)S(1)} collective-permute-done((f32[27,8,128]{2,1,0:T(8,128)S(1)}, f32[27,8,128]{2,1,0:T(8,128)S(1)}, u32[]{:S(2)}, u32[]{:S(2)}) %collective-permute-start.5) | collective-permute-done | bytes 110624 | tf_op jit(solution)/shard_map/ppermute | solution.py:574
  35.9 8.7 %shard_map.51 = (f32[16,5,8,128]{3,2,1,0:T(8,128)S(1)}, f32[12,24,128]{2,1,0:T(8,128)S(1)}, f32[12,24,128]{2,1,0:T(8,128)S(1)}, f32[144,8,256]{2,1,0:T(8,128)S(1...) custom-call(f32[72,6,8,128]{3,2,1,0:T(8,128)S(1)} %get-tuple-element, ...), custom_call_target="tpu_custom_call" | custom-call | tf_op jit(solution)/shard_map/pallas_call | solution.py:540
  44.7 22.1 %all_to_all.15.gathered = f32[16,5,8,128]{3,2,1,0:T(8,128)S(1)} all-to-all(f32[16,5,8,128]{3,2,1,0:T(8,128)S(1)} %get-tuple-element.21), channel_id=1, replica_groups=mesh['gx'=4,'gy'=8,'gz'=16] {'gz'}, dimensions={0} | all-to-all | bytes 655360 | tf_op jit(solution)/shard_map/all_to_all | solution.py:588
  66.8 0.1 shard_map.52
  66.9 27.8 %all_to_all.16.gathered = f32[8,14,8,128]{3,2,1,0:T(8,128)S(1)} all-to-all(f32[8,14,8,128]{3,2,1,0:T(8,128)S(1)} %get-tuple-element.23), channel_id=1, replica_groups=mesh['gx'=4,'gy'=8,'gz'=16] {'gy'}, dimensions={0} | all-to-all | bytes 917504 | tf_op jit(solution)/shard_map/all_to_all | solution.py:589
  94.7 0.2 shard_map.53
  94.9 18.5 %all_to_all.17.gathered = f32[4,67,8,128]{3,2,1,0:T(8,128)S(1)} all-to-all(f32[4,67,8,128]{3,2,1,0:T(8,128)S(1)} %get-tuple-element.25), channel_id=1, replica_groups=mesh['gx'=4,'gy'=8,'gz'=16] {'gx'}, dimensions={0} | all-to-all | bytes 2195456 | tf_op jit(solution)/shard_map/all_to_all | solution.py:590
  113.4 3.5 %collective-permute-start.6 = (f32[4,67,8,128]{3,2,1,0:T(8,128)S(1)}, f32[4,67,8,128]{3,2,1,0:T(8,128)S(1)}, u32[]{:S(2)}, u32[]{:S(2)}) collective-permute-start(f32[4,67,8,128]{3,2,1,0:T(8,128)S(1)} %all_to_all.17.gathered), channel_id=1, source_target_pairs={{0,1},{1,0},{2,3},{3,2},{4,5},{5,4},{6,7},{7,6},{8,9},{9,8},{10,11... | collective-permute-start | bytes 3293192 | tf_op jit(solution)/shard_map/ppermute | solution.py:591
  116.9 2.3 %collective-permute-done.6.other = f32[4,67,8,128]{3,2,1,0:T(8,128)S(1)} collective-permute-done((f32[4,67,8,128]{3,2,1,0:T(8,128)S(1)}, f32[4,67,8,128]{3,2,1,0:T(8,128)S(1)}, u32[]{:S(2)}, u32[]{:S(2)}) %collective-permute-start.6) | collective-permute-done | bytes 1097760 | tf_op jit(solution)/shard_map/ppermute | solution.py:591
  119.2 14.5 %shard_map.54 = (f32[8,32,128]{2,1,0:T(8,128)}, f32[8,32,128]{2,1,0:T(8,128)}) custom-call(f32[4,67,8,128]{3,2,1,0:T(8,128)S(1)} %all_to_all.17.gathered, f32[4,67,8,128]{3,2,1,0:T(8,128)S(1)} %collective-permute-done.6.other, f32[12,24,128]{2,1,0:T(8,128)S(1)} %get-tuple-element.26.pair, f32[12,24,128]{2,1,0:T(8,128)S(1)} %get-tuple-element.27.k1, ...), custom_call_target="tpu_custom_call" | custom-call | tf_op jit(solution)/shard_map/pallas_call | solution.py:540
Async XLA Ops:
  1.7 10.7 %collective-permute-start.1 = (f32[3,8,32,128]{3,2,1,0:T(8,128)S(1)}, f32[3,8,32,128]{3,2,1,0:T(8,128)S(1)}, u32[]{:S(2)}, u32[]{:S(2)}) collective-permute-start(f32[3,8,32,128]{3,2,1,0:T(8,128)S(1)} %pad_maximum_fusion.mid), channel_id=1, source_target_pairs={{1,0},{2,1},{3,2},{4,3},{5,4},{6,5},{7,6},{8,7},{9,8},{10,9},{11,1... | collective-permute-start | bytes 1179656 | tf_op jit(solution)/shard_map/ppermute | solution.py:574
  10.5 6.6 %collective-permute-start = (f32[3,8,32,128]{3,2,1,0:T(8,128)S(1)}, f32[3,8,32,128]{3,2,1,0:T(8,128)S(1)}, u32[]{:S(2)}, u32[]{:S(2)}) collective-permute-start(f32[3,8,32,128]{3,2,1,0:T(8,128)S(1)} %pad_maximum_fusion.mid), channel_id=1, source_target_pairs={{0,1},{1,2},{2,3},{3,4},{4,5},{5,6},{6,7},{7,8},{8,9},{9,10},{10,1... | collective-permute-start | bytes 1179656 | tf_op jit(solution)/shard_map/ppermute | solution.py:574
  18.0 8.2 %collective-permute-start.3 = (f32[3,24,8,128]{3,2,1,0:T(8,128)S(1)}, f32[3,24,8,128]{3,2,1,0:T(8,128)S(1)}, u32[]{:S(2)}, u32[]{:S(2)}) collective-permute-start(f32[3,24,8,128]{3,2,1,0:T(8,128)S(1)} %get-tuple-element.34), channel_id=1, source_target_pairs={{16,0},{32,16},{48,32},{64,48},{80,64},{96,80},{112,96},{17,1},{33... | collective-permute-start | bytes 884744 | tf_op jit(solution)/shard_map/ppermute | solution.py:574
  19.3 8.7 %collective-permute-start.2 = (f32[3,24,8,128]{3,2,1,0:T(8,128)S(1)}, f32[3,24,8,128]{3,2,1,0:T(8,128)S(1)}, u32[]{:S(2)}, u32[]{:S(2)}) collective-permute-start(f32[3,24,8,128]{3,2,1,0:T(8,128)S(1)} %get-tuple-element.35), channel_id=1, source_target_pairs={{0,16},{16,32},{32,48},{48,64},{64,80},{80,96},{96,112},{1,17},{17... | collective-permute-start | bytes 884744 | tf_op jit(solution)/shard_map/ppermute | solution.py:574
  29.1 3.0 %collective-permute-start.4 = (f32[27,8,128]{2,1,0:T(8,128)S(1)}, f32[27,8,128]{2,1,0:T(8,128)S(1)}, u32[]{:S(2)}, u32[]{:S(2)}) collective-permute-start(f32[27,8,128]{2,1,0:T(8,128)S(1)} %get-tuple-element.19), channel_id=1, source_target_pairs={{0,128},{128,256},{256,384},{1,129},{129,257},{257,385},{2,130},{1... | collective-permute-start | bytes 331784 | tf_op jit(solution)/shard_map/ppermute | solution.py:574
  30.4 5.5 %collective-permute-start.5 = (f32[27,8,128]{2,1,0:T(8,128)S(1)}, f32[27,8,128]{2,1,0:T(8,128)S(1)}, u32[]{:S(2)}, u32[]{:S(2)}) collective-permute-start(f32[27,8,128]{2,1,0:T(8,128)S(1)} %get-tuple-element.20), channel_id=1, source_target_pairs={{128,0},{256,128},{384,256},{129,1},{257,129},{385,257},{130,2},{2... | collective-permute-start | bytes 331784 | tf_op jit(solution)/shard_map/ppermute | solution.py:574
  113.4 5.8 %collective-permute-start.6 = (f32[4,67,8,128]{3,2,1,0:T(8,128)S(1)}, f32[4,67,8,128]{3,2,1,0:T(8,128)S(1)}, u32[]{:S(2)}, u32[]{:S(2)}) collective-permute-start(f32[4,67,8,128]{3,2,1,0:T(8,128)S(1)} %all_to_all.17.gathered), channel_id=1, source_target_pairs={{0,1},{1,0},{2,3},{3,2},{4,5},{5,4},{6,7},{7,6},{8,9},{9,8},{10,11... | collective-permute-start | bytes 3293192 | tf_op jit(solution)/shard_map/ppermute | solution.py:591

commit v4 on v3

--- a/solution.py
+++ b/solution.py
@@ -16,13 +16,15 @@
 KEEP = RHO_NEXT * RHO
 GAIN = 2.0 * RHO_NEXT / DELTA
 
+INNER = 16
+OUTER = 16
 F32 = jnp.float32
 BF16 = jnp.bfloat16
 VMEM = pl.BlockSpec(memory_space=pltpu.VMEM)
 LIMIT = 20 * 1024 * 1024
 
 
-def loop(first, end, body, carry, unroll=8):
+def loop(first, end, body, carry, unroll=16):
     count = end - first
     while count % unroll:
         unroll -= 1
@@ -62,6 +64,13 @@
 
 def pick(condition, number):
     return jnp.where(condition, jnp.float32(number), jnp.float32(0.0))
+
+
+def reciprocal(value):
+    guess = pl.reciprocal(value, approx=True)
+    for _ in range(2):
+        guess = guess * (2.0 - value * guess)
+    return guess
 
 
 def refine_matrix(size, out_size):
@@ -74,6 +83,12 @@
         own = jnp.where(child >= out_size * 3 // 4, own + size - wide, own)
         other = (own + 2 * (child & 1) - 1 + size) & (size - 1)
     return (pick(parent == own, 0.75) + pick(parent == other, 0.25)).astype(BF16)
+
+
+def ypack_kernel(mid, low, high, to_low, to_high):
+    for part, ref in enumerate((low, mid, high)):
+        to_low[:, 8 * part : 8 * part + 8] = ref[:, :, 0:8]
+        to_high[:, 8 * part : 8 * part + 8] = ref[:, :, 24:32]
 
 
 def xpack_kernel(mid, low, high, ylow, yhigh, window, to_left, to_right):
@@ -143,7 +158,7 @@
     diag = wx + behind(wx, 2) + wy + behind(wy, 1)
     diag = diag + jnp.concatenate([wz, pad], 0) + jnp.concatenate([pad, wz], 0)
     inside = kappa > 0.0
-    inverse = jnp.where(inside, 1.0 / jnp.where(inside, diag, 1.0), 0.0)
+    inverse = jnp.where(inside, reciprocal(diag), 0.0)
     return wx, wy, wz, inverse
 
 
@@ -191,7 +206,7 @@
         put(wx, z, x)
         put(wy, z, y)
         put(wz, z, above)
-        put(inverse, z, jnp.where(inside, 1.0 / jnp.where(inside, diag, 1.0), 0.0))
+        put(inverse, z, jnp.where(inside, reciprocal(diag), 0.0))
         return (after, above)
 
     half0 = 0.5 * plane(kappa, 0)
@@ -348,11 +363,11 @@
     lane = iota((8, 128), 1)
     group = lax.shift_right_logical(lane, 5)
     nothing = jnp.zeros((64, 128), F32)
-    for ref in (kappa, direction):
-        cput(ref, 0, nothing)
-        cput(ref, 33, nothing)
+    cput(kappa, 0, nothing)
+    cput(kappa, 33, nothing)
+    cput(rest, 32, nothing)
     cput(wz, 0, nothing)
-    answer[...] = jnp.zeros_like(answer)
+    direction[...] = jnp.zeros_like(direction)
 
     for source, parity in ((gathered, lax.axis_index("gz") & 1), (other, 1 - (lax.axis_index("gz") & 1))):
 
@@ -367,7 +382,6 @@
                     merged = shift(merged, -32 * q, 1)
                     if q < 2:
                         rest[(2 * gz + q) * 8 + gy] = merged
-                        direction[(2 * gz + q + 1) * 8 + gy] = merged
                     else:
                         kappa[(2 * gz + q - 1) * 8 + gy] = merged
             return carry
@@ -400,59 +414,60 @@
 
     norm = whole(loop(0, 32, weights, zero))
 
-    def apply(z, total):
-        v = cplane(direction, z + 1)
-        x = cplane(wx, z)
-        y = cplane(wy, z)
-        w = cplane(diag, z) * v
-        w = w - (x * ahead(v, 1) + behind(x * v, 1))
-        w = w - (y * ahead(v, 0) + behind(y * v, 0))
-        w = w - (cplane(wz, z + 1) * cplane(direction, z + 2) + cplane(wz, z) * cplane(direction, z))
-        cput(image, z, w)
-        return total + (v * w).reshape(8, 8, 128).sum(0)
-
-    def add_answer(z, alpha):
-        at = pl.ds((z + 3) * 10 + 1, 8)
-        answer[at] = answer[at] + (alpha * cplane(direction, z + 1)).reshape(8, 8, 128)
-
-    for repeat in range(ITERS):
-        alpha = norm / whole(loop(0, 32, apply, zero))
-        if repeat + 1 < ITERS:
-
-            def step(z, total):
-                add_answer(z, alpha)
-                r = cplane(rest, z) - alpha * cplane(image, z)
-                cput(rest, z, r)
-                return total + (r * r).reshape(8, 8, 128).sum(0)
-
-            norm_next = whole(loop(0, 32, step, zero))
-            beta = norm_next / norm
-
-            def turn(z, carry):
-                cput(direction, z + 1, cplane(rest, z) + beta * cplane(direction, z + 1))
-                return carry
-
-            loop(0, 32, turn, 0)
-            norm = norm_next
-        else:
-
-            def finish(z, carry):
-                add_answer(z, alpha)
-                return carry
-
-            loop(0, 32, finish, 0)
+    def image_of(beta):
+        def turned(z):
+            v = cplane(rest, z) + beta * cplane(direction, z + 1)
+            cput(direction, z + 1, v)
+            return v
+
+        def apply(z, carry):
+            before, v, total = carry
+            after = turned(z + 1)
+            x = cplane(wx, z)
+            y = cplane(wy, z)
+            w = cplane(diag, z) * v
+            w = w - (x * ahead(v, 1) + behind(x * v, 1))
+            w = w - (y * ahead(v, 0) + behind(y * v, 0))
+            w = w - (cplane(wz, z + 1) * after + cplane(wz, z) * before)
+            cput(image, z, w)
+            return v, after, total + (v * w).reshape(8, 8, 128).sum(0)
+
+        return whole(loop(0, 32, apply, (nothing, turned(0), zero), INNER)[2])
 
     gx = lax.axis_index("gx")
     gy = lax.axis_index("gy")
     gz = lax.axis_index("gz")
-    wide = iota((24, 128), 1)
+    answer[...] = jnp.zeros_like(answer)
+    picked = [(3 * z + t, 2 * gz - 3 + z, gy - 1 + t) for z in range(8) for t in range(3)]
+
+    def add_answer(alpha):
+        for k, z, y in picked:
+            tile = direction[(jnp.clip(z, 0, 31) + 1) * 8 + jnp.clip(y, 0, 7)]
+            answer[k] = answer[k] + alpha * tile
+
+    def iterate(repeat, carry):
+        norm, beta = carry
+        alpha = norm / image_of(beta)
+
+        def step(z, total):
+            r = cplane(rest, z) - alpha * cplane(image, z)
+            cput(rest, z, r)
+            return total + (r * r).reshape(8, 8, 128).sum(0)
+
+        add_answer(alpha)
+        norm_next = whole(loop(0, 32, step, zero, OUTER))
+        return norm_next, norm_next / norm
+
+    norm, beta = lax.fori_loop(0, ITERS - 1, iterate, (norm, jnp.zeros((1, 1), F32)))
+    add_answer(norm / image_of(beta))
+    wide = iota((8, 128), 1)
     position = jnp.where(wide < 64, wide, wide - 128) + 32 * gx
     known = (position >= 0) & (position < 128)
-    planes = []
-    for z in range(8):
-        block = answer[pl.ds((2 * gz + z) * 10 + gy, 3)].reshape(24, 128)
-        planes.append(jnp.where(known, pltpu.roll(block, (128 - 32 * gx) & 127, 1), 0.0))
-    return jnp.stack(planes)
+    tiles = []
+    for k, z, y in picked:
+        inside = known & (z >= 0) & (z < 32) & (y >= 0) & (y < 8)
+        tiles.append(jnp.where(inside, pltpu.roll(answer[k], (128 - 32 * gx) & 127, 1), 0.0))
+    return jnp.stack(tiles).reshape(8, 24, 128)
 
 
 def middle_fields(gathered, pair):
@@ -551,6 +566,7 @@
 MIDDLE = (12, 24, 128)
 COARSE = (256, 8, 128)
 PADDED = (272, 8, 128)
+YPACK = ([(3, 24, 8, 128)] * 2, [])
 XPACK = ([(72, 6, 8, 128), (27, 8, 128), (27, 8, 128)], [])
 DOWN = ([(16, 5, 8, 128), MIDDLE, MIDDLE] + [FINE] * 6, [FINE] * 5 + [(960, 128)] * 2 + [(24, 128)])
 TURN = ([(8, 14, 8, 128), MIDDLE], [])
@@ -558,7 +574,7 @@
 UP = (
     [(8, 32, 128)] * 2,
     [(576, 128)] + [(768, 128)] * 2 + [FINE] * 4
-    + [PADDED] + [COARSE] * 2 + [PADDED] + [COARSE] * 2 + [PADDED, COARSE, (380, 8, 128)],
+    + [PADDED] + [COARSE] * 2 + [PADDED, COARSE] + [PADDED] * 2 + [COARSE, (24, 8, 128)],
 )
 
 
@@ -577,8 +593,7 @@
 def local(right_side, guess, coefficient):
     mine = jnp.stack([guess, right_side, coefficient])
     low, high = both_ways(mine, mine, "gz")
-    column = jnp.concatenate([low, mine, high], 1)
-    ylow, yhigh = both_ways(column[:, :, :8], column[:, :, 24:], "gy")
+    ylow, yhigh = both_ways(*run(ypack_kernel, *YPACK, mine, low, high), "gy")
     window, to_left, to_right = run(
         xpack_kernel, *XPACK, mine, low, high, ylow, yhigh
     )

time: 134 us -> 130 us (0.970)
  Pallas kernels: 24.8 us -> 21 us
  starting transfers between devices: 22 us -> 19.6 us
  waiting for transfers between devices: 15.9 us -> 18.1 us
    pallas_call x5 -> x6, Pallas kernels: 24.8 us -> 21 us  [run(): pl.pallas_call(kernel, out_shape=[jax.ShapeDtypeStruct(shape, F32) for sh...]
    all_to_all x1, blocking collectives: 22.1 us -> 25.1 us  [local(): lax.all_to_all(share, 'gz', 0, 0)]
    ppermute x3, starting transfers between devices: 7.22 us -> 4.74 us  [both_ways(): lax.ppermute(to_high, axis, up(axis))]
    all_to_all x1, blocking collectives: 27.8 us -> 25.4 us  [local(): lax.all_to_all(share, 'gy', 0, 0)]
where the time goes in v4:
time: 130 us
  blocking collectives  69.1 us (53%)
  Pallas kernels  21 us (16%)
  starting transfers between devices  19.6 us (15%)
  waiting for transfers between devices  18.1 us (14%)
    all_to_all x1, blocking collectives, local(): lax.all_to_all(share, 'gy', 0, 0)  25.4 us
    all_to_all x1, blocking collectives, local(): lax.all_to_all(share, 'gz', 0, 0)  25.1 us
    pallas_call x6, Pallas kernels, run(): pl.pallas_call(kernel, out_shape=[jax.ShapeDtypeStruct(shape, F32) for sh...  21 us
    all_to_all x1, blocking collectives, local(): whole = lax.all_to_all(share, 'gx', 0, 0)  18.5 us
    ppermute x3, starting transfers between devices, both_ways(): lax.ppermute(to_low, axis, down(axis))  11.4 us
    ppermute x3, waiting for transfers between devices, both_ways(): lax.ppermute(to_high, axis, up(axis))  7.92 us
    ppermute x3, waiting for transfers between devices, both_ways(): lax.ppermute(to_low, axis, down(axis))  7.88 us
    ppermute x3, starting transfers between devices, both_ways(): lax.ppermute(to_high, axis, up(axis))  4.74 us
  transfers between devices with their start and end apart: 7, of which 6 were waited for; matrix products, arithmetic and copies ran while one was open for 0% of the time, Pallas kernels for 0%

profile of v4, /device:TPU:1, one launch (start us, length us, event | category | flops | bytes accessed | tf_op | source)
XLA Modules:
  0.0 129.6 jit_solution(16602909437593465730)
XLA Ops:
  0.6 1.1 pad_maximum_fusion.mid
  1.7 8.8 %collective-permute-start.1 = (f32[3,8,32,128]{3,2,1,0:T(8,128)S(1)}, f32[3,8,32,128]{3,2,1,0:T(8,128)S(1)}, u32[]{:S(2)}, u32[]{:S(2)}) collective-permute-start(f32[3,8,32,128]{3,2,1,0:T(8,128)S(1)} %pad_maximum_fusion.mid), channel_id=1, source_target_pairs={{1,0},{2,1},{3,2},{4,3},{5,4},{6,5},{7,6},{8,7},{9,8},{10,9},{11,1... | collective-permute-start | bytes 1179656 | tf_op jit(solution)/shard_map/ppermute | solution.py:590
  10.5 1.9 %collective-permute-start = (f32[3,8,32,128]{3,2,1,0:T(8,128)S(1)}, f32[3,8,32,128]{3,2,1,0:T(8,128)S(1)}, u32[]{:S(2)}, u32[]{:S(2)}) collective-permute-start(f32[3,8,32,128]{3,2,1,0:T(8,128)S(1)} %pad_maximum_fusion.mid), channel_id=1, source_target_pairs={{0,1},{1,2},{2,3},{3,4},{4,5},{5,6},{6,7},{7,8},{8,9},{9,10},{10,1... | collective-permute-start | bytes 1179656 | tf_op jit(solution)/shard_map/ppermute | solution.py:590
  12.4 0.0 collective-permute-done.1.high
  12.4 4.7 %collective-permute-done.low = f32[3,8,32,128]{3,2,1,0:T(8,128)S(1)} collective-permute-done((f32[3,8,32,128]{3,2,1,0:T(8,128)S(1)}, f32[3,8,32,128]{3,2,1,0:T(8,128)S(1)}, u32[]{:S(2)}, u32[]{:S(2)}) %collective-permute-start) | collective-permute-done | bytes 393248 | tf_op jit(solution)/shard_map/ppermute | solution.py:590
  17.2 1.3 %collective-permute-start.2 = (f32[3,24,8,128]{3,2,1,0:T(8,128)S(1)}, f32[3,24,8,128]{3,2,1,0:T(8,128)S(1)}, u32[]{:S(2)}, u32[]{:S(2)}) collective-permute-start(f32[3,24,8,128]{3,2,1,0:T(8,128)S(1)} %get-tuple-element.20), channel_id=1, source_target_pairs={{0,16},{16,32},{32,48},{48,64},{64,80},{80,96},{96,112},{1,17},{17... | collective-permute-start | bytes 884744 | tf_op jit(solution)/shard_map/ppermute | solution.py:590
  18.5 1.3 collective-permute-start.3
  19.8 2.8 %collective-permute-done.2.ylow = f32[3,24,8,128]{3,2,1,0:T(8,128)S(1)} collective-permute-done((f32[3,24,8,128]{3,2,1,0:T(8,128)S(1)}, f32[3,24,8,128]{3,2,1,0:T(8,128)S(1)}, u32[]{:S(2)}, u32[]{:S(2)}) %collective-permute-start.2) | collective-permute-done | bytes 294944 | tf_op jit(solution)/shard_map/ppermute | solution.py:590
  22.6 4.1 %collective-permute-done.3.yhigh = f32[3,24,8,128]{3,2,1,0:T(8,128)S(1)} collective-permute-done((f32[3,24,8,128]{3,2,1,0:T(8,128)S(1)}, f32[3,24,8,128]{3,2,1,0:T(8,128)S(1)}, u32[]{:S(2)}, u32[]{:S(2)}) %collective-permute-start.3) | collective-permute-done | bytes 294944 | tf_op jit(solution)/shard_map/ppermute | solution.py:590
  26.7 0.9 shard_map.51
  27.6 1.5 %collective-permute-start.4 = (f32[27,8,128]{2,1,0:T(8,128)S(1)}, f32[27,8,128]{2,1,0:T(8,128)S(1)}, u32[]{:S(2)}, u32[]{:S(2)}) collective-permute-start(f32[27,8,128]{2,1,0:T(8,128)S(1)} %get-tuple-element.23), channel_id=1, source_target_pairs={{0,128},{128,256},{256,384},{1,129},{129,257},{257,385},{2,130},{1... | collective-permute-start | bytes 331784 | tf_op jit(solution)/shard_map/ppermute | solution.py:590
  29.1 1.3 collective-permute-start.5
  30.4 0.4 collective-permute-done.4.from_left
  30.9 3.8 %collective-permute-done.5.from_right = f32[27,8,128]{2,1,0:T(8,128)S(1)} collective-permute-done((f32[27,8,128]{2,1,0:T(8,128)S(1)}, f32[27,8,128]{2,1,0:T(8,128)S(1)}, u32[]{:S(2)}, u32[]{:S(2)}) %collective-permute-start.5) | collective-permute-done | bytes 110624 | tf_op jit(solution)/shard_map/ppermute | solution.py:590
  34.6 8.2 %shard_map.52 = (f32[16,5,8,128]{3,2,1,0:T(8,128)S(1)}, f32[12,24,128]{2,1,0:T(8,128)S(1)}, f32[12,24,128]{2,1,0:T(8,128)S(1)}, f32[144,8,256]{2,1,0:T(8,128)S(1...) custom-call(f32[72,6,8,128]{3,2,1,0:T(8,128)S(1)} %get-tuple-element, ...), custom_call_target="tpu_custom_call" | custom-call | tf_op jit(solution)/shard_map/pallas_call | solution.py:555
  42.9 25.1 %all_to_all.15.gathered = f32[16,5,8,128]{3,2,1,0:T(8,128)S(1)} all-to-all(f32[16,5,8,128]{3,2,1,0:T(8,128)S(1)} %get-tuple-element.25), channel_id=1, replica_groups=mesh['gx'=4,'gy'=8,'gz'=16] {'gz'}, dimensions={0} | all-to-all | bytes 655360 | tf_op jit(solution)/shard_map/all_to_all | solution.py:603
  68.0 0.1 shard_map.53
  68.2 25.4 %all_to_all.16.gathered = f32[8,14,8,128]{3,2,1,0:T(8,128)S(1)} all-to-all(f32[8,14,8,128]{3,2,1,0:T(8,128)S(1)} %get-tuple-element.27), channel_id=1, replica_groups=mesh['gx'=4,'gy'=8,'gz'=16] {'gy'}, dimensions={0} | all-to-all | bytes 917504 | tf_op jit(solution)/shard_map/all_to_all | solution.py:604
  93.6 0.2 shard_map.54
  93.7 18.5 %all_to_all.17.gathered = f32[4,67,8,128]{3,2,1,0:T(8,128)S(1)} all-to-all(f32[4,67,8,128]{3,2,1,0:T(8,128)S(1)} %get-tuple-element.29), channel_id=1, replica_groups=mesh['gx'=4,'gy'=8,'gz'=16] {'gx'}, dimensions={0} | all-to-all | bytes 2195456 | tf_op jit(solution)/shard_map/all_to_all | solution.py:605
  112.3 3.5 %collective-permute-start.6 = (f32[4,67,8,128]{3,2,1,0:T(8,128)S(1)}, f32[4,67,8,128]{3,2,1,0:T(8,128)S(1)}, u32[]{:S(2)}, u32[]{:S(2)}) collective-permute-start(f32[4,67,8,128]{3,2,1,0:T(8,128)S(1)} %all_to_all.17.gathered), channel_id=1, source_target_pairs={{0,1},{1,0},{2,3},{3,2},{4,5},{5,4},{6,7},{7,6},{8,9},{9,8},{10,11... | collective-permute-start | bytes 3293192 | tf_op jit(solution)/shard_map/ppermute | solution.py:606
  115.7 2.3 %collective-permute-done.6.other = f32[4,67,8,128]{3,2,1,0:T(8,128)S(1)} collective-permute-done((f32[4,67,8,128]{3,2,1,0:T(8,128)S(1)}, f32[4,67,8,128]{3,2,1,0:T(8,128)S(1)}, u32[]{:S(2)}, u32[]{:S(2)}) %collective-permute-start.6) | collective-permute-done | bytes 1097760 | tf_op jit(solution)/shard_map/ppermute | solution.py:606
  118.1 11.5 %shard_map.55 = (f32[8,32,128]{2,1,0:T(8,128)}, f32[8,32,128]{2,1,0:T(8,128)}) custom-call(f32[4,67,8,128]{3,2,1,0:T(8,128)S(1)} %all_to_all.17.gathered, f32[4,67,8,128]{3,2,1,0:T(8,128)S(1)} %collective-permute-done.6.other, f32[12,24,128]{2,1,0:T(8,128)S(1)} %get-tuple-element.30.pair, f32[12,24,128]{2,1,0:T(8,128)S(1)} %get-tuple-element.31.k1, ...), custom_call_target="tpu_custom_call" | custom-call | tf_op jit(solution)/shard_map/pallas_call | solution.py:555
  (1 shorter events, 0.0 us)
Async XLA Ops:
  1.7 10.7 %collective-permute-start.1 = (f32[3,8,32,128]{3,2,1,0:T(8,128)S(1)}, f32[3,8,32,128]{3,2,1,0:T(8,128)S(1)}, u32[]{:S(2)}, u32[]{:S(2)}) collective-permute-start(f32[3,8,32,128]{3,2,1,0:T(8,128)S(1)} %pad_maximum_fusion.mid), channel_id=1, source_target_pairs={{1,0},{2,1},{3,2},{4,3},{5,4},{6,5},{7,6},{8,7},{9,8},{10,9},{11,1... | collective-permute-start | bytes 1179656 | tf_op jit(solution)/shard_map/ppermute | solution.py:590
  10.5 6.6 %collective-permute-start = (f32[3,8,32,128]{3,2,1,0:T(8,128)S(1)}, f32[3,8,32,128]{3,2,1,0:T(8,128)S(1)}, u32[]{:S(2)}, u32[]{:S(2)}) collective-permute-start(f32[3,8,32,128]{3,2,1,0:T(8,128)S(1)} %pad_maximum_fusion.mid), channel_id=1, source_target_pairs={{0,1},{1,2},{2,3},{3,4},{4,5},{5,6},{6,7},{7,8},{8,9},{9,10},{10,1... | collective-permute-start | bytes 1179656 | tf_op jit(solution)/shard_map/ppermute | solution.py:590
  17.2 5.4 %collective-permute-start.2 = (f32[3,24,8,128]{3,2,1,0:T(8,128)S(1)}, f32[3,24,8,128]{3,2,1,0:T(8,128)S(1)}, u32[]{:S(2)}, u32[]{:S(2)}) collective-permute-start(f32[3,24,8,128]{3,2,1,0:T(8,128)S(1)} %get-tuple-element.20), channel_id=1, source_target_pairs={{0,16},{16,32},{32,48},{48,64},{64,80},{80,96},{96,112},{1,17},{17... | collective-permute-start | bytes 884744 | tf_op jit(solution)/shard_map/ppermute | solution.py:590
  18.5 8.2 %collective-permute-start.3 = (f32[3,24,8,128]{3,2,1,0:T(8,128)S(1)}, f32[3,24,8,128]{3,2,1,0:T(8,128)S(1)}, u32[]{:S(2)}, u32[]{:S(2)}) collective-permute-start(f32[3,24,8,128]{3,2,1,0:T(8,128)S(1)} %get-tuple-element.21), channel_id=1, source_target_pairs={{16,0},{32,16},{48,32},{64,48},{80,64},{96,80},{112,96},{17,1},{33... | collective-permute-start | bytes 884744 | tf_op jit(solution)/shard_map/ppermute | solution.py:590
  27.6 3.3 %collective-permute-start.4 = (f32[27,8,128]{2,1,0:T(8,128)S(1)}, f32[27,8,128]{2,1,0:T(8,128)S(1)}, u32[]{:S(2)}, u32[]{:S(2)}) collective-permute-start(f32[27,8,128]{2,1,0:T(8,128)S(1)} %get-tuple-element.23), channel_id=1, source_target_pairs={{0,128},{128,256},{256,384},{1,129},{129,257},{257,385},{2,130},{1... | collective-permute-start | bytes 331784 | tf_op jit(solution)/shard_map/ppermute | solution.py:590
  29.1 5.5 %collective-permute-start.5 = (f32[27,8,128]{2,1,0:T(8,128)S(1)}, f32[27,8,128]{2,1,0:T(8,128)S(1)}, u32[]{:S(2)}, u32[]{:S(2)}) collective-permute-start(f32[27,8,128]{2,1,0:T(8,128)S(1)} %get-tuple-element.24), channel_id=1, source_target_pairs={{128,0},{256,128},{384,256},{129,1},{257,129},{385,257},{130,2},{2... | collective-permute-start | bytes 331784 | tf_op jit(solution)/shard_map/ppermute | solution.py:590
  112.3 5.8 %collective-permute-start.6 = (f32[4,67,8,128]{3,2,1,0:T(8,128)S(1)}, f32[4,67,8,128]{3,2,1,0:T(8,128)S(1)}, u32[]{:S(2)}, u32[]{:S(2)}) collective-permute-start(f32[4,67,8,128]{3,2,1,0:T(8,128)S(1)} %all_to_all.17.gathered), channel_id=1, source_target_pairs={{0,1},{1,0},{2,3},{3,2},{4,5},{5,4},{6,7},{7,6},{8,9},{9,8},{10,11... | collective-permute-start | bytes 3293192 | tf_op jit(solution)/shard_map/ppermute | solution.py:606

commit v5 on v4

--- a/solution.py
+++ b/solution.py
@@ -85,19 +85,27 @@
     return (pick(parent == own, 0.75) + pick(parent == other, 0.25)).astype(BF16)
 
 
-def ypack_kernel(mid, low, high, to_low, to_high):
-    for part, ref in enumerate((low, mid, high)):
-        to_low[:, 8 * part : 8 * part + 8] = ref[:, :, 0:8]
-        to_high[:, 8 * part : 8 * part + 8] = ref[:, :, 24:32]
-
-
-def xpack_kernel(mid, low, high, ylow, yhigh, window, to_left, to_right):
-    for a in range(3):
-        window[a * 24 : a * 24 + 8, 1:5] = low[a].reshape(8, 4, 8, 128)
-        window[a * 24 + 8 : a * 24 + 16, 1:5] = mid[a].reshape(8, 4, 8, 128)
-        window[a * 24 + 16 : a * 24 + 24, 1:5] = high[a].reshape(8, 4, 8, 128)
-        window[a * 24 : a * 24 + 24, 0] = ylow[a]
-        window[a * 24 : a * 24 + 24, 5] = yhigh[a]
+TRAVEL = [(a, z) for a, skip in enumerate((1, 2, 0)) for z in range(skip, 24 - skip)]
+
+
+def window_rows(mine, chip, beside, a, z, rows):
+    if z // 8 == 1:
+        return mine[a, z - 8, rows]
+    odd = (lax.axis_index("gz") & 1) == 1
+    return jnp.where(odd == (z < 8), chip[a, z % 8, rows], beside[a, z % 8, rows])
+
+
+def ypack_kernel(mine, chip, beside, to_high, to_low):
+    for i, (a, z) in enumerate(TRAVEL):
+        to_low[i] = window_rows(mine, chip, beside, a, z, slice(0, 8))
+        to_high[i] = window_rows(mine, chip, beside, a, z, slice(24, 32))
+
+
+def xpack_kernel(mine, chip, beside, ylow, yhigh, window, to_right, to_left):
+    for i, (a, z) in enumerate(TRAVEL):
+        window[24 * a + z, 0] = ylow[i]
+        window[24 * a + z, 1:5] = window_rows(mine, chip, beside, a, z, slice(0, 32)).reshape(4, 8, 128)
+        window[24 * a + z, 5] = yhigh[i]
     slot = lax.shift_right_logical(iota((8, 128), 1), 3)
 
     def group(i, carry):
@@ -209,17 +217,17 @@
         put(inverse, z, jnp.where(inside, reciprocal(diag), 0.0))
         return (after, above)
 
-    half0 = 0.5 * plane(kappa, 0)
     half1 = 0.5 * plane(kappa, 1)
-    put(wz, 0, half0 + half1)
-    loop(1, 23, weights, (half1, half0 + half1))
+    half2 = 0.5 * plane(kappa, 2)
+    put(wz, 1, half1 + half2)
+    loop(2, 22, weights, (half2, half1 + half2))
 
     def first(z, v, minus):
         r = plane(right, z) + minus
         put(rest, z, r)
         put(update, z, FIRST * r * plane(inverse, z))
 
-    sweep(1, 22, guess, wx, wy, wz, first)
+    sweep(2, 21, guess, wx, wy, wz, first)
 
     def next_step(z, v, minus):
         r = plane(rest, z) + minus
@@ -228,12 +236,12 @@
         put(second, z, d)
         put(iterate, z, plane(guess, z) + v + d)
 
-    sweep(2, 21, update, wx, wy, wz, next_step)
+    sweep(3, 20, update, wx, wy, wz, next_step)
 
     def last(z, v, minus):
         put(rest, z, plane(rest, z) + minus)
 
-    sweep(3, 20, second, wx, wy, wz, last)
+    sweep(4, 19, second, wx, wy, wz, last)
 
     def add_pairs(ref, start, count, at):
         def body(m, carry):
@@ -566,7 +574,7 @@
 MIDDLE = (12, 24, 128)
 COARSE = (256, 8, 128)
 PADDED = (272, 8, 128)
-YPACK = ([(3, 24, 8, 128)] * 2, [])
+YPACK = ([(66, 8, 128)] * 2, [])
 XPACK = ([(72, 6, 8, 128), (27, 8, 128), (27, 8, 128)], [])
 DOWN = ([(16, 5, 8, 128), MIDDLE, MIDDLE] + [FINE] * 6, [FINE] * 5 + [(960, 128)] * 2 + [(24, 128)])
 TURN = ([(8, 14, 8, 128), MIDDLE], [])
@@ -592,10 +600,12 @@
 
 def local(right_side, guess, coefficient):
     mine = jnp.stack([guess, right_side, coefficient])
-    low, high = both_ways(mine, mine, "gz")
-    ylow, yhigh = both_ways(*run(ypack_kernel, *YPACK, mine, low, high), "gy")
-    window, to_left, to_right = run(
-        xpack_kernel, *XPACK, mine, low, high, ylow, yhigh
+    beside = lax.ppermute(mine, "gz", [(i, ((i + 1) ^ 1) - 1) for i in range(1, 15)])
+    chip = lax.ppermute(mine, "gz", [(i, i ^ 1) for i in range(16)])
+    to_high, to_low = run(ypack_kernel, *YPACK, mine, chip, beside)
+    ylow, yhigh = both_ways(to_low, to_high, "gy")
+    window, to_right, to_left = run(
+        xpack_kernel, *XPACK, mine, chip, beside, ylow, yhigh
     )
     from_left, from_right = both_ways(to_left, to_right, "gx")
 

time: 130 us -> 127 us (0.977)
  blocking collectives: 69.1 us -> 65.9 us
  starting transfers between devices: 19.6 us -> 21.9 us
    ppermute x0 -> x2, starting transfers between devices: none -> 9.47 us  [the longest x1 4.88 us: local(): chip = lax.ppermute(mine, 'gz', [(i, i ^ 1) for i in range(16)])]
    ppermute x3 -> x2, starting transfers between devices: 11.4 us -> 2.58 us  [both_ways(): lax.ppermute(to_low, axis, down(axis))]
    all_to_all x1, blocking collectives: 25.1 us -> 22.2 us  [local(): lax.all_to_all(share, 'gz', 0, 0)]
    ppermute x3 -> x2, waiting for transfers between devices: 7.92 us -> 5.22 us  [both_ways(): lax.ppermute(to_high, axis, up(axis))]
    ppermute x3 -> x2, starting transfers between devices: 4.74 us -> 6.37 us  [both_ways(): lax.ppermute(to_high, axis, up(axis))]
    ppermute x0 -> x2, waiting for transfers between devices: none -> 1.33 us  [the longest x1 0.77 us: local(): chip = lax.ppermute(mine, 'gz', [(i, i ^ 1) for i in range(16)])]
    ppermute x3 -> x2, waiting for transfers between devices: 7.88 us -> 8.49 us  [both_ways(): lax.ppermute(to_low, axis, down(axis))]
  transfers between devices with their start and end apart: 7 -> 7, of which waited for: 6 -> 7; matrix products, arithmetic and copies ran while one was open for 0% -> 0% of each run, Pallas kernels for 0% -> 0%
where the time goes in v5:
time: 127 us
  blocking collectives  65.9 us (52%)
  starting transfers between devices  21.9 us (17%)
  Pallas kernels  20 us (16%)
  waiting for transfers between devices  17.4 us (14%)
    all_to_all x1, blocking collectives, local(): lax.all_to_all(share, 'gy', 0, 0)  25.2 us
    all_to_all x1, blocking collectives, local(): lax.all_to_all(share, 'gz', 0, 0)  22.2 us
    pallas_call x6, Pallas kernels, run(): pl.pallas_call(kernel, out_shape=[jax.ShapeDtypeStruct(shape, F32) for sh...  20 us
    all_to_all x1, blocking collectives, local(): whole = lax.all_to_all(share, 'gx', 0, 0)  18.5 us
    ppermute x2, waiting for transfers between devices, both_ways(): lax.ppermute(to_low, axis, down(axis))  8.49 us
    ppermute x2, starting transfers between devices, both_ways(): lax.ppermute(to_high, axis, up(axis))  6.37 us
    ppermute x2, waiting for transfers between devices, both_ways(): lax.ppermute(to_high, axis, up(axis))  5.22 us
    ppermute x1, starting transfers between devices, local(): chip = lax.ppermute(mine, 'gz', [(i, i ^ 1) for i in range(16)])  4.88 us
  transfers between devices with their start and end apart: 7, of which 7 were waited for; matrix products, arithmetic and copies ran while one was open for 0% of the time, Pallas kernels for 0%

profile of v5, /device:TPU:1, one launch (start us, length us, event | category | flops | bytes accessed | tf_op | source)
XLA Modules:
  0.0 126.9 jit_solution(6989822611971249059)
XLA Ops:
  0.6 1.1 pad_maximum_fusion.mine
  1.7 4.6 %collective-permute-start.1 = (f32[3,8,32,128]{3,2,1,0:T(8,128)S(1)}, f32[3,8,32,128]{3,2,1,0:T(8,128)S(1)}, u32[]{:S(2)}, u32[]{:S(2)}) collective-permute-start(f32[3,8,32,128]{3,2,1,0:T(8,128)S(1)} %pad_maximum_fusion.mine), channel_id=1, source_target_pairs={{1,2},{2,1},{3,4},{4,3},{5,6},{6,5},{7,8},{8,7},{9,10},{10,9},{11,... | collective-permute-start | bytes 1179656 | tf_op jit(solution)/shard_map/ppermute | solution.py:603
  6.3 4.9 %collective-permute-start = (f32[3,8,32,128]{3,2,1,0:T(8,128)S(1)}, f32[3,8,32,128]{3,2,1,0:T(8,128)S(1)}, u32[]{:S(2)}, u32[]{:S(2)}) collective-permute-start(f32[3,8,32,128]{3,2,1,0:T(8,128)S(1)} %pad_maximum_fusion.mine), channel_id=1, source_target_pairs={{0,1},{1,0},{2,3},{3,2},{4,5},{5,4},{6,7},{7,6},{8,9},{9,8},{10,11... | collective-permute-start | bytes 1179656 | tf_op jit(solution)/shard_map/ppermute | solution.py:604
  11.2 0.6 collective-permute-done.1.beside
  11.7 0.8 collective-permute-done.chip
  12.6 3.2 %collective-permute-start.2 = (f32[66,8,128]{2,1,0:T(8,128)S(1)}, f32[66,8,128]{2,1,0:T(8,128)S(1)}, u32[]{:S(2)}, u32[]{:S(2)}) collective-permute-start(f32[66,8,128]{2,1,0:T(8,128)S(1)} %get-tuple-element.20), channel_id=1, source_target_pairs={{0,16},{16,32},{32,48},{48,64},{64,80},{80,96},{96,112},{1,17},{17... | collective-permute-start | bytes 811016 | tf_op jit(solution)/shard_map/ppermute | solution.py:598
  15.8 1.3 %collective-permute-start.3 = (f32[66,8,128]{2,1,0:T(8,128)S(1)}, f32[66,8,128]{2,1,0:T(8,128)S(1)}, u32[]{:S(2)}, u32[]{:S(2)}) collective-permute-start(f32[66,8,128]{2,1,0:T(8,128)S(1)} %get-tuple-element.21), channel_id=1, source_target_pairs={{16,0},{32,16},{48,32},{64,48},{80,64},{96,80},{112,96},{17,1},{33... | collective-permute-start | bytes 811016 | tf_op jit(solution)/shard_map/ppermute | solution.py:598
  17.1 3.7 %collective-permute-done.2.ylow = f32[66,8,128]{2,1,0:T(8,128)S(1)} collective-permute-done((f32[66,8,128]{2,1,0:T(8,128)S(1)}, f32[66,8,128]{2,1,0:T(8,128)S(1)}, u32[]{:S(2)}, u32[]{:S(2)}) %collective-permute-start.2) | collective-permute-done | bytes 270368 | tf_op jit(solution)/shard_map/ppermute | solution.py:598
  20.8 4.5 %collective-permute-done.3.yhigh = f32[66,8,128]{2,1,0:T(8,128)S(1)} collective-permute-done((f32[66,8,128]{2,1,0:T(8,128)S(1)}, f32[66,8,128]{2,1,0:T(8,128)S(1)}, u32[]{:S(2)}, u32[]{:S(2)}) %collective-permute-start.3) | collective-permute-done | bytes 270368 | tf_op jit(solution)/shard_map/ppermute | solution.py:598
  25.3 0.9 shard_map.51
  26.2 3.1 %collective-permute-start.4 = (f32[27,8,128]{2,1,0:T(8,128)S(1)}, f32[27,8,128]{2,1,0:T(8,128)S(1)}, u32[]{:S(2)}, u32[]{:S(2)}) collective-permute-start(f32[27,8,128]{2,1,0:T(8,128)S(1)} %get-tuple-element.23), channel_id=1, source_target_pairs={{0,128},{128,256},{256,384},{1,129},{129,257},{257,385},{2,130},{1... | collective-permute-start | bytes 331784 | tf_op jit(solution)/shard_map/ppermute | solution.py:598
  29.4 1.3 %collective-permute-start.5 = (f32[27,8,128]{2,1,0:T(8,128)S(1)}, f32[27,8,128]{2,1,0:T(8,128)S(1)}, u32[]{:S(2)}, u32[]{:S(2)}) collective-permute-start(f32[27,8,128]{2,1,0:T(8,128)S(1)} %get-tuple-element.24), channel_id=1, source_target_pairs={{128,0},{256,128},{384,256},{129,1},{257,129},{385,257},{130,2},{2... | collective-permute-start | bytes 331784 | tf_op jit(solution)/shard_map/ppermute | solution.py:598
  30.7 1.5 %collective-permute-done.4.from_left = f32[27,8,128]{2,1,0:T(8,128)S(1)} collective-permute-done((f32[27,8,128]{2,1,0:T(8,128)S(1)}, f32[27,8,128]{2,1,0:T(8,128)S(1)}, u32[]{:S(2)}, u32[]{:S(2)}) %collective-permute-start.4) | collective-permute-done | bytes 110624 | tf_op jit(solution)/shard_map/ppermute | solution.py:598
  32.1 4.0 %collective-permute-done.5.from_right = f32[27,8,128]{2,1,0:T(8,128)S(1)} collective-permute-done((f32[27,8,128]{2,1,0:T(8,128)S(1)}, f32[27,8,128]{2,1,0:T(8,128)S(1)}, u32[]{:S(2)}, u32[]{:S(2)}) %collective-permute-start.5) | collective-permute-done | bytes 110624 | tf_op jit(solution)/shard_map/ppermute | solution.py:598
  36.2 7.2 %shard_map.52 = (f32[16,5,8,128]{3,2,1,0:T(8,128)S(1)}, f32[12,24,128]{2,1,0:T(8,128)S(1)}, f32[12,24,128]{2,1,0:T(8,128)S(1)}, f32[144,8,256]{2,1,0:T(8,128)S(1...) custom-call(f32[72,6,8,128]{3,2,1,0:T(8,128)S(1)} %get-tuple-element, ...), custom_call_target="tpu_custom_call" | custom-call | tf_op jit(solution)/shard_map/pallas_call | solution.py:563
  43.4 22.2 %all_to_all.15.gathered = f32[16,5,8,128]{3,2,1,0:T(8,128)S(1)} all-to-all(f32[16,5,8,128]{3,2,1,0:T(8,128)S(1)} %get-tuple-element.25), channel_id=1, replica_groups=mesh['gx'=4,'gy'=8,'gz'=16] {'gz'}, dimensions={0} | all-to-all | bytes 655360 | tf_op jit(solution)/shard_map/all_to_all | solution.py:613
  65.6 0.1 shard_map.53
  65.7 25.2 %all_to_all.16.gathered = f32[8,14,8,128]{3,2,1,0:T(8,128)S(1)} all-to-all(f32[8,14,8,128]{3,2,1,0:T(8,128)S(1)} %get-tuple-element.27), channel_id=1, replica_groups=mesh['gx'=4,'gy'=8,'gz'=16] {'gy'}, dimensions={0} | all-to-all | bytes 917504 | tf_op jit(solution)/shard_map/all_to_all | solution.py:614
  90.9 0.2 shard_map.54
  91.1 18.5 %all_to_all.17.gathered = f32[4,67,8,128]{3,2,1,0:T(8,128)S(1)} all-to-all(f32[4,67,8,128]{3,2,1,0:T(8,128)S(1)} %get-tuple-element.29), channel_id=1, replica_groups=mesh['gx'=4,'gy'=8,'gz'=16] {'gx'}, dimensions={0} | all-to-all | bytes 2195456 | tf_op jit(solution)/shard_map/all_to_all | solution.py:615
  109.6 3.5 %collective-permute-start.6 = (f32[4,67,8,128]{3,2,1,0:T(8,128)S(1)}, f32[4,67,8,128]{3,2,1,0:T(8,128)S(1)}, u32[]{:S(2)}, u32[]{:S(2)}) collective-permute-start(f32[4,67,8,128]{3,2,1,0:T(8,128)S(1)} %all_to_all.17.gathered), channel_id=1, source_target_pairs={{0,1},{1,0},{2,3},{3,2},{4,5},{5,4},{6,7},{7,6},{8,9},{9,8},{10,11... | collective-permute-start | bytes 3293192 | tf_op jit(solution)/shard_map/ppermute | solution.py:616
  113.1 2.3 %collective-permute-done.6.other = f32[4,67,8,128]{3,2,1,0:T(8,128)S(1)} collective-permute-done((f32[4,67,8,128]{3,2,1,0:T(8,128)S(1)}, f32[4,67,8,128]{3,2,1,0:T(8,128)S(1)}, u32[]{:S(2)}, u32[]{:S(2)}) %collective-permute-start.6) | collective-permute-done | bytes 1097760 | tf_op jit(solution)/shard_map/ppermute | solution.py:616
  115.4 11.5 %shard_map.55 = (f32[8,32,128]{2,1,0:T(8,128)}, f32[8,32,128]{2,1,0:T(8,128)}) custom-call(f32[4,67,8,128]{3,2,1,0:T(8,128)S(1)} %all_to_all.17.gathered, f32[4,67,8,128]{3,2,1,0:T(8,128)S(1)} %collective-permute-done.6.other, f32[12,24,128]{2,1,0:T(8,128)S(1)} %get-tuple-element.30.pair, f32[12,24,128]{2,1,0:T(8,128)S(1)} %get-tuple-element.31.k1, ...), custom_call_target="tpu_custom_call" | custom-call | tf_op jit(solution)/shard_map/pallas_call | solution.py:563
  (1 shorter events, 0.0 us)
Async XLA Ops:
  1.7 10.0 %collective-permute-start.1 = (f32[3,8,32,128]{3,2,1,0:T(8,128)S(1)}, f32[3,8,32,128]{3,2,1,0:T(8,128)S(1)}, u32[]{:S(2)}, u32[]{:S(2)}) collective-permute-start(f32[3,8,32,128]{3,2,1,0:T(8,128)S(1)} %pad_maximum_fusion.mine), channel_id=1, source_target_pairs={{1,2},{2,1},{3,4},{4,3},{5,6},{6,5},{7,8},{8,7},{9,10},{10,9},{11,... | collective-permute-start | bytes 1179656 | tf_op jit(solution)/shard_map/ppermute | solution.py:603
  6.3 6.2 %collective-permute-start = (f32[3,8,32,128]{3,2,1,0:T(8,128)S(1)}, f32[3,8,32,128]{3,2,1,0:T(8,128)S(1)}, u32[]{:S(2)}, u32[]{:S(2)}) collective-permute-start(f32[3,8,32,128]{3,2,1,0:T(8,128)S(1)} %pad_maximum_fusion.mine), channel_id=1, source_target_pairs={{0,1},{1,0},{2,3},{3,2},{4,5},{5,4},{6,7},{7,6},{8,9},{9,8},{10,11... | collective-permute-start | bytes 1179656 | tf_op jit(solution)/shard_map/ppermute | solution.py:604
  12.6 8.3 %collective-permute-start.2 = (f32[66,8,128]{2,1,0:T(8,128)S(1)}, f32[66,8,128]{2,1,0:T(8,128)S(1)}, u32[]{:S(2)}, u32[]{:S(2)}) collective-permute-start(f32[66,8,128]{2,1,0:T(8,128)S(1)} %get-tuple-element.20), channel_id=1, source_target_pairs={{0,16},{16,32},{32,48},{48,64},{64,80},{80,96},{96,112},{1,17},{17... | collective-permute-start | bytes 811016 | tf_op jit(solution)/shard_map/ppermute | solution.py:598
  15.8 9.5 %collective-permute-start.3 = (f32[66,8,128]{2,1,0:T(8,128)S(1)}, f32[66,8,128]{2,1,0:T(8,128)S(1)}, u32[]{:S(2)}, u32[]{:S(2)}) collective-permute-start(f32[66,8,128]{2,1,0:T(8,128)S(1)} %get-tuple-element.21), channel_id=1, source_target_pairs={{16,0},{32,16},{48,32},{64,48},{80,64},{96,80},{112,96},{17,1},{33... | collective-permute-start | bytes 811016 | tf_op jit(solution)/shard_map/ppermute | solution.py:598
  26.2 5.9 %collective-permute-start.4 = (f32[27,8,128]{2,1,0:T(8,128)S(1)}, f32[27,8,128]{2,1,0:T(8,128)S(1)}, u32[]{:S(2)}, u32[]{:S(2)}) collective-permute-start(f32[27,8,128]{2,1,0:T(8,128)S(1)} %get-tuple-element.23), channel_id=1, source_target_pairs={{0,128},{128,256},{256,384},{1,129},{129,257},{257,385},{2,130},{1... | collective-permute-start | bytes 331784 | tf_op jit(solution)/shard_map/ppermute | solution.py:598
  29.4 6.8 %collective-permute-start.5 = (f32[27,8,128]{2,1,0:T(8,128)S(1)}, f32[27,8,128]{2,1,0:T(8,128)S(1)}, u32[]{:S(2)}, u32[]{:S(2)}) collective-permute-start(f32[27,8,128]{2,1,0:T(8,128)S(1)} %get-tuple-element.24), channel_id=1, source_target_pairs={{128,0},{256,128},{384,256},{129,1},{257,129},{385,257},{130,2},{2... | collective-permute-start | bytes 331784 | tf_op jit(solution)/shard_map/ppermute | solution.py:598
  109.6 5.8 %collective-permute-start.6 = (f32[4,67,8,128]{3,2,1,0:T(8,128)S(1)}, f32[4,67,8,128]{3,2,1,0:T(8,128)S(1)}, u32[]{:S(2)}, u32[]{:S(2)}) collective-permute-start(f32[4,67,8,128]{3,2,1,0:T(8,128)S(1)} %all_to_all.17.gathered), channel_id=1, source_target_pairs={{0,1},{1,0},{2,3},{3,2},{4,5},{5,4},{6,7},{7,6},{8,9},{9,8},{10,11... | collective-permute-start | bytes 3293192 | tf_op jit(solution)/shard_map/ppermute | solution.py:616

commit v6 on v5

--- a/solution.py
+++ b/solution.py
@@ -17,6 +17,8 @@
 GAIN = 2.0 * RHO_NEXT / DELTA
 
 INNER = 16
+SWEEP = 8
+SWEEP_UP = 16
 OUTER = 16
 F32 = jnp.float32
 BF16 = jnp.bfloat16
@@ -115,8 +117,9 @@
             for s in range(16):
                 j = packed * 16 + s
                 tile = window[8 * i + j // 6, j % 6]
-                left = jnp.where(slot == s, shift(tile, 8 * s, 1), left)
-                right = jnp.where(slot == s, shift(tile, 8 * s + 8, 1), right)
+                rolled = shift(tile, 8 * s, 1)
+                left = jnp.where(slot == s, rolled, left)
+                right = jnp.where(slot == (s - 1) % 16, rolled, right)
             to_left[3 * i + packed] = left
             to_right[3 * i + packed] = right
         return carry
@@ -130,6 +133,10 @@
 
 def put(ref, z, value):
     ref[pl.ds(6 * z, 6)] = value.reshape(6, 8, 256)
+
+
+def put_own(ref, z, value):
+    ref[pl.ds(6 * z + 1, 4), :, :128] = value[8:40, :128].reshape(4, 8, 128)
 
 
 def inner_flux(v, wx, wy):
@@ -138,7 +145,7 @@
     return (fx - behind(fx, 1)) + (fy - behind(fy, 0))
 
 
-def sweep(first, last, source, wx, wy, wz, step):
+def sweep(first, last, source, wx, wy, wz, step, unroll):
     v = plane(source, first)
     carry = (v, plane(wz, first - 1) * (v - plane(source, first - 1)))
 
@@ -149,7 +156,7 @@
         step(z, v, inner_flux(v, plane(wx, z), plane(wy, z)) + (above - below))
         return (after, above)
 
-    loop(first, last + 1, body, carry)
+    loop(first, last + 1, body, carry, unroll)
 
 
 def zpair(low_face):
@@ -183,6 +190,8 @@
     kappa, guess, rest, update, second, sums_a, sums_b, line,
 ):
     lane = iota((8, 128), 1)
+    slot_of = lax.shift_right_logical(lane, 3)
+    beside = (lane < 8) | (lane >= 120)
 
     def unpack(i, dest, base):
         for packed in range(3):
@@ -190,8 +199,7 @@
             lo = from_left[base * 9 + 3 * i + packed]
             for s in range(16):
                 j = packed * 16 + s
-                edge = jnp.where(lane < 8, shift(hi, -8 * s, 1), 0.0)
-                edge = jnp.where(lane >= 120, shift(lo, 120 - 8 * s, 1), edge)
+                edge = jnp.where(beside, shift(jnp.where(slot_of == s, hi, lo), -8 * s, 1), 0.0)
                 dest[48 * i + j, :, 0:128] = window[base * 24 + 8 * i + j // 6, j % 6]
                 dest[48 * i + j, :, 128:256] = edge
 
@@ -220,14 +228,14 @@
     half1 = 0.5 * plane(kappa, 1)
     half2 = 0.5 * plane(kappa, 2)
     put(wz, 1, half1 + half2)
-    loop(2, 22, weights, (half2, half1 + half2))
+    loop(2, 22, weights, (half2, half1 + half2), SWEEP)
 
     def first(z, v, minus):
         r = plane(right, z) + minus
         put(rest, z, r)
         put(update, z, FIRST * r * plane(inverse, z))
 
-    sweep(2, 21, guess, wx, wy, wz, first)
+    sweep(2, 21, guess, wx, wy, wz, first, SWEEP)
 
     def next_step(z, v, minus):
         r = plane(rest, z) + minus
@@ -236,12 +244,12 @@
         put(second, z, d)
         put(iterate, z, plane(guess, z) + v + d)
 
-    sweep(3, 20, update, wx, wy, wz, next_step)
+    sweep(3, 20, update, wx, wy, wz, next_step, SWEEP)
 
     def last(z, v, minus):
         put(rest, z, plane(rest, z) + minus)
 
-    sweep(4, 19, second, wx, wy, wz, last)
+    sweep(4, 19, second, wx, wy, wz, last, SWEEP)
 
     def add_pairs(ref, start, count, at):
         def body(m, carry):
@@ -541,22 +549,22 @@
         put(rest, z, r)
         put(update, z, FIRST * r * plane(inverse, z))
 
-    sweep(5, 18, current, wx, wy, wz, first)
+    sweep(5, 18, current, wx, wy, wz, first, SWEEP_UP)
 
     def next_step(z, v, minus):
         r = plane(rest, z) + minus
         d = KEEP * v + GAIN * (r * plane(inverse, z))
-        put(rest, z, r)
         put(second, z, d)
-        put(current, z, plane(current, z) + v + d)
-
-    sweep(6, 17, update, wx, wy, wz, next_step)
+        put_own(rest, z, r)
+        put_own(current, z, plane(current, z) + v + d)
+
+    sweep(6, 17, update, wx, wy, wz, next_step, SWEEP_UP)
 
     def last(z, v, minus):
         residual_out[z - 8] = (plane(rest, z) + minus)[8:40, :128]
         solution_out[z - 8] = plane(current, z)[8:40, :128]
 
-    sweep(8, 15, second, wx, wy, wz, last)
+    sweep(8, 15, second, wx, wy, wz, last, SWEEP_UP)
 
 
 def run(kernel, outs, scratch, *args):

time: 127 us -> 126 us (level)
  no operation moved by 1% of the time
where the time goes in v6:
time: 126 us
  blocking collectives  65.9 us (52%)
  starting transfers between devices  21.9 us (17%)
  Pallas kernels  18.8 us (15%)
  waiting for transfers between devices  17.4 us (14%)
    all_to_all x1, blocking collectives, local(): lax.all_to_all(share, 'gy', 0, 0)  25.2 us
    all_to_all x1, blocking collectives, local(): lax.all_to_all(share, 'gz', 0, 0)  22.2 us
    pallas_call x6, Pallas kernels, run(): pl.pallas_call(kernel, out_shape=[jax.ShapeDtypeStruct(shape, F32) for sh...  18.8 us
    all_to_all x1, blocking collectives, local(): whole = lax.all_to_all(share, 'gx', 0, 0)  18.5 us
    ppermute x2, waiting for transfers between devices, both_ways(): lax.ppermute(to_low, axis, down(axis))  8.49 us
    ppermute x2, starting transfers between devices, both_ways(): lax.ppermute(to_high, axis, up(axis))  6.37 us
    ppermute x2, waiting for transfers between devices, both_ways(): lax.ppermute(to_high, axis, up(axis))  5.22 us
    ppermute x1, starting transfers between devices, local(): chip = lax.ppermute(mine, 'gz', [(i, i ^ 1) for i in range(16)])  4.88 us
  transfers between devices with their start and end apart: 7, of which 7 were waited for; matrix products, arithmetic and copies ran while one was open for 0% of the time, Pallas kernels for 0%

profile of v6, /device:TPU:1, one launch (start us, length us, event | category | flops | bytes accessed | tf_op | source)
XLA Modules:
  0.0 125.8 jit_solution(5484184669237926973)
XLA Ops:
  0.6 1.1 pad_maximum_fusion.mine
  1.7 4.6 %collective-permute-start.1 = (f32[3,8,32,128]{3,2,1,0:T(8,128)S(1)}, f32[3,8,32,128]{3,2,1,0:T(8,128)S(1)}, u32[]{:S(2)}, u32[]{:S(2)}) collective-permute-start(f32[3,8,32,128]{3,2,1,0:T(8,128)S(1)} %pad_maximum_fusion.mine), channel_id=1, source_target_pairs={{1,2},{2,1},{3,4},{4,3},{5,6},{6,5},{7,8},{8,7},{9,10},{10,9},{11,... | collective-permute-start | bytes 1179656 | tf_op jit(solution)/shard_map/ppermute | solution.py:611
  6.3 4.9 %collective-permute-start = (f32[3,8,32,128]{3,2,1,0:T(8,128)S(1)}, f32[3,8,32,128]{3,2,1,0:T(8,128)S(1)}, u32[]{:S(2)}, u32[]{:S(2)}) collective-permute-start(f32[3,8,32,128]{3,2,1,0:T(8,128)S(1)} %pad_maximum_fusion.mine), channel_id=1, source_target_pairs={{0,1},{1,0},{2,3},{3,2},{4,5},{5,4},{6,7},{7,6},{8,9},{9,8},{10,11... | collective-permute-start | bytes 1179656 | tf_op jit(solution)/shard_map/ppermute | solution.py:612
  11.2 0.6 collective-permute-done.1.beside
  11.7 0.8 collective-permute-done.chip
  12.6 3.2 %collective-permute-start.2 = (f32[66,8,128]{2,1,0:T(8,128)S(1)}, f32[66,8,128]{2,1,0:T(8,128)S(1)}, u32[]{:S(2)}, u32[]{:S(2)}) collective-permute-start(f32[66,8,128]{2,1,0:T(8,128)S(1)} %get-tuple-element.20), channel_id=1, source_target_pairs={{0,16},{16,32},{32,48},{48,64},{64,80},{80,96},{96,112},{1,17},{17... | collective-permute-start | bytes 811016 | tf_op jit(solution)/shard_map/ppermute | solution.py:606
  15.8 1.3 %collective-permute-start.3 = (f32[66,8,128]{2,1,0:T(8,128)S(1)}, f32[66,8,128]{2,1,0:T(8,128)S(1)}, u32[]{:S(2)}, u32[]{:S(2)}) collective-permute-start(f32[66,8,128]{2,1,0:T(8,128)S(1)} %get-tuple-element.21), channel_id=1, source_target_pairs={{16,0},{32,16},{48,32},{64,48},{80,64},{96,80},{112,96},{17,1},{33... | collective-permute-start | bytes 811016 | tf_op jit(solution)/shard_map/ppermute | solution.py:606
  17.1 3.7 %collective-permute-done.2.ylow = f32[66,8,128]{2,1,0:T(8,128)S(1)} collective-permute-done((f32[66,8,128]{2,1,0:T(8,128)S(1)}, f32[66,8,128]{2,1,0:T(8,128)S(1)}, u32[]{:S(2)}, u32[]{:S(2)}) %collective-permute-start.2) | collective-permute-done | bytes 270368 | tf_op jit(solution)/shard_map/ppermute | solution.py:606
  20.8 4.5 %collective-permute-done.3.yhigh = f32[66,8,128]{2,1,0:T(8,128)S(1)} collective-permute-done((f32[66,8,128]{2,1,0:T(8,128)S(1)}, f32[66,8,128]{2,1,0:T(8,128)S(1)}, u32[]{:S(2)}, u32[]{:S(2)}) %collective-permute-start.3) | collective-permute-done | bytes 270368 | tf_op jit(solution)/shard_map/ppermute | solution.py:606
  25.3 0.5 shard_map.51
  25.8 3.1 %collective-permute-start.4 = (f32[27,8,128]{2,1,0:T(8,128)S(1)}, f32[27,8,128]{2,1,0:T(8,128)S(1)}, u32[]{:S(2)}, u32[]{:S(2)}) collective-permute-start(f32[27,8,128]{2,1,0:T(8,128)S(1)} %get-tuple-element.23), channel_id=1, source_target_pairs={{0,128},{128,256},{256,384},{1,129},{129,257},{257,385},{2,130},{1... | collective-permute-start | bytes 331784 | tf_op jit(solution)/shard_map/ppermute | solution.py:606
  28.9 1.3 %collective-permute-start.5 = (f32[27,8,128]{2,1,0:T(8,128)S(1)}, f32[27,8,128]{2,1,0:T(8,128)S(1)}, u32[]{:S(2)}, u32[]{:S(2)}) collective-permute-start(f32[27,8,128]{2,1,0:T(8,128)S(1)} %get-tuple-element.24), channel_id=1, source_target_pairs={{128,0},{256,128},{384,256},{129,1},{257,129},{385,257},{130,2},{2... | collective-permute-start | bytes 331784 | tf_op jit(solution)/shard_map/ppermute | solution.py:606
  30.2 1.5 %collective-permute-done.4.from_left = f32[27,8,128]{2,1,0:T(8,128)S(1)} collective-permute-done((f32[27,8,128]{2,1,0:T(8,128)S(1)}, f32[27,8,128]{2,1,0:T(8,128)S(1)}, u32[]{:S(2)}, u32[]{:S(2)}) %collective-permute-start.4) | collective-permute-done | bytes 110624 | tf_op jit(solution)/shard_map/ppermute | solution.py:606
  31.7 4.0 %collective-permute-done.5.from_right = f32[27,8,128]{2,1,0:T(8,128)S(1)} collective-permute-done((f32[27,8,128]{2,1,0:T(8,128)S(1)}, f32[27,8,128]{2,1,0:T(8,128)S(1)}, u32[]{:S(2)}, u32[]{:S(2)}) %collective-permute-start.5) | collective-permute-done | bytes 110624 | tf_op jit(solution)/shard_map/ppermute | solution.py:606
  35.8 6.4 %shard_map.52 = (f32[16,5,8,128]{3,2,1,0:T(8,128)S(1)}, f32[12,24,128]{2,1,0:T(8,128)S(1)}, f32[12,24,128]{2,1,0:T(8,128)S(1)}, f32[144,8,256]{2,1,0:T(8,128)S(1...) custom-call(f32[72,6,8,128]{3,2,1,0:T(8,128)S(1)} %get-tuple-element, ...), custom_call_target="tpu_custom_call" | custom-call | tf_op jit(solution)/shard_map/pallas_call | solution.py:571
  42.2 22.2 %all_to_all.15.gathered = f32[16,5,8,128]{3,2,1,0:T(8,128)S(1)} all-to-all(f32[16,5,8,128]{3,2,1,0:T(8,128)S(1)} %get-tuple-element.25), channel_id=1, replica_groups=mesh['gx'=4,'gy'=8,'gz'=16] {'gz'}, dimensions={0} | all-to-all | bytes 655360 | tf_op jit(solution)/shard_map/all_to_all | solution.py:621
  64.4 0.1 shard_map.53
  64.5 25.2 %all_to_all.16.gathered = f32[8,14,8,128]{3,2,1,0:T(8,128)S(1)} all-to-all(f32[8,14,8,128]{3,2,1,0:T(8,128)S(1)} %get-tuple-element.27), channel_id=1, replica_groups=mesh['gx'=4,'gy'=8,'gz'=16] {'gy'}, dimensions={0} | all-to-all | bytes 917504 | tf_op jit(solution)/shard_map/all_to_all | solution.py:622
  89.7 0.2 shard_map.54
  89.9 18.5 %all_to_all.17.gathered = f32[4,67,8,128]{3,2,1,0:T(8,128)S(1)} all-to-all(f32[4,67,8,128]{3,2,1,0:T(8,128)S(1)} %get-tuple-element.29), channel_id=1, replica_groups=mesh['gx'=4,'gy'=8,'gz'=16] {'gx'}, dimensions={0} | all-to-all | bytes 2195456 | tf_op jit(solution)/shard_map/all_to_all | solution.py:623
  108.5 3.5 %collective-permute-start.6 = (f32[4,67,8,128]{3,2,1,0:T(8,128)S(1)}, f32[4,67,8,128]{3,2,1,0:T(8,128)S(1)}, u32[]{:S(2)}, u32[]{:S(2)}) collective-permute-start(f32[4,67,8,128]{3,2,1,0:T(8,128)S(1)} %all_to_all.17.gathered), channel_id=1, source_target_pairs={{0,1},{1,0},{2,3},{3,2},{4,5},{5,4},{6,7},{7,6},{8,9},{9,8},{10,11... | collective-permute-start | bytes 3293192 | tf_op jit(solution)/shard_map/ppermute | solution.py:624
  111.9 2.3 %collective-permute-done.6.other = f32[4,67,8,128]{3,2,1,0:T(8,128)S(1)} collective-permute-done((f32[4,67,8,128]{3,2,1,0:T(8,128)S(1)}, f32[4,67,8,128]{3,2,1,0:T(8,128)S(1)}, u32[]{:S(2)}, u32[]{:S(2)}) %collective-permute-start.6) | collective-permute-done | bytes 1097760 | tf_op jit(solution)/shard_map/ppermute | solution.py:624
  114.3 11.5 %shard_map.55 = (f32[8,32,128]{2,1,0:T(8,128)}, f32[8,32,128]{2,1,0:T(8,128)}) custom-call(f32[4,67,8,128]{3,2,1,0:T(8,128)S(1)} %all_to_all.17.gathered, f32[4,67,8,128]{3,2,1,0:T(8,128)S(1)} %collective-permute-done.6.other, f32[12,24,128]{2,1,0:T(8,128)S(1)} %get-tuple-element.30.pair, f32[12,24,128]{2,1,0:T(8,128)S(1)} %get-tuple-element.31.k1, ...), custom_call_target="tpu_custom_call" | custom-call | tf_op jit(solution)/shard_map/pallas_call | solution.py:571
  (1 shorter events, 0.0 us)
Async XLA Ops:
  1.7 10.0 %collective-permute-start.1 = (f32[3,8,32,128]{3,2,1,0:T(8,128)S(1)}, f32[3,8,32,128]{3,2,1,0:T(8,128)S(1)}, u32[]{:S(2)}, u32[]{:S(2)}) collective-permute-start(f32[3,8,32,128]{3,2,1,0:T(8,128)S(1)} %pad_maximum_fusion.mine), channel_id=1, source_target_pairs={{1,2},{2,1},{3,4},{4,3},{5,6},{6,5},{7,8},{8,7},{9,10},{10,9},{11,... | collective-permute-start | bytes 1179656 | tf_op jit(solution)/shard_map/ppermute | solution.py:611
  6.3 6.2 %collective-permute-start = (f32[3,8,32,128]{3,2,1,0:T(8,128)S(1)}, f32[3,8,32,128]{3,2,1,0:T(8,128)S(1)}, u32[]{:S(2)}, u32[]{:S(2)}) collective-permute-start(f32[3,8,32,128]{3,2,1,0:T(8,128)S(1)} %pad_maximum_fusion.mine), channel_id=1, source_target_pairs={{0,1},{1,0},{2,3},{3,2},{4,5},{5,4},{6,7},{7,6},{8,9},{9,8},{10,11... | collective-permute-start | bytes 1179656 | tf_op jit(solution)/shard_map/ppermute | solution.py:612
  12.6 8.3 %collective-permute-start.2 = (f32[66,8,128]{2,1,0:T(8,128)S(1)}, f32[66,8,128]{2,1,0:T(8,128)S(1)}, u32[]{:S(2)}, u32[]{:S(2)}) collective-permute-start(f32[66,8,128]{2,1,0:T(8,128)S(1)} %get-tuple-element.20), channel_id=1, source_target_pairs={{0,16},{16,32},{32,48},{48,64},{64,80},{80,96},{96,112},{1,17},{17... | collective-permute-start | bytes 811016 | tf_op jit(solution)/shard_map/ppermute | solution.py:606
  15.8 9.5 %collective-permute-start.3 = (f32[66,8,128]{2,1,0:T(8,128)S(1)}, f32[66,8,128]{2,1,0:T(8,128)S(1)}, u32[]{:S(2)}, u32[]{:S(2)}) collective-permute-start(f32[66,8,128]{2,1,0:T(8,128)S(1)} %get-tuple-element.21), channel_id=1, source_target_pairs={{16,0},{32,16},{48,32},{64,48},{80,64},{96,80},{112,96},{17,1},{33... | collective-permute-start | bytes 811016 | tf_op jit(solution)/shard_map/ppermute | solution.py:606
  25.8 5.9 %collective-permute-start.4 = (f32[27,8,128]{2,1,0:T(8,128)S(1)}, f32[27,8,128]{2,1,0:T(8,128)S(1)}, u32[]{:S(2)}, u32[]{:S(2)}) collective-permute-start(f32[27,8,128]{2,1,0:T(8,128)S(1)} %get-tuple-element.23), channel_id=1, source_target_pairs={{0,128},{128,256},{256,384},{1,129},{129,257},{257,385},{2,130},{1... | collective-permute-start | bytes 331784 | tf_op jit(solution)/shard_map/ppermute | solution.py:606
  28.9 6.8 %collective-permute-start.5 = (f32[27,8,128]{2,1,0:T(8,128)S(1)}, f32[27,8,128]{2,1,0:T(8,128)S(1)}, u32[]{:S(2)}, u32[]{:S(2)}) collective-permute-start(f32[27,8,128]{2,1,0:T(8,128)S(1)} %get-tuple-element.24), channel_id=1, source_target_pairs={{128,0},{256,128},{384,256},{129,1},{257,129},{385,257},{130,2},{2... | collective-permute-start | bytes 331784 | tf_op jit(solution)/shard_map/ppermute | solution.py:606
  108.5 5.8 %collective-permute-start.6 = (f32[4,67,8,128]{3,2,1,0:T(8,128)S(1)}, f32[4,67,8,128]{3,2,1,0:T(8,128)S(1)}, u32[]{:S(2)}, u32[]{:S(2)}) collective-permute-start(f32[4,67,8,128]{3,2,1,0:T(8,128)S(1)} %all_to_all.17.gathered), channel_id=1, source_target_pairs={{0,1},{1,0},{2,3},{3,2},{4,5},{5,4},{6,7},{7,6},{8,9},{9,8},{10,11... | collective-permute-start | bytes 3293192 | tf_op jit(solution)/shard_map/ppermute | solution.py:624

commit v7 on v6

--- a/solution.py
+++ b/solution.py
@@ -103,7 +103,7 @@
         to_high[i] = window_rows(mine, chip, beside, a, z, slice(24, 32))
 
 
-def xpack_kernel(mine, chip, beside, ylow, yhigh, window, to_right, to_left):
+def xpack_kernel(mine, chip, beside, yhigh, ylow, window, to_right, to_left):
     for i, (a, z) in enumerate(TRAVEL):
         window[24 * a + z, 0] = ylow[i]
         window[24 * a + z, 1:5] = window_rows(mine, chip, beside, a, z, slice(0, 32)).reshape(4, 8, 128)
@@ -185,7 +185,7 @@
 
 
 def down_kernel(
-    window, from_left, from_right,
+    window, from_right, from_left,
     share, pair_out, k1_out, iterate, right, wx, wy, wz, inverse,
     kappa, guess, rest, update, second, sums_a, sums_b, line,
 ):
@@ -613,11 +613,11 @@
     to_high, to_low = run(ypack_kernel, *YPACK, mine, chip, beside)
     ylow, yhigh = both_ways(to_low, to_high, "gy")
     window, to_right, to_left = run(
-        xpack_kernel, *XPACK, mine, chip, beside, ylow, yhigh
+        xpack_kernel, *XPACK, mine, chip, beside, yhigh, ylow
     )
     from_left, from_right = both_ways(to_left, to_right, "gx")
 
-    share, pair, k1, *arrays = run(down_kernel, *DOWN, window, from_left, from_right)
+    share, pair, k1, *arrays = run(down_kernel, *DOWN, window, from_right, from_left)
     share, pair = run(turn_kernel, *TURN, lax.all_to_all(share, "gz", 0, 0), pair)
     share, pair = run(cross_kernel, *CROSS, lax.all_to_all(share, "gy", 0, 0), pair)
     whole = lax.all_to_all(share, "gx", 0, 0)

time: 126 us -> 125 us (level)
  waiting for transfers between devices: 17.4 us -> 10.5 us
  blocking collectives: 65.9 us -> 70.2 us
  starting transfers between devices: 21.9 us -> 23.5 us
    ppermute x2, waiting for transfers between devices: 8.49 us -> 4.47 us  [both_ways(): lax.ppermute(to_low, axis, down(axis))]
    ppermute x2, waiting for transfers between devices: 5.22 us -> 2.4 us  [both_ways(): lax.ppermute(to_high, axis, up(axis))]
    all_to_all x1, blocking collectives: 25.2 us -> 27.7 us  [local(): lax.all_to_all(share, 'gy', 0, 0)]
    ppermute x2, starting transfers between devices: 6.37 us -> 8 us  [both_ways(): lax.ppermute(to_high, axis, up(axis))]
where the time goes in v7:
time: 125 us
  blocking collectives  70.2 us (56%)
  starting transfers between devices  23.5 us (19%)
  Pallas kernels  18.8 us (15%)
  waiting for transfers between devices  10.5 us (8%)
    all_to_all x1, blocking collectives, local(): lax.all_to_all(share, 'gy', 0, 0)  27.7 us
    all_to_all x1, blocking collectives, local(): lax.all_to_all(share, 'gz', 0, 0)  22.7 us
    all_to_all x1, blocking collectives, local(): whole = lax.all_to_all(share, 'gx', 0, 0)  19.8 us
    pallas_call x6, Pallas kernels, run(): pl.pallas_call(kernel, out_shape=[jax.ShapeDtypeStruct(shape, F32) for sh...  18.8 us
    ppermute x2, starting transfers between devices, both_ways(): lax.ppermute(to_high, axis, up(axis))  8 us
    ppermute x1, starting transfers between devices, local(): chip = lax.ppermute(mine, 'gz', [(i, i ^ 1) for i in range(16)])  4.88 us
    ppermute x1, starting transfers between devices, local(): lax.ppermute(mine, 'gz', [(i, (i + 1 ^ 1) - 1) for i in range(1, 15)])  4.59 us
    ppermute x2, waiting for transfers between devices, both_ways(): lax.ppermute(to_low, axis, down(axis))  4.47 us
  transfers between devices with their start and end apart: 7, of which 7 were waited for; matrix products, arithmetic and copies ran while one was open for 0% of the time, Pallas kernels for 0%

profile of v7, /device:TPU:1, one launch (start us, length us, event | category | flops | bytes accessed | tf_op | source)
XLA Modules:
  0.0 124.9 jit_solution(18061314721845451699)
XLA Ops:
  0.6 1.1 pad_maximum_fusion.mine
  1.7 4.6 %collective-permute-start.1 = (f32[3,8,32,128]{3,2,1,0:T(8,128)S(1)}, f32[3,8,32,128]{3,2,1,0:T(8,128)S(1)}, u32[]{:S(2)}, u32[]{:S(2)}) collective-permute-start(f32[3,8,32,128]{3,2,1,0:T(8,128)S(1)} %pad_maximum_fusion.mine), channel_id=1, source_target_pairs={{1,2},{2,1},{3,4},{4,3},{5,6},{6,5},{7,8},{8,7},{9,10},{10,9},{11,... | collective-permute-start | bytes 1179656 | tf_op jit(solution)/shard_map/ppermute | solution.py:611
  6.3 4.9 %collective-permute-start = (f32[3,8,32,128]{3,2,1,0:T(8,128)S(1)}, f32[3,8,32,128]{3,2,1,0:T(8,128)S(1)}, u32[]{:S(2)}, u32[]{:S(2)}) collective-permute-start(f32[3,8,32,128]{3,2,1,0:T(8,128)S(1)} %pad_maximum_fusion.mine), channel_id=1, source_target_pairs={{0,1},{1,0},{2,3},{3,2},{4,5},{5,4},{6,7},{7,6},{8,9},{9,8},{10,11... | collective-permute-start | bytes 1179656 | tf_op jit(solution)/shard_map/ppermute | solution.py:612
  11.2 0.6 collective-permute-done.1.beside
  11.7 0.8 collective-permute-done.chip
  12.6 1.3 %collective-permute-start.2 = (f32[66,8,128]{2,1,0:T(8,128)S(1)}, f32[66,8,128]{2,1,0:T(8,128)S(1)}, u32[]{:S(2)}, u32[]{:S(2)}) collective-permute-start(f32[66,8,128]{2,1,0:T(8,128)S(1)} %get-tuple-element.20), channel_id=1, source_target_pairs={{16,0},{32,16},{48,32},{64,48},{80,64},{96,80},{112,96},{17,1},{33... | collective-permute-start | bytes 811016 | tf_op jit(solution)/shard_map/ppermute | solution.py:606
  13.9 4.0 %collective-permute-start.3 = (f32[66,8,128]{2,1,0:T(8,128)S(1)}, f32[66,8,128]{2,1,0:T(8,128)S(1)}, u32[]{:S(2)}, u32[]{:S(2)}) collective-permute-start(f32[66,8,128]{2,1,0:T(8,128)S(1)} %get-tuple-element.21), channel_id=1, source_target_pairs={{0,16},{16,32},{32,48},{48,64},{64,80},{80,96},{96,112},{1,17},{17... | collective-permute-start | bytes 811016 | tf_op jit(solution)/shard_map/ppermute | solution.py:606
  17.9 4.3 %collective-permute-done.2.yhigh = f32[66,8,128]{2,1,0:T(8,128)S(1)} collective-permute-done((f32[66,8,128]{2,1,0:T(8,128)S(1)}, f32[66,8,128]{2,1,0:T(8,128)S(1)}, u32[]{:S(2)}, u32[]{:S(2)}) %collective-permute-start.2) | collective-permute-done | bytes 270368 | tf_op jit(solution)/shard_map/ppermute | solution.py:606
  22.1 0.9 collective-permute-done.3.ylow
  23.0 0.5 shard_map.51
  23.5 1.3 %collective-permute-start.4 = (f32[27,8,128]{2,1,0:T(8,128)S(1)}, f32[27,8,128]{2,1,0:T(8,128)S(1)}, u32[]{:S(2)}, u32[]{:S(2)}) collective-permute-start(f32[27,8,128]{2,1,0:T(8,128)S(1)} %get-tuple-element.23), channel_id=1, source_target_pairs={{128,0},{256,128},{384,256},{129,1},{257,129},{385,257},{130,2},{2... | collective-permute-start | bytes 331784 | tf_op jit(solution)/shard_map/ppermute | solution.py:606
  24.8 4.0 %collective-permute-start.5 = (f32[27,8,128]{2,1,0:T(8,128)S(1)}, f32[27,8,128]{2,1,0:T(8,128)S(1)}, u32[]{:S(2)}, u32[]{:S(2)}) collective-permute-start(f32[27,8,128]{2,1,0:T(8,128)S(1)} %get-tuple-element.24), channel_id=1, source_target_pairs={{0,128},{128,256},{256,384},{1,129},{129,257},{257,385},{2,130},{1... | collective-permute-start | bytes 331784 | tf_op jit(solution)/shard_map/ppermute | solution.py:606
  28.8 0.2 collective-permute-done.4.from_right
  29.0 1.5 %collective-permute-done.5.from_left = f32[27,8,128]{2,1,0:T(8,128)S(1)} collective-permute-done((f32[27,8,128]{2,1,0:T(8,128)S(1)}, f32[27,8,128]{2,1,0:T(8,128)S(1)}, u32[]{:S(2)}, u32[]{:S(2)}) %collective-permute-start.5) | collective-permute-done | bytes 110624 | tf_op jit(solution)/shard_map/ppermute | solution.py:606
  30.5 6.4 %shard_map.52 = (f32[16,5,8,128]{3,2,1,0:T(8,128)S(1)}, f32[12,24,128]{2,1,0:T(8,128)S(1)}, f32[12,24,128]{2,1,0:T(8,128)S(1)}, f32[144,8,256]{2,1,0:T(8,128)S(1...) custom-call(f32[72,6,8,128]{3,2,1,0:T(8,128)S(1)} %get-tuple-element, ...), custom_call_target="tpu_custom_call" | custom-call | tf_op jit(solution)/shard_map/pallas_call | solution.py:571
  37.0 22.7 %all_to_all.15.gathered = f32[16,5,8,128]{3,2,1,0:T(8,128)S(1)} all-to-all(f32[16,5,8,128]{3,2,1,0:T(8,128)S(1)} %get-tuple-element.25), channel_id=1, replica_groups=mesh['gx'=4,'gy'=8,'gz'=16] {'gz'}, dimensions={0} | all-to-all | bytes 655360 | tf_op jit(solution)/shard_map/all_to_all | solution.py:621
  59.7 0.1 shard_map.53
  59.8 27.7 %all_to_all.16.gathered = f32[8,14,8,128]{3,2,1,0:T(8,128)S(1)} all-to-all(f32[8,14,8,128]{3,2,1,0:T(8,128)S(1)} %get-tuple-element.27), channel_id=1, replica_groups=mesh['gx'=4,'gy'=8,'gz'=16] {'gy'}, dimensions={0} | all-to-all | bytes 917504 | tf_op jit(solution)/shard_map/all_to_all | solution.py:622
  87.6 0.2 shard_map.54
  87.8 19.8 %all_to_all.17.gathered = f32[4,67,8,128]{3,2,1,0:T(8,128)S(1)} all-to-all(f32[4,67,8,128]{3,2,1,0:T(8,128)S(1)} %get-tuple-element.29), channel_id=1, replica_groups=mesh['gx'=4,'gy'=8,'gz'=16] {'gx'}, dimensions={0} | all-to-all | bytes 2195456 | tf_op jit(solution)/shard_map/all_to_all | solution.py:623
  107.6 3.5 %collective-permute-start.6 = (f32[4,67,8,128]{3,2,1,0:T(8,128)S(1)}, f32[4,67,8,128]{3,2,1,0:T(8,128)S(1)}, u32[]{:S(2)}, u32[]{:S(2)}) collective-permute-start(f32[4,67,8,128]{3,2,1,0:T(8,128)S(1)} %all_to_all.17.gathered), channel_id=1, source_target_pairs={{0,1},{1,0},{2,3},{3,2},{4,5},{5,4},{6,7},{7,6},{8,9},{9,8},{10,11... | collective-permute-start | bytes 3293192 | tf_op jit(solution)/shard_map/ppermute | solution.py:624
  111.0 2.3 %collective-permute-done.6.other = f32[4,67,8,128]{3,2,1,0:T(8,128)S(1)} collective-permute-done((f32[4,67,8,128]{3,2,1,0:T(8,128)S(1)}, f32[4,67,8,128]{3,2,1,0:T(8,128)S(1)}, u32[]{:S(2)}, u32[]{:S(2)}) %collective-permute-start.6) | collective-permute-done | bytes 1097760 | tf_op jit(solution)/shard_map/ppermute | solution.py:624
  113.3 11.5 %shard_map.55 = (f32[8,32,128]{2,1,0:T(8,128)}, f32[8,32,128]{2,1,0:T(8,128)}) custom-call(f32[4,67,8,128]{3,2,1,0:T(8,128)S(1)} %all_to_all.17.gathered, f32[4,67,8,128]{3,2,1,0:T(8,128)S(1)} %collective-permute-done.6.other, f32[12,24,128]{2,1,0:T(8,128)S(1)} %get-tuple-element.30.pair, f32[12,24,128]{2,1,0:T(8,128)S(1)} %get-tuple-element.31.k1, ...), custom_call_target="tpu_custom_call" | custom-call | tf_op jit(solution)/shard_map/pallas_call | solution.py:571
  (1 shorter events, 0.0 us)
Async XLA Ops:
  1.7 10.0 %collective-permute-start.1 = (f32[3,8,32,128]{3,2,1,0:T(8,128)S(1)}, f32[3,8,32,128]{3,2,1,0:T(8,128)S(1)}, u32[]{:S(2)}, u32[]{:S(2)}) collective-permute-start(f32[3,8,32,128]{3,2,1,0:T(8,128)S(1)} %pad_maximum_fusion.mine), channel_id=1, source_target_pairs={{1,2},{2,1},{3,4},{4,3},{5,6},{6,5},{7,8},{8,7},{9,10},{10,9},{11,... | collective-permute-start | bytes 1179656 | tf_op jit(solution)/shard_map/ppermute | solution.py:611
  6.3 6.2 %collective-permute-start = (f32[3,8,32,128]{3,2,1,0:T(8,128)S(1)}, f32[3,8,32,128]{3,2,1,0:T(8,128)S(1)}, u32[]{:S(2)}, u32[]{:S(2)}) collective-permute-start(f32[3,8,32,128]{3,2,1,0:T(8,128)S(1)} %pad_maximum_fusion.mine), channel_id=1, source_target_pairs={{0,1},{1,0},{2,3},{3,2},{4,5},{5,4},{6,7},{7,6},{8,9},{9,8},{10,11... | collective-permute-start | bytes 1179656 | tf_op jit(solution)/shard_map/ppermute | solution.py:612
  12.6 9.6 %collective-permute-start.2 = (f32[66,8,128]{2,1,0:T(8,128)S(1)}, f32[66,8,128]{2,1,0:T(8,128)S(1)}, u32[]{:S(2)}, u32[]{:S(2)}) collective-permute-start(f32[66,8,128]{2,1,0:T(8,128)S(1)} %get-tuple-element.20), channel_id=1, source_target_pairs={{16,0},{32,16},{48,32},{64,48},{80,64},{96,80},{112,96},{17,1},{33... | collective-permute-start | bytes 811016 | tf_op jit(solution)/shard_map/ppermute | solution.py:606
  13.9 9.1 %collective-permute-start.3 = (f32[66,8,128]{2,1,0:T(8,128)S(1)}, f32[66,8,128]{2,1,0:T(8,128)S(1)}, u32[]{:S(2)}, u32[]{:S(2)}) collective-permute-start(f32[66,8,128]{2,1,0:T(8,128)S(1)} %get-tuple-element.21), channel_id=1, source_target_pairs={{0,16},{16,32},{32,48},{48,64},{64,80},{80,96},{96,112},{1,17},{17... | collective-permute-start | bytes 811016 | tf_op jit(solution)/shard_map/ppermute | solution.py:606
  23.5 5.5 %collective-permute-start.4 = (f32[27,8,128]{2,1,0:T(8,128)S(1)}, f32[27,8,128]{2,1,0:T(8,128)S(1)}, u32[]{:S(2)}, u32[]{:S(2)}) collective-permute-start(f32[27,8,128]{2,1,0:T(8,128)S(1)} %get-tuple-element.23), channel_id=1, source_target_pairs={{128,0},{256,128},{384,256},{129,1},{257,129},{385,257},{130,2},{2... | collective-permute-start | bytes 331784 | tf_op jit(solution)/shard_map/ppermute | solution.py:606
  24.8 5.7 %collective-permute-start.5 = (f32[27,8,128]{2,1,0:T(8,128)S(1)}, f32[27,8,128]{2,1,0:T(8,128)S(1)}, u32[]{:S(2)}, u32[]{:S(2)}) collective-permute-start(f32[27,8,128]{2,1,0:T(8,128)S(1)} %get-tuple-element.24), channel_id=1, source_target_pairs={{0,128},{128,256},{256,384},{1,129},{129,257},{257,385},{2,130},{1... | collective-permute-start | bytes 331784 | tf_op jit(solution)/shard_map/ppermute | solution.py:606
  107.6 5.8 %collective-permute-start.6 = (f32[4,67,8,128]{3,2,1,0:T(8,128)S(1)}, f32[4,67,8,128]{3,2,1,0:T(8,128)S(1)}, u32[]{:S(2)}, u32[]{:S(2)}) collective-permute-start(f32[4,67,8,128]{3,2,1,0:T(8,128)S(1)} %all_to_all.17.gathered), channel_id=1, source_target_pairs={{0,1},{1,0},{2,3},{3,2},{4,5},{5,4},{6,7},{7,6},{8,9},{9,8},{10,11... | collective-permute-start | bytes 3293192 | tf_op jit(solution)/shard_map/ppermute | solution.py:624

commit v8 on v7

--- a/solution.py
+++ b/solution.py
@@ -90,11 +90,26 @@
 TRAVEL = [(a, z) for a, skip in enumerate((1, 2, 0)) for z in range(skip, 24 - skip)]
 
 
+DEPTH = (7, 6, 8)
+START = (0, 7, 13)
+
+
+def zpack_kernel(mine, to_chip, to_beside):
+    odd = (lax.axis_index("gz") & 1) == 1
+    for a in range(3):
+        for z in range(DEPTH[a]):
+            low = mine[a, z]
+            high = mine[a, 8 - DEPTH[a] + z]
+            to_chip[START[a] + z] = jnp.where(odd, low, high)
+            to_beside[START[a] + z] = jnp.where(odd, high, low)
+
+
 def window_rows(mine, chip, beside, a, z, rows):
     if z // 8 == 1:
         return mine[a, z - 8, rows]
+    i = START[a] + (z - 8 + DEPTH[a] if z < 8 else z - 16)
     odd = (lax.axis_index("gz") & 1) == 1
-    return jnp.where(odd == (z < 8), chip[a, z % 8, rows], beside[a, z % 8, rows])
+    return jnp.where(odd == (z < 8), chip[i, rows], beside[i, rows])
 
 
 def ypack_kernel(mine, chip, beside, to_high, to_low):
@@ -608,8 +623,9 @@
 
 def local(right_side, guess, coefficient):
     mine = jnp.stack([guess, right_side, coefficient])
-    beside = lax.ppermute(mine, "gz", [(i, ((i + 1) ^ 1) - 1) for i in range(1, 15)])
-    chip = lax.ppermute(mine, "gz", [(i, i ^ 1) for i in range(16)])
+    to_chip, to_beside = run(zpack_kernel, [(21, 32, 128)] * 2, [], mine)
+    beside = lax.ppermute(to_beside, "gz", [(i, ((i + 1) ^ 1) - 1) for i in range(1, 15)])
+    chip = lax.ppermute(to_chip, "gz", [(i, i ^ 1) for i in range(16)])
     to_high, to_low = run(ypack_kernel, *YPACK, mine, chip, beside)
     ylow, yhigh = both_ways(to_low, to_high, "gy")
     window, to_right, to_left = run(

time: 125 us -> 127 us (1.016)
  waiting for transfers between devices: 10.5 us -> 14.4 us
  blocking collectives: 70.2 us -> 67.2 us
    ppermute x2, waiting for transfers between devices: 1.33 us -> 6.93 us  [the longest x1 6.92 us: local(): lax.ppermute(to_beside, 'gz', [(i, (i + 1 ^ 1) - 1) for i in range(1, 15)])]
    all_to_all x1, blocking collectives: 22.7 us -> 19.7 us  [local(): lax.all_to_all(share, 'gz', 0, 0)]
    ppermute x2, waiting for transfers between devices: 4.47 us -> 2.09 us  [both_ways(): lax.ppermute(to_low, axis, down(axis))]
    pallas_call x6 -> x7, Pallas kernels: 18.8 us -> 18.9 us  [run(): pl.pallas_call(kernel, out_shape=[jax.ShapeDtypeStruct(shape, F32) for sh...]
  transfers between devices with their start and end apart: 7 -> 7, of which waited for: 7 -> 6; matrix products, arithmetic and copies ran while one was open for 0% -> 0% of each run, Pallas kernels for 0% -> 0%
where the time goes in v8:
time: 127 us
  blocking collectives  67.2 us (53%)
  starting transfers between devices  24.7 us (19%)
  Pallas kernels  18.9 us (15%)
  waiting for transfers between devices  14.4 us (11%)
    all_to_all x1, blocking collectives, local(): lax.all_to_all(share, 'gy', 0, 0)  27.7 us
    all_to_all x1, blocking collectives, local(): whole = lax.all_to_all(share, 'gx', 0, 0)  19.8 us
    all_to_all x1, blocking collectives, local(): lax.all_to_all(share, 'gz', 0, 0)  19.7 us
    pallas_call x7, Pallas kernels, run(): pl.pallas_call(kernel, out_shape=[jax.ShapeDtypeStruct(shape, F32) for sh...  18.9 us
    ppermute x1, starting transfers between devices, local(): chip = lax.ppermute(to_chip, 'gz', [(i, i ^ 1) for i in range(16)])  8.79 us
    ppermute x2, starting transfers between devices, both_ways(): lax.ppermute(to_high, axis, up(axis))  8 us
    ppermute x1, waiting for transfers between devices, local(): lax.ppermute(to_beside, 'gz', [(i, (i + 1 ^ 1) - 1) for i in range(1, 15)])  6.92 us
    ppermute x1, starting transfers between devices, local(): other = lax.ppermute(whole, 'gz', [(i, i ^ 1) for i in range(16)])  3.45 us
  transfers between devices with their start and end apart: 7, of which 6 were waited for; matrix products, arithmetic and copies ran while one was open for 0% of the time, Pallas kernels for 0%

profile of v8, /device:TPU:1, one launch (start us, length us, event | category | flops | bytes accessed | tf_op | source)
XLA Modules:
  0.0 127.0 jit_solution(8699200576822924651)
XLA Ops:
  0.6 1.1 pad_maximum_fusion.mine
  1.7 0.1 shard_map.50
  1.8 8.8 %collective-permute-start = (f32[21,32,128]{2,1,0:T(8,128)S(1)}, f32[21,32,128]{2,1,0:T(8,128)S(1)}, u32[]{:S(2)}, u32[]{:S(2)}) collective-permute-start(f32[21,32,128]{2,1,0:T(8,128)S(1)} %get-tuple-element.22), channel_id=1, source_target_pairs={{0,1},{1,0},{2,3},{3,2},{4,5},{5,4},{6,7},{7,6},{8,9},{9,8},{10,11... | collective-permute-start | bytes 1032200 | tf_op jit(solution)/shard_map/ppermute | solution.py:628
  10.5 1.9 %collective-permute-start.1 = (f32[21,32,128]{2,1,0:T(8,128)S(1)}, f32[21,32,128]{2,1,0:T(8,128)S(1)}, u32[]{:S(2)}, u32[]{:S(2)}) collective-permute-start(f32[21,32,128]{2,1,0:T(8,128)S(1)} %get-tuple-element.23), channel_id=1, source_target_pairs={{1,2},{2,1},{3,4},{4,3},{5,6},{6,5},{7,8},{8,7},{9,10},{10,9},{11,... | collective-permute-start | bytes 1032200 | tf_op jit(solution)/shard_map/ppermute | solution.py:627
  12.5 0.0 collective-permute-done.chip
  12.5 6.9 %collective-permute-done.1.beside = f32[21,32,128]{2,1,0:T(8,128)S(1)} collective-permute-done((f32[21,32,128]{2,1,0:T(8,128)S(1)}, f32[21,32,128]{2,1,0:T(8,128)S(1)}, u32[]{:S(2)}, u32[]{:S(2)}) %collective-permute-start.1) | collective-permute-done | bytes 344096 | tf_op jit(solution)/shard_map/ppermute | solution.py:627
  19.5 1.3 %collective-permute-start.2 = (f32[66,8,128]{2,1,0:T(8,128)S(1)}, f32[66,8,128]{2,1,0:T(8,128)S(1)}, u32[]{:S(2)}, u32[]{:S(2)}) collective-permute-start(f32[66,8,128]{2,1,0:T(8,128)S(1)} %get-tuple-element.24), channel_id=1, source_target_pairs={{16,0},{32,16},{48,32},{64,48},{80,64},{96,80},{112,96},{17,1},{33... | collective-permute-start | bytes 811016 | tf_op jit(solution)/shard_map/ppermute | solution.py:621
  20.8 4.0 %collective-permute-start.3 = (f32[66,8,128]{2,1,0:T(8,128)S(1)}, f32[66,8,128]{2,1,0:T(8,128)S(1)}, u32[]{:S(2)}, u32[]{:S(2)}) collective-permute-start(f32[66,8,128]{2,1,0:T(8,128)S(1)} %get-tuple-element.25), channel_id=1, source_target_pairs={{0,16},{16,32},{32,48},{48,64},{64,80},{80,96},{96,112},{1,17},{17... | collective-permute-start | bytes 811016 | tf_op jit(solution)/shard_map/ppermute | solution.py:621
  24.8 1.9 %collective-permute-done.2.yhigh = f32[66,8,128]{2,1,0:T(8,128)S(1)} collective-permute-done((f32[66,8,128]{2,1,0:T(8,128)S(1)}, f32[66,8,128]{2,1,0:T(8,128)S(1)}, u32[]{:S(2)}, u32[]{:S(2)}) %collective-permute-start.2) | collective-permute-done | bytes 270368 | tf_op jit(solution)/shard_map/ppermute | solution.py:621
  26.7 1.5 %collective-permute-done.3.ylow = f32[66,8,128]{2,1,0:T(8,128)S(1)} collective-permute-done((f32[66,8,128]{2,1,0:T(8,128)S(1)}, f32[66,8,128]{2,1,0:T(8,128)S(1)}, u32[]{:S(2)}, u32[]{:S(2)}) %collective-permute-start.3) | collective-permute-done | bytes 270368 | tf_op jit(solution)/shard_map/ppermute | solution.py:621
  28.1 0.5 shard_map.52
  28.6 1.3 %collective-permute-start.4 = (f32[27,8,128]{2,1,0:T(8,128)S(1)}, f32[27,8,128]{2,1,0:T(8,128)S(1)}, u32[]{:S(2)}, u32[]{:S(2)}) collective-permute-start(f32[27,8,128]{2,1,0:T(8,128)S(1)} %get-tuple-element.27), channel_id=1, source_target_pairs={{128,0},{256,128},{384,256},{129,1},{257,129},{385,257},{130,2},{2... | collective-permute-start | bytes 331784 | tf_op jit(solution)/shard_map/ppermute | solution.py:621
  29.9 4.0 %collective-permute-start.5 = (f32[27,8,128]{2,1,0:T(8,128)S(1)}, f32[27,8,128]{2,1,0:T(8,128)S(1)}, u32[]{:S(2)}, u32[]{:S(2)}) collective-permute-start(f32[27,8,128]{2,1,0:T(8,128)S(1)} %get-tuple-element.28), channel_id=1, source_target_pairs={{0,128},{128,256},{256,384},{1,129},{129,257},{257,385},{2,130},{1... | collective-permute-start | bytes 331784 | tf_op jit(solution)/shard_map/ppermute | solution.py:621
  33.9 0.2 collective-permute-done.4.from_right
  34.1 1.5 %collective-permute-done.5.from_left = f32[27,8,128]{2,1,0:T(8,128)S(1)} collective-permute-done((f32[27,8,128]{2,1,0:T(8,128)S(1)}, f32[27,8,128]{2,1,0:T(8,128)S(1)}, u32[]{:S(2)}, u32[]{:S(2)}) %collective-permute-start.5) | collective-permute-done | bytes 110624 | tf_op jit(solution)/shard_map/ppermute | solution.py:621
  35.7 6.4 %shard_map.53 = (f32[16,5,8,128]{3,2,1,0:T(8,128)S(1)}, f32[12,24,128]{2,1,0:T(8,128)S(1)}, f32[12,24,128]{2,1,0:T(8,128)S(1)}, f32[144,8,256]{2,1,0:T(8,128)S(1...) custom-call(f32[72,6,8,128]{3,2,1,0:T(8,128)S(1)} %get-tuple-element, ...), custom_call_target="tpu_custom_call" | custom-call | tf_op jit(solution)/shard_map/pallas_call | solution.py:586
  42.1 19.7 %all_to_all.15.gathered = f32[16,5,8,128]{3,2,1,0:T(8,128)S(1)} all-to-all(f32[16,5,8,128]{3,2,1,0:T(8,128)S(1)} %get-tuple-element.29), channel_id=1, replica_groups=mesh['gx'=4,'gy'=8,'gz'=16] {'gz'}, dimensions={0} | all-to-all | bytes 655360 | tf_op jit(solution)/shard_map/all_to_all | solution.py:637
  61.8 0.1 shard_map.54
  61.9 27.7 %all_to_all.16.gathered = f32[8,14,8,128]{3,2,1,0:T(8,128)S(1)} all-to-all(f32[8,14,8,128]{3,2,1,0:T(8,128)S(1)} %get-tuple-element.31), channel_id=1, replica_groups=mesh['gx'=4,'gy'=8,'gz'=16] {'gy'}, dimensions={0} | all-to-all | bytes 917504 | tf_op jit(solution)/shard_map/all_to_all | solution.py:638
  89.7 0.2 shard_map.55
  89.9 19.8 %all_to_all.17.gathered = f32[4,67,8,128]{3,2,1,0:T(8,128)S(1)} all-to-all(f32[4,67,8,128]{3,2,1,0:T(8,128)S(1)} %get-tuple-element.33), channel_id=1, replica_groups=mesh['gx'=4,'gy'=8,'gz'=16] {'gx'}, dimensions={0} | all-to-all | bytes 2195456 | tf_op jit(solution)/shard_map/all_to_all | solution.py:639
  109.7 3.5 %collective-permute-start.6 = (f32[4,67,8,128]{3,2,1,0:T(8,128)S(1)}, f32[4,67,8,128]{3,2,1,0:T(8,128)S(1)}, u32[]{:S(2)}, u32[]{:S(2)}) collective-permute-start(f32[4,67,8,128]{3,2,1,0:T(8,128)S(1)} %all_to_all.17.gathered), channel_id=1, source_target_pairs={{0,1},{1,0},{2,3},{3,2},{4,5},{5,4},{6,7},{7,6},{8,9},{9,8},{10,11... | collective-permute-start | bytes 3293192 | tf_op jit(solution)/shard_map/ppermute | solution.py:640
  113.1 2.3 %collective-permute-done.6.other = f32[4,67,8,128]{3,2,1,0:T(8,128)S(1)} collective-permute-done((f32[4,67,8,128]{3,2,1,0:T(8,128)S(1)}, f32[4,67,8,128]{3,2,1,0:T(8,128)S(1)}, u32[]{:S(2)}, u32[]{:S(2)}) %collective-permute-start.6) | collective-permute-done | bytes 1097760 | tf_op jit(solution)/shard_map/ppermute | solution.py:640
  115.5 11.5 %shard_map.56 = (f32[8,32,128]{2,1,0:T(8,128)}, f32[8,32,128]{2,1,0:T(8,128)}) custom-call(f32[4,67,8,128]{3,2,1,0:T(8,128)S(1)} %all_to_all.17.gathered, f32[4,67,8,128]{3,2,1,0:T(8,128)S(1)} %collective-permute-done.6.other, f32[12,24,128]{2,1,0:T(8,128)S(1)} %get-tuple-element.34.pair, f32[12,24,128]{2,1,0:T(8,128)S(1)} %get-tuple-element.35.k1, ...), custom_call_target="tpu_custom_call" | custom-call | tf_op jit(solution)/shard_map/pallas_call | solution.py:586
  (1 shorter events, 0.0 us)
Async XLA Ops:
  1.8 10.7 %collective-permute-start = (f32[21,32,128]{2,1,0:T(8,128)S(1)}, f32[21,32,128]{2,1,0:T(8,128)S(1)}, u32[]{:S(2)}, u32[]{:S(2)}) collective-permute-start(f32[21,32,128]{2,1,0:T(8,128)S(1)} %get-tuple-element.22), channel_id=1, source_target_pairs={{0,1},{1,0},{2,3},{3,2},{4,5},{5,4},{6,7},{7,6},{8,9},{9,8},{10,11... | collective-permute-start | bytes 1032200 | tf_op jit(solution)/shard_map/ppermute | solution.py:628
  10.5 8.9 %collective-permute-start.1 = (f32[21,32,128]{2,1,0:T(8,128)S(1)}, f32[21,32,128]{2,1,0:T(8,128)S(1)}, u32[]{:S(2)}, u32[]{:S(2)}) collective-permute-start(f32[21,32,128]{2,1,0:T(8,128)S(1)} %get-tuple-element.23), channel_id=1, source_target_pairs={{1,2},{2,1},{3,4},{4,3},{5,6},{6,5},{7,8},{8,7},{9,10},{10,9},{11,... | collective-permute-start | bytes 1032200 | tf_op jit(solution)/shard_map/ppermute | solution.py:627
  19.5 7.2 %collective-permute-start.2 = (f32[66,8,128]{2,1,0:T(8,128)S(1)}, f32[66,8,128]{2,1,0:T(8,128)S(1)}, u32[]{:S(2)}, u32[]{:S(2)}) collective-permute-start(f32[66,8,128]{2,1,0:T(8,128)S(1)} %get-tuple-element.24), channel_id=1, source_target_pairs={{16,0},{32,16},{48,32},{64,48},{80,64},{96,80},{112,96},{17,1},{33... | collective-permute-start | bytes 811016 | tf_op jit(solution)/shard_map/ppermute | solution.py:621
  20.8 7.4 %collective-permute-start.3 = (f32[66,8,128]{2,1,0:T(8,128)S(1)}, f32[66,8,128]{2,1,0:T(8,128)S(1)}, u32[]{:S(2)}, u32[]{:S(2)}) collective-permute-start(f32[66,8,128]{2,1,0:T(8,128)S(1)} %get-tuple-element.25), channel_id=1, source_target_pairs={{0,16},{16,32},{32,48},{48,64},{64,80},{80,96},{96,112},{1,17},{17... | collective-permute-start | bytes 811016 | tf_op jit(solution)/shard_map/ppermute | solution.py:621
  28.6 5.5 %collective-permute-start.4 = (f32[27,8,128]{2,1,0:T(8,128)S(1)}, f32[27,8,128]{2,1,0:T(8,128)S(1)}, u32[]{:S(2)}, u32[]{:S(2)}) collective-permute-start(f32[27,8,128]{2,1,0:T(8,128)S(1)} %get-tuple-element.27), channel_id=1, source_target_pairs={{128,0},{256,128},{384,256},{129,1},{257,129},{385,257},{130,2},{2... | collective-permute-start | bytes 331784 | tf_op jit(solution)/shard_map/ppermute | solution.py:621
  29.9 5.7 %collective-permute-start.5 = (f32[27,8,128]{2,1,0:T(8,128)S(1)}, f32[27,8,128]{2,1,0:T(8,128)S(1)}, u32[]{:S(2)}, u32[]{:S(2)}) collective-permute-start(f32[27,8,128]{2,1,0:T(8,128)S(1)} %get-tuple-element.28), channel_id=1, source_target_pairs={{0,128},{128,256},{256,384},{1,129},{129,257},{257,385},{2,130},{1... | collective-permute-start | bytes 331784 | tf_op jit(solution)/shard_map/ppermute | solution.py:621
  109.7 5.8 %collective-permute-start.6 = (f32[4,67,8,128]{3,2,1,0:T(8,128)S(1)}, f32[4,67,8,128]{3,2,1,0:T(8,128)S(1)}, u32[]{:S(2)}, u32[]{:S(2)}) collective-permute-start(f32[4,67,8,128]{3,2,1,0:T(8,128)S(1)} %all_to_all.17.gathered), channel_id=1, source_target_pairs={{0,1},{1,0},{2,3},{3,2},{4,5},{5,4},{6,7},{7,6},{8,9},{9,8},{10,11... | collective-permute-start | bytes 3293192 | tf_op jit(solution)/shard_map/ppermute | solution.py:640
